TPU v7x, 32 devices: a whole 2x2x4 slice. The times are simulated.
32 devices in a mesh: dp: 8 (over z, y), ctx: 4 (over x, core).
Axes of the slice: x: 2, y: 2, z: 4, core: 2. Of those that a mesh axis runs over, the one named last changes fastest.
Arguments:
- layer_input: bfloat16 [8192, 1024], P(('dp', 'ctx')), may hold values from -6 to 6
- dest_slot: int32 [8192], P(('dp', 'ctx')), may hold values from 0 to 8191, as said below
- doc_len: int32 [8, 2], P('dp'), may hold values from 0 to 1024, as said below
- out_grad: bfloat16 [8192, 1024], P(('dp', 'ctx')), may hold values from -6 to 6
- attn_gain: bfloat16 [1024], P(('dp', 'ctx')), may hold values from 0.5 to 1.5
- w_query: bfloat16 [1024, 2048], P(('dp', 'ctx')), may hold values from -0.1875 to 0.1875
- w_key: bfloat16 [1024, 1024], P(('dp', 'ctx')), may hold values from -0.1875 to 0.1875
- w_value: bfloat16 [1024, 1024], P(('dp', 'ctx')), may hold values from -0.1875 to 0.1875
- q_gain: bfloat16 [128], P(('dp', 'ctx')), may hold values from 1 to 2
- k_gain: bfloat16 [128], P(('dp', 'ctx')), may hold values from 0.5 to 1.5
- w_out: bfloat16 [2048, 1024], P(('dp', 'ctx')), may hold values from -0.5 to 0.5
- mlp_gain: bfloat16 [1024], P(('dp', 'ctx')), may hold values from 0.5 to 1.5
- w_gate: bfloat16 [1024, 3072], P(('dp', 'ctx')), may hold values from -0.1875 to 0.1875
- w_up: bfloat16 [1024, 3072], P(('dp', 'ctx')), may hold values from -0.1875 to 0.1875
- w_down: bfloat16 [3072, 1024], P(('dp', 'ctx')), may hold values from -0.109375 to 0.109375
Outputs:
- layer_output: bfloat16 [8192, 1024], P(('dp', 'ctx'))
- input_grad: bfloat16 [8192, 1024], P(('dp', 'ctx'))
- grad_attn_gain: float32 [1024], P(('dp', 'ctx'))
- grad_query: float32 [1024, 2048], P(('dp', 'ctx'))
- grad_key: float32 [1024, 1024], P(('dp', 'ctx'))
- grad_value: float32 [1024, 1024], P(('dp', 'ctx'))
- grad_q_gain: float32 [128], P(('dp', 'ctx'))
- grad_k_gain: float32 [128], P(('dp', 'ctx'))
- grad_out: float32 [2048, 1024], P(('dp', 'ctx'))
- grad_mlp_gain: float32 [1024], P(('dp', 'ctx'))
- grad_gate: float32 [1024, 3072], P(('dp', 'ctx'))
- grad_up: float32 [1024, 3072], P(('dp', 'ctx'))
- grad_down: float32 [3072, 1024], P(('dp', 'ctx'))
Inputs may be any that keep to these rules, and one draw needn't show every extreme that they name: `dest_slot`: A permutation of the rows that keeps a row's ctx index: the row held by the device at (dp i, ctx c) goes to a device at (dp j, ctx c). At most 64 rows of one device go to one device, and in every draw some pairs carry exactly 64. `doc_len`: row g gives the lengths of group g's documents in slot order: the nonzero entries come first, each at least 1024, and a row sums to at most 1024; in every draw some row holds one document of 1024 tokens.
All inputs are finite; a program needn't handle non-finite values.
Results may differ from a plain program's by a relative error of at most 0.02.
Values may be sent and summed in bfloat16 or wider, within the bound.
A program may use at most 192 MiB of HBM per device.

v0:
```python
import math

import jax
import jax.numpy as jnp
from jax import lax
from jax.sharding import PartitionSpec as P

H = 16
KVH = 8
HD = 128
DOCS = 2


EPS = 1e-06
THETA = 1000000.0
MASKED = -1e30


def doc_layout(lengths, slot_ids):
    doc_ends = jnp.cumsum(lengths, dtype=jnp.int32)
    starts = doc_ends - lengths
    documents = jnp.sum(
        (slot_ids[:, None] >= doc_ends[None, :]).astype(jnp.int32), axis=1, dtype=jnp.int32
    )
    one_hot = (documents[:, None] == jnp.arange(lengths.shape[0], dtype=jnp.int32)[None, :]).astype(
        jnp.int32
    )
    positions = slot_ids - jnp.sum(one_hot * starts[None, :], axis=1, dtype=jnp.int32)
    return (documents, positions)


def allowed_mask(query_slots, query_docs, key_slots, key_docs):
    same_doc = (
        (query_docs[:, None] == key_docs[None, :])
        & (query_docs[:, None] < DOCS)
        & (key_slots[None, :] <= query_slots[:, None])
    )
    return same_doc | (key_slots[None, :] == query_slots[:, None])


def rope_tables(positions):
    freq_index = jnp.arange(HD // 2, dtype=jnp.float32)
    inverse = jnp.exp(freq_index * (-2.0 / HD) * math.log(THETA))
    doubled = jnp.concatenate([inverse, inverse])
    angles = positions.astype(jnp.float32)[:, None] * doubled[None, :]
    return (jnp.cos(angles), jnp.sin(angles))


def rms_scale(values_in, gain_vec):
    factor = lax.rsqrt(jnp.mean(values_in * values_in, axis=-1, keepdims=True) + EPS)
    return values_in * factor * gain_vec


def qk_rope(projected, gain_vec, cosine_table, sine_table):
    row_count = projected.shape[0]
    per_head = projected.reshape(row_count, -1, HD)
    normed = rms_scale(per_head, gain_vec)
    half_dim = HD // 2
    turned = jnp.concatenate([-normed[..., half_dim:], normed[..., :half_dim]], axis=-1)
    rotated = normed * cosine_table[:, None, :] + turned * sine_table[:, None, :]
    return rotated.reshape(row_count, -1)


def swiglu(gate_proj, up_proj):
    return jax.nn.silu(gate_proj) * up_proj


def project(left_rows, weight):
    return jnp.dot(left_rows, weight, preferred_element_type=jnp.float32)


def contract_rows(left_rows, right_rows):
    return lax.dot_general(
        left_rows, right_rows, (((0,), (0,)), ((), ())), preferred_element_type=jnp.float32
    )


def times_transpose(left_rows, weight):
    return lax.dot_general(
        left_rows, weight, (((1,), (1,)), ((), ())), preferred_element_type=jnp.float32
    )


def local(
    layer_input,
    dest_slot,
    doc_len,
    out_grad,
    attn_gain,
    w_query,
    w_key,
    w_value,
    q_gain,
    k_gain,
    w_out,
    mlp_gain,
    w_gate,
    w_up,
    w_down,
):
    tok_rows, model_width = layer_input.shape
    n_data = lax.axis_size("dp")
    n_ctx = lax.axis_size("ctx")
    capacity = 2 * tok_rows // n_data
    group_rows = tok_rows * n_ctx
    head_groups = H // KVH
    score_scale = HD ** (-0.5)
    owner_dp = dest_slot // tok_rows // n_ctx
    local_slot = dest_slot % tok_rows
    one_hot = (owner_dp[:, None] == jnp.arange(n_data, dtype=jnp.int32)[None, :]).astype(jnp.int32)
    earlier = jnp.cumsum(one_hot, axis=0, dtype=jnp.int32) - one_hot
    send_slot = owner_dp * capacity + jnp.sum(earlier * one_hot, axis=1, dtype=jnp.int32)
    outgoing = (
        jnp.zeros((n_data * capacity, model_width), jnp.bfloat16).at[send_slot].set(layer_input)
    )
    labels = jnp.full((n_data * capacity,), tok_rows, jnp.int32).at[send_slot].set(local_slot)
    received = lax.all_to_all(
        outgoing.reshape(n_data, capacity, model_width),
        "dp",
        split_axis=0,
        concat_axis=0,
        tiled=True,
    )
    in_labels = lax.all_to_all(
        labels.reshape(n_data, capacity), "dp", split_axis=0, concat_axis=0, tiled=True
    ).reshape(-1)
    owned_rows = (
        jnp.zeros((tok_rows, model_width), jnp.bfloat16)
        .at[in_labels]
        .set(received.reshape(-1, model_width), mode="drop")
    )
    ctx_index = lax.axis_index("ctx")
    query_slots = ctx_index * tok_rows + jnp.arange(tok_rows, dtype=jnp.int32)
    key_slots = jnp.arange(group_rows, dtype=jnp.int32)
    lengths = doc_len[0]
    query_docs, query_pos = doc_layout(lengths, query_slots)
    key_docs = doc_layout(lengths, key_slots)[0]
    allowed = allowed_mask(query_slots, query_docs, key_slots, key_docs)
    cosine_table, sine_table = rope_tables(query_pos)
    gathered = (
        lax.all_gather(attn_gain, ("dp", "ctx"), axis=0, tiled=True),
        lax.all_gather(w_query, ("dp", "ctx"), axis=0, tiled=True),
        lax.all_gather(w_key, ("dp", "ctx"), axis=0, tiled=True),
        lax.all_gather(w_value, ("dp", "ctx"), axis=0, tiled=True),
        lax.all_gather(q_gain, ("dp", "ctx"), axis=0, tiled=True),
        lax.all_gather(k_gain, ("dp", "ctx"), axis=0, tiled=True),
        lax.all_gather(w_out, ("dp", "ctx"), axis=0, tiled=True),
    )
    full_gain_a, full_query, full_key, full_value, full_gain_q, full_gain_k, full_out = gathered
    inputs = owned_rows.astype(jnp.float32)
    gain_attn = full_gain_a.astype(jnp.float32)
    gain_q = full_gain_q.astype(jnp.float32)
    gain_k = full_gain_k.astype(jnp.float32)
    normed_attn = rms_scale(inputs, gain_attn).astype(jnp.bfloat16)
    q_proj = project(normed_attn, full_query)
    k_proj = project(normed_attn, full_key)
    value_rows = project(normed_attn, full_value).astype(jnp.bfloat16)
    queries = qk_rope(q_proj, gain_q, cosine_table, sine_table).astype(jnp.bfloat16)
    key_rows = qk_rope(k_proj, gain_k, cosine_table, sine_table).astype(jnp.bfloat16)
    key_all, value_all = (
        lax.all_gather(key_rows, "ctx", axis=0, tiled=True),
        lax.all_gather(value_rows, "ctx", axis=0, tiled=True),
    )
    query_heads = queries.reshape(tok_rows, KVH, head_groups, HD).transpose(1, 2, 0, 3)
    key_heads = key_all.reshape(group_rows, KVH, HD).transpose(1, 0, 2)
    value_heads = value_all.reshape(group_rows, KVH, HD).transpose(1, 0, 2)

    def head_scores(q_head, k_head):
        scores = (
            jnp.einsum("gqd,kd->gqk", q_head, k_head, preferred_element_type=jnp.float32)
            * score_scale
        )
        return jnp.where(allowed[None], scores, MASKED)

    def attend_head(packed):
        q_head, k_head, v_head = packed
        scores = head_scores(q_head, k_head)
        row_max = jnp.max(scores, axis=-1, keepdims=True)
        exp_scores = jnp.exp(scores - row_max)
        row_total = jnp.sum(exp_scores, axis=-1, keepdims=True)
        probs_low = (exp_scores / row_total).astype(jnp.bfloat16)
        mixed_rows = jnp.einsum(
            "gqk,kd->gqd", probs_low, v_head, preferred_element_type=jnp.float32
        )
        return (mixed_rows, (row_max + jnp.log(row_total))[..., 0])

    mixed_heads, log_totals = lax.map(attend_head, (query_heads, key_heads, value_heads))
    attended = mixed_heads.transpose(2, 0, 1, 3).reshape(tok_rows, H * HD).astype(jnp.bfloat16)
    middle = inputs + project(attended, full_out)
    mlp_set = (
        lax.all_gather(mlp_gain, ("dp", "ctx"), axis=0, tiled=True),
        lax.all_gather(w_gate, ("dp", "ctx"), axis=0, tiled=True),
        lax.all_gather(w_up, ("dp", "ctx"), axis=0, tiled=True),
        lax.all_gather(w_down, ("dp", "ctx"), axis=0, tiled=True),
    )
    gain_mlp = mlp_set[0].astype(jnp.float32)
    normed_mlp = rms_scale(middle, gain_mlp).astype(jnp.bfloat16)
    gate_proj = project(normed_mlp, mlp_set[1])
    up_proj = project(normed_mlp, mlp_set[2])
    hidden = swiglu(gate_proj, up_proj).astype(jnp.bfloat16)
    layer_output = (middle + project(hidden, mlp_set[3])).astype(jnp.bfloat16)
    back_set = (
        lax.all_gather(mlp_gain, ("dp", "ctx"), axis=0, tiled=True),
        lax.all_gather(w_gate, ("dp", "ctx"), axis=0, tiled=True),
        lax.all_gather(w_up, ("dp", "ctx"), axis=0, tiled=True),
        lax.all_gather(w_down, ("dp", "ctx"), axis=0, tiled=True),
    )
    grad_down_full = contract_rows(hidden, out_grad)
    d_hidden = times_transpose(out_grad, back_set[3])
    swiglu_out, swiglu_pull = jax.vjp(swiglu, gate_proj, up_proj)
    d_gate_full, d_up_full = swiglu_pull(d_hidden)
    d_gate = d_gate_full.astype(jnp.bfloat16)
    d_up = d_up_full.astype(jnp.bfloat16)
    grad_gate_full = contract_rows(normed_mlp, d_gate)
    grad_up_full = contract_rows(normed_mlp, d_up)
    d_normed_mlp = times_transpose(d_gate, back_set[1]) + times_transpose(d_up, back_set[2])
    norm_out, mlp_norm_pull = jax.vjp(rms_scale, middle, gain_mlp)
    d_middle_norm, grad_gain_m = mlp_norm_pull(d_normed_mlp)
    d_middle = out_grad.astype(jnp.float32) + d_middle_norm
    mlp_grads = (
        lax.psum_scatter(grad_gain_m, ("dp", "ctx"), scatter_dimension=0, tiled=True),
        lax.psum_scatter(grad_gate_full, ("dp", "ctx"), scatter_dimension=0, tiled=True),
        lax.psum_scatter(grad_up_full, ("dp", "ctx"), scatter_dimension=0, tiled=True),
        lax.psum_scatter(grad_down_full, ("dp", "ctx"), scatter_dimension=0, tiled=True),
    )
    attn_back = (
        lax.all_gather(attn_gain, ("dp", "ctx"), axis=0, tiled=True),
        lax.all_gather(w_query, ("dp", "ctx"), axis=0, tiled=True),
        lax.all_gather(w_key, ("dp", "ctx"), axis=0, tiled=True),
        lax.all_gather(w_value, ("dp", "ctx"), axis=0, tiled=True),
        lax.all_gather(q_gain, ("dp", "ctx"), axis=0, tiled=True),
        lax.all_gather(k_gain, ("dp", "ctx"), axis=0, tiled=True),
        lax.all_gather(w_out, ("dp", "ctx"), axis=0, tiled=True),
    )
    d_branch = d_middle.astype(jnp.bfloat16)
    grad_out_full = contract_rows(attended, d_branch)
    d_attended = times_transpose(d_branch, attn_back[6]).astype(jnp.bfloat16)
    d_heads = d_attended.reshape(tok_rows, KVH, head_groups, HD).transpose(1, 2, 0, 3)

    def attend_back(packed):
        q_head, k_head, v_head, d_head, log_head = packed
        scores = head_scores(q_head, k_head)
        attn_probs = jnp.exp(scores - log_head[..., None])
        d_probs = jnp.einsum("gqd,kd->gqk", d_head, v_head, preferred_element_type=jnp.float32)
        row_inner = jnp.sum(attn_probs * d_probs, axis=-1, keepdims=True)
        d_scores = (attn_probs * (d_probs - row_inner)).astype(jnp.bfloat16)
        d_query = (
            jnp.einsum("gqk,kd->gqd", d_scores, k_head, preferred_element_type=jnp.float32)
            * score_scale
        )
        d_key = (
            jnp.einsum("gqk,gqd->kd", d_scores, q_head, preferred_element_type=jnp.float32)
            * score_scale
        )
        d_value = jnp.einsum(
            "gqk,gqd->kd",
            attn_probs.astype(jnp.bfloat16),
            d_head,
            preferred_element_type=jnp.float32,
        )
        return (d_query, d_key, d_value)

    d_query_heads, d_key_heads, d_value_heads = lax.map(
        attend_back, (query_heads, key_heads, value_heads, d_heads, log_totals)
    )
    d_queries = d_query_heads.transpose(2, 0, 1, 3).reshape(tok_rows, H * HD)
    d_key_all = d_key_heads.transpose(1, 0, 2).reshape(group_rows, KVH * HD)
    d_value_all = d_value_heads.transpose(1, 0, 2).reshape(group_rows, KVH * HD)
    d_key_rows, d_value_rows = (
        lax.psum_scatter(
            d_key_all.astype(jnp.bfloat16), "ctx", scatter_dimension=0, tiled=True
        ).astype(jnp.float32),
        lax.psum_scatter(
            d_value_all.astype(jnp.bfloat16), "ctx", scatter_dimension=0, tiled=True
        ).astype(jnp.float32),
    )

    def rope_part(projected, gain_vec):
        return qk_rope(projected, gain_vec, cosine_table, sine_table)

    rope_q_out, rope_q_pull = jax.vjp(rope_part, q_proj, gain_q)
    d_q_full, grad_gain_q = rope_q_pull(d_queries)
    rope_k_out, rope_k_pull = jax.vjp(rope_part, k_proj, gain_k)
    d_k_full, grad_gain_k = rope_k_pull(d_key_rows)
    d_q_proj = d_q_full.astype(jnp.bfloat16)
    d_k_proj = d_k_full.astype(jnp.bfloat16)
    d_v_proj = d_value_rows.astype(jnp.bfloat16)
    grad_query_full = contract_rows(normed_attn, d_q_proj)
    grad_key_full = contract_rows(normed_attn, d_k_proj)
    grad_value_full = contract_rows(normed_attn, d_v_proj)
    d_normed_attn = (
        times_transpose(d_q_proj, attn_back[1])
        + times_transpose(d_k_proj, attn_back[2])
        + times_transpose(d_v_proj, attn_back[3])
    )
    attn_norm_out, attn_norm_pull = jax.vjp(rms_scale, inputs, gain_attn)
    d_inputs_norm, grad_gain_a = attn_norm_pull(d_normed_attn)
    attn_grads = (
        lax.psum_scatter(grad_gain_a, ("dp", "ctx"), scatter_dimension=0, tiled=True),
        lax.psum_scatter(grad_query_full, ("dp", "ctx"), scatter_dimension=0, tiled=True),
        lax.psum_scatter(grad_key_full, ("dp", "ctx"), scatter_dimension=0, tiled=True),
        lax.psum_scatter(grad_value_full, ("dp", "ctx"), scatter_dimension=0, tiled=True),
        lax.psum_scatter(grad_gain_q, ("dp", "ctx"), scatter_dimension=0, tiled=True),
        lax.psum_scatter(grad_gain_k, ("dp", "ctx"), scatter_dimension=0, tiled=True),
        lax.psum_scatter(grad_out_full, ("dp", "ctx"), scatter_dimension=0, tiled=True),
    )
    owned_grad = (d_middle + d_inputs_norm).astype(jnp.bfloat16)
    picked = owned_grad[jnp.minimum(in_labels, tok_rows - 1)]
    returned = lax.all_to_all(
        picked.reshape(n_data, capacity, model_width), "dp", split_axis=0, concat_axis=0, tiled=True
    ).reshape(-1, model_width)
    input_grad = returned[send_slot]
    return (
        layer_output,
        input_grad,
        attn_grads[0],
        attn_grads[1],
        attn_grads[2],
        attn_grads[3],
        attn_grads[4],
        attn_grads[5],
        attn_grads[6],
        mlp_grads[0],
        mlp_grads[1],
        mlp_grads[2],
        mlp_grads[3],
    )


def solution(mesh):
    placed = (
        P(("dp", "ctx"), None),
        P(("dp", "ctx")),
        P("dp", None),
        P(("dp", "ctx"), None),
        P(("dp", "ctx")),
        P(("dp", "ctx"), None),
        P(("dp", "ctx"), None),
        P(("dp", "ctx"), None),
        P(("dp", "ctx")),
        P(("dp", "ctx")),
        P(("dp", "ctx"), None),
        P(("dp", "ctx")),
        P(("dp", "ctx"), None),
        P(("dp", "ctx"), None),
        P(("dp", "ctx"), None),
    )
    return jax.shard_map(
        local,
        mesh=mesh,
        in_specs=placed,
        out_specs=(
            P(("dp", "ctx"), None),
            P(("dp", "ctx"), None),
            P(("dp", "ctx")),
            P(("dp", "ctx"), None),
            P(("dp", "ctx"), None),
            P(("dp", "ctx"), None),
            P(("dp", "ctx")),
            P(("dp", "ctx")),
            P(("dp", "ctx"), None),
            P(("dp", "ctx")),
            P(("dp", "ctx"), None),
            P(("dp", "ctx"), None),
            P(("dp", "ctx"), None),
        ),
        check_vma=False,
    )
```

profile of v0, /device:TPU:3, one launch (start us, length us, event | category | flops | bytes accessed | tf_op | source)
XLA Modules:
  0.0 1786.8 jit_solution(14793432927163131255)
XLA Ops:
  11.7 5.6 all-to-all-start
  17.3 3.2 scatter_custom_fusion.1
  22.5 3.6 all-to-all-start.1
  27.9 46.8 %all-reduce.13 = (bf16[128]{0:T(256)(128)(2,1)S(1)}, bf16[1024]{0:T(1024)(128)(2,1)S(1)}, bf16[128]{0:T(256)(128)(2,1)S(1)}, bf16[1024]{0:T(1024)(128)(2,1)S(1)}) all-reduce(bf16[128]{0:T(256)(128)(2,1)S(1)} %dynamic-update-slice.1, bf16[1024]{0:T(1024)(128)(2,1)S(1)} %dynamic-update-slice, ...), channel_id=1, replica_groups=mesh['dp'=8,'ctx'=4] {'dp','ctx'}, use_global_device_ids=true, to_apply=%add.5 | all-reduce | flops 2304 | bytes 9216
  77.5 2.8 scatter_custom_fusion.2
  80.6 2.3 fusion.109
  86.7 47.6 %all-gather.16.cloned.1.call-done = bf16[1024,1024]{1,0:T(8,128)(2,1)} async-done(((bf16[32,1024]{1,0:T(8,128)(2,1)}), bf16[1024,1024]{1,0:T(8,128)(2,1)}) %all-gather.16.cloned.1.call-update) | async-done | bytes 2097168 | tf_op jit(solution)/shard_map/all_gather | solution.py:144
  134.3 3.1 convolution_convert_fusion.1
  143.2 13.6 all-gather.14.cloned.1.call-done
  156.8 3.3 bitcast_bitcast_fusion.1
  160.1 21.3 %all-gather.18.cloned.1.call-done = bf16[1024,1024]{1,0:T(8,128)(2,1)} async-done(((bf16[256,1024]{1,0:T(8,128)(2,1)}), bf16[1024,1024]{1,0:T(8,128)(2,1)}) %all-gather.18.cloned.1.call-update) | async-done | bytes 2097168 | tf_op jit(solution)/shard_map/all_gather | solution.py:162
  181.4 3.3 bitcast_bitcast_fusion
  184.7 62.4 %all-gather.10.cloned.1.call-done = bf16[1024,2048]{1,0:T(8,128)(2,1)} async-done(((bf16[32,2048]{1,0:T(8,128)(2,1)}), bf16[1024,2048]{1,0:T(8,128)(2,1)}) %all-gather.10.cloned.1.call-update) | async-done | bytes 4194320 | tf_op jit(solution)/shard_map/all_gather | solution.py:142
  247.1 3.5 fusion.111
  260.0 3.2 fusion.58
  265.2 46.9 %while.28 = (s32[]{:T(128)}, bf16[8,2,256,128]{2,3,1,0:T(8,128)(2,1)S(1)}, f32[8,2,256]{2,1,0:T(2,128)}, bf16[8,2,256,128]{3,2,1,0:T(8,128)(2,1)}, bf16[8,1024,1...) while((s32[]{:T(128)}, ...), condition=%wide.region_16.17_spmd.clone, body=%wide.region_13.16_spmd.clone.sunk | while | flops 276299264 | bytes 8282489 | solution.py:187
  313.2 3.9 multiply_reduce_fusion.8
  317.3 64.4 %all-gather.22.cloned.1.call-done = bf16[1024,3072]{1,0:T(8,128)(2,1)} async-done(((bf16[32,3072]{1,0:T(8,128)(2,1)}), bf16[1024,3072]{1,0:T(8,128)(2,1)}) %all-gather.22.cloned.1.call-update) | async-done | bytes 6291472 | tf_op jit(solution)/shard_map/all_gather | solution.py:192
  381.7 6.2 fusion.115
  387.9 64.7 %all-gather.24.cloned.1.call-done = bf16[1024,3072]{1,0:T(8,128)(2,1)} async-done(((bf16[32,3072]{1,0:T(8,128)(2,1)}), bf16[1024,3072]{1,0:T(8,128)(2,1)}) %all-gather.24.cloned.1.call-update) | async-done | bytes 6291472 | tf_op jit(solution)/shard_map/all_gather | solution.py:193
  452.6 6.2 fusion.116
  458.8 64.7 %all-gather.26.cloned.1.call-done = bf16[3072,1024]{1,0:T(8,128)(2,1)} async-done(((bf16[96,1024]{1,0:T(8,128)(2,1)}), bf16[3072,1024]{1,0:T(8,128)(2,1)}) %all-gather.26.cloned.1.call-update) | async-done | bytes 6291472 | tf_op jit(solution)/shard_map/all_gather | solution.py:194
  523.5 9.8 multiply_convert_fusion.1
  533.3 5.8 fusion.117
  539.1 2.9 multiply_reduce_fusion.4
  546.7 108.5 %while.29 = (s32[]{:T(128)}, f32[8,2,256,128]{3,2,1,0:T(8,128)}, bf16[8,1024,128]{1,2,0:T(8,128)(2,1)}, bf16[8,1024,128]{1,2,0:T(8,128)(2,1)}, bf16[8,2,256,128]...) while((s32[]{:T(128)}, f32[8,2,256,128]{3,2,1,0:T(8,128)}, ...), condition=%wide.region_21.22_spmd.clone, body=%wide.region_19.21_spmd.clone.sunk | while | flops 677707264 | bytes 19681688 | solution.py:263
  552.4 2.1 fusion.190
  554.6 2.1 fusion.191
  566.0 2.1 fusion.190
  568.1 2.1 fusion.191
  579.5 2.1 fusion.190
  581.6 2.1 fusion.191
  595.2 2.1 fusion.191
  606.6 2.1 fusion.190
  608.7 2.1 fusion.191
  620.1 2.1 fusion.190
  622.2 2.1 fusion.191
  633.7 2.1 fusion.190
  635.8 2.1 fusion.191
  647.2 2.1 fusion.190
  649.3 2.1 fusion.191
  656.0 27.9 %reduce-scatter.10.cloned.1.call-done = bf16[256,1024]{0,1:T(8,128)(2,1)} async-done(((bf16[1024,1024]{0,1:T(8,128)(2,1)}), bf16[256,1024]{0,1:T(8,128)(2,1)}) %reduce-scatter.10.cloned.1.call-update) | async-done | bytes 524304 | tf_op jit(solution)/shard_map/reduce_scatter | solution.py:270
  689.9 2.8 fusion.79
  692.8 25.3 %reduce-scatter.12.cloned.1.call-done = bf16[256,1024]{0,1:T(8,128)(2,1)} async-done(((bf16[1024,1024]{0,1:T(8,128)(2,1)}), bf16[256,1024]{0,1:T(8,128)(2,1)}) %reduce-scatter.12.cloned.1.call-update) | async-done | bytes 524304 | tf_op jit(solution)/shard_map/reduce_scatter | solution.py:273
  718.1 3.9 fusion.104
  727.1 5.9 multiply_reduce_fusion.1
  733.1 3.4 fusion.57
  737.5 4.6 fusion.71
  743.6 4.6 fusion.86
  749.2 7.8 fusion.118
  757.1 7.8 fusion.119
  765.9 7.9 fusion.120
  775.0 3.6 fusion.73
  781.8 2.8 gather_fusion
  784.6 5.4 all-to-all-start.2
  790.0 5.9 fusion.60
  795.9 45.9 %all-reduce.12 = (f32[1024]{0:T(1024)S(1)}, f32[128]{0:T(128)S(1)}, f32[128]{0:T(128)S(1)}, f32[1024]{0:T(1024)S(1)}) all-reduce(f32[1024]{0:T(1024)S(1)} %get-tuple-element.172, f32[128]{0:T(128)S(1)} %copy-done.51, f32[128]{0:T(128)S(1)} %get-tuple-element.174, ...), channel_id=4, replica_groups=mesh['dp'=8,'ctx'=4] {'dp','ctx'}, use_global_device_ids=true, to_apply=%region_28.29.clone | all-reduce | flops 2304 | bytes 18432
  846.1 8.9 reduce-scatter.16.cloned.1.call-done
  855.0 139.8 %reduce-scatter.18.cloned.1.call-done = f32[32,1024]{1,0:T(8,128)} async-done(((f32[1024,1024]{1,0:T(8,128)}), f32[32,1024]{1,0:T(8,128)}) %reduce-scatter.18.cloned.1.call-update) | async-done | bytes 131088 | tf_op jit(solution)/shard_map/reduce_scatter | solution.py:302
  994.9 147.6 %reduce-scatter.14.cloned.1.call-done = f32[32,2048]{1,0:T(8,128)} async-done(((f32[1024,2048]{1,0:T(8,128)}), f32[32,2048]{1,0:T(8,128)}) %reduce-scatter.14.cloned.1.call-update) | async-done | bytes 262160 | tf_op jit(solution)/shard_map/reduce_scatter | solution.py:300
  1142.5 147.1 %reduce-scatter.20.cloned.1.call-done = f32[64,1024]{1,0:T(8,128)} async-done(((f32[2048,1024]{1,0:T(8,128)}), f32[64,1024]{1,0:T(8,128)}) %reduce-scatter.20.cloned.1.call-update) | async-done | bytes 262160 | tf_op jit(solution)/shard_map/reduce_scatter | solution.py:305
  1289.6 167.2 %reduce-scatter.22.cloned.1.call-done = f32[32,3072]{1,0:T(8,128)} async-done(((f32[1024,3072]{1,0:T(8,128)}), f32[32,3072]{1,0:T(8,128)}) %reduce-scatter.22.cloned.1.call-update) | async-done | bytes 393232 | tf_op jit(solution)/shard_map/reduce_scatter | solution.py:222
  1456.8 162.0 %reduce-scatter.24.cloned.1.call-done = f32[32,3072]{1,0:T(8,128)} async-done(((f32[1024,3072]{1,0:T(8,128)}), f32[32,3072]{1,0:T(8,128)}) %reduce-scatter.24.cloned.1.call-update) | async-done | bytes 393232 | tf_op jit(solution)/shard_map/reduce_scatter | solution.py:223
  1618.8 161.0 %reduce-scatter.26.cloned.1.call-done = f32[96,1024]{1,0:T(8,128)} async-done(((f32[3072,1024]{1,0:T(8,128)}), f32[96,1024]{1,0:T(8,128)}) %reduce-scatter.26.cloned.1.call-update) | async-done | bytes 393232 | tf_op jit(solution)/shard_map/reduce_scatter | solution.py:224
  (364 shorter events, 185.9 us)
Async XLA Ops:
  7.2 19.7 %copy-start.54 = (bf16[4]{0:T(256)(128)(2,1)S(1)}, bf16[4]{0:T(256)(128)(2,1)}, u32[]{:S(2)}) copy-start(bf16[4]{0:T(256)(128)(2,1)} %param.27) | copy-start | bytes 28
  7.2 20.0 %copy-start.55 = (bf16[4]{0:T(256)(128)(2,1)S(1)}, bf16[4]{0:T(256)(128)(2,1)}, u32[]{:S(2)}) copy-start(bf16[4]{0:T(256)(128)(2,1)} %param.28) | copy-start | bytes 28
  7.2 20.2 %copy-start.56 = (bf16[32]{0:T(256)(128)(2,1)S(1)}, bf16[32]{0:T(256)(128)(2,1)}, u32[]{:S(2)}) copy-start(bf16[32]{0:T(256)(128)(2,1)} %param.23) | copy-start | bytes 196
  7.2 20.4 %copy-start.57 = (bf16[32]{0:T(256)(128)(2,1)S(1)}, bf16[32]{0:T(256)(128)(2,1)}, u32[]{:S(2)}) copy-start(bf16[32]{0:T(256)(128)(2,1)} %param.30) | copy-start | bytes 196
  7.2 67.4 %copy-start.58 = (s32[1,2]{1,0:T(1,128)S(1)}, s32[1,2]{1,0:T(1,128)}, u32[]{:S(2)}) copy-start(s32[1,2]{1,0:T(1,128)} %param.21) | copy-start | bytes 28
  7.2 73.4 %all-gather.12.cloned.1.call-start = ((), (), s32[]{:S(2)}) async-start(), calls=%async_computation.13 | async-start | bytes 2162688 | tf_op jit(solution)/shard_map/all_gather | solution.py:143
  9.6 12.9 copy-start.48
  11.7 10.8 all-to-all-start
  22.5 55.0 %all-to-all-start.1 = ((bf16[8,64,1024]{2,1,0:T(8,128)(2,1)}), bf16[8,64,1024]{2,1,0:T(8,128)(2,1)S(1)}, u32[]{:S(2)}, u32[]{:S(2)}) async-start(bf16[8,64,1024]{2,1,0:T(8,128)(2,1)} %bitcast.4), calls=%async_computation.1 | async-start | bytes 2097152 | tf_op jit(solution)/shard_map/all_to_all | solution.py:117
  26.1 108.2 %all-gather.16.cloned.1.call-start = ((), (), s32[]{:S(2)}) async-start(), calls=%async_computation.15 | async-start | bytes 2162688 | tf_op jit(solution)/shard_map/all_gather | solution.py:144
  26.8 130.0 %all-gather.14.cloned.1.call-start = ((), (), s32[]{:S(2)}) async-start(), calls=%async_computation.14 | async-start | bytes 2621440 | tf_op jit(solution)/shard_map/all_gather | solution.py:161
  74.8 8.9 copy-start.43
  75.6 182.0 %copy-start.21 = (f32[256,128]{1,0:T(8,128)}, f32[256,128]{1,0:T(8,128)S(1)}, u32[]{:S(2)}) copy-start(f32[256,128]{1,0:T(8,128)S(1)} %get-tuple-element.250) | copy-start | bytes 393220
  80.3 166.8 %copy-start.2 = (bf16[256,1024]{1,0:T(8,128)(2,1)}, bf16[256,1024]{1,0:T(8,128)(2,1)S(1)}, u32[]{:S(2)}) copy-start(bf16[256,1024]{1,0:T(8,128)(2,1)S(1)} %scatter_custom_fusion.2) | copy-start | bytes 1572868
  80.5 2.6 copy-start.41
  80.6 166.6 %copy-start.35 = (f32[256]{0:T(256)}, f32[256]{0:T(256)S(1)}, u32[]{:S(2)}) copy-start(f32[256]{0:T(256)S(1)} %fusion.101) | copy-start | bytes 3076
  86.6 94.8 %all-gather.18.cloned.1.call-start = ((), (), s32[]{:S(2)}) async-start(), calls=%async_computation.16 | async-start | bytes 2621440 | tf_op jit(solution)/shard_map/all_gather | solution.py:162
  137.5 109.7 %all-gather.10.cloned.1.call-start = ((), (), s32[]{:S(2)}) async-start(), calls=%async_computation.12 | async-start | bytes 4325376 | tf_op jit(solution)/shard_map/all_gather | solution.py:142
  138.1 174.2 %all-gather.20.cloned.1.call-start = ((), (), s32[]{:S(2)}) async-start(), calls=%async_computation.17 | async-start | bytes 4325376 | tf_op jit(solution)/shard_map/all_gather | solution.py:147
  138.6 243.0 %all-gather.22.cloned.1.call-start = ((), (), s32[]{:S(2)}) async-start(), calls=%async_computation.18 | async-start | bytes 6488064 | tf_op jit(solution)/shard_map/all_gather | solution.py:192
  139.4 313.2 %all-gather.24.cloned.1.call-start = ((), (), s32[]{:S(2)}) async-start(), calls=%async_computation.19 | async-start | bytes 6488064 | tf_op jit(solution)/shard_map/all_gather | solution.py:193
  140.1 383.3 %all-gather.26.cloned.1.call-start = ((), (), s32[]{:S(2)}) async-start(), calls=%async_computation.20 | async-start | bytes 6488064 | tf_op jit(solution)/shard_map/all_gather | solution.py:194
  140.9 543.0 %reduce-scatter.10.cloned.1.call-start = ((), (), s32[]{:S(2)}) async-start(), calls=%async_computation.21 | async-start | bytes 2621440 | tf_op jit(solution)/shard_map/reduce_scatter | solution.py:270
  142.0 18.1 %copy-start.45 = (f32[128]{0:T(128)}, f32[128]{0:T(128)S(1)}, u32[]{:S(2)}) copy-start(f32[128]{0:T(128)S(1)} %convert_element_type.133) | copy-start | bytes 1540
  252.0 5.0 copy-start
  255.5 3.0 copy-start.19
  258.4 1.6 copy-start.12
  258.4 1.6 copy-start.40
  265.2 47.9 %copy-start.3 = (bf16[256,1024]{1,0:T(8,128)(2,1)S(1)}, bf16[256,1024]{1,0:T(8,128)(2,1)}, u32[]{:S(2)}) copy-start(bf16[256,1024]{1,0:T(8,128)(2,1)} %copy-done.2) | copy-start | bytes 1572868
  313.2 3.9 copy-start.39
  317.1 225.0 %copy-start.17 = (f32[256,1024]{1,0:T(8,128)}, f32[256,1024]{1,0:T(8,128)S(1)}, u32[]{:S(2)}) copy-start(f32[256,1024]{1,0:T(8,128)S(1)} %get-tuple-element.254) | copy-start | bytes 3145732
  317.3 135.3 %copy-start.13 = (bf16[256,1024]{1,0:T(8,128)(2,1)}, bf16[256,1024]{1,0:T(8,128)(2,1)S(1)}, u32[]{:S(2)}) copy-start(bf16[256,1024]{1,0:T(8,128)(2,1)S(1)} %multiply_convert_fusion.3) | copy-start | bytes 1572868
  387.9 135.6 %copy-start.27 = (bf16[256,1024]{1,0:T(8,128)(2,1)S(1)}, bf16[256,1024]{1,0:T(8,128)(2,1)}, u32[]{:S(2)}) copy-start(bf16[256,1024]{1,0:T(8,128)(2,1)} %param.22) | copy-start | bytes 1572868
  533.3 5.8 copy-start.33
  533.3 5.8 copy-start.32
  533.3 5.8 copy-start.52
  539.1 4.2 copy-start.53
  655.2 30.1 %copy-start.22 = (f32[256,128]{1,0:T(8,128)S(1)}, f32[256,128]{1,0:T(8,128)}, u32[]{:S(2)}) copy-start(f32[256,128]{1,0:T(8,128)} %copy-done.21) | copy-start | bytes 393220
  655.2 62.8 %reduce-scatter.12.cloned.1.call-start = ((), (), s32[]{:S(2)}) async-start(), calls=%async_computation.22 | async-start | bytes 2621440 | tf_op jit(solution)/shard_map/reduce_scatter | solution.py:273
  656.0 199.1 %reduce-scatter.16.cloned.1.call-start = ((), (), s32[]{:S(2)}) async-start(), calls=%async_computation.24 | async-start | bytes 4325376 | tf_op jit(solution)/shard_map/reduce_scatter | solution.py:301
  686.3 1.7 copy-start.38
  687.9 2.0 copy-start.4
  687.9 2.0 copy-start.36
  692.8 302.1 %reduce-scatter.18.cloned.1.call-start = ((), (), s32[]{:S(2)}) async-start(), calls=%async_computation.25 | async-start | bytes 4325376 | tf_op jit(solution)/shard_map/reduce_scatter | solution.py:302
  722.0 1.6 copy-start.8
  722.0 420.4 %reduce-scatter.14.cloned.1.call-start = ((), (), s32[]{:S(2)}) async-start(), calls=%async_computation.23 | async-start | bytes 8650752 | tf_op jit(solution)/shard_map/reduce_scatter | solution.py:300
  724.8 1.6 copy-start.1
  724.8 2.2 copy-start.9
  724.8 2.2 copy-start.20
  724.9 2.2 copy-start.46
  727.1 5.9 copy-start.34
  733.1 4.3 copy-start.5
  742.1 1.5 copy-start.31
  742.1 547.5 %reduce-scatter.20.cloned.1.call-start = ((), (), s32[]{:S(2)}) async-start(), calls=%async_computation.26 | async-start | bytes 8650752 | tf_op jit(solution)/shard_map/reduce_scatter | solution.py:305
  748.2 708.6 %reduce-scatter.22.cloned.1.call-start = ((), (), s32[]{:S(2)}) async-start(), calls=%async_computation.27 | async-start | bytes 12976128 | tf_op jit(solution)/shard_map/reduce_scatter | solution.py:222
  757.0 861.8 %reduce-scatter.24.cloned.1.call-start = ((), (), s32[]{:S(2)}) async-start(), calls=%async_computation.28 | async-start | bytes 12976128 | tf_op jit(solution)/shard_map/reduce_scatter | solution.py:223
  764.9 1014.9 %reduce-scatter.26.cloned.1.call-start = ((), (), s32[]{:S(2)}) async-start(), calls=%async_computation.29 | async-start | bytes 12976128 | tf_op jit(solution)/shard_map/reduce_scatter | solution.py:224
  775.0 3.6 copy-start.10
  778.7 1.8 copy-start.26
  784.6 5.4 copy-start.49
  784.6 5.4 copy-start.18
  784.6 59.6 %all-to-all-start.2 = ((bf16[8,64,1024]{2,1,0:T(8,128)(2,1)}), bf16[8,64,1024]{2,1,0:T(8,128)(2,1)S(1)}, u32[]{:S(2)}, u32[]{:S(2)}) async-start(bf16[8,64,1024]{2,1,0:T(8,128)(2,1)} %bitcast.28), calls=%async_computation.4 | async-start | bytes 2097152 | tf_op jit(solution)/shard_map/all_to_all | solution.py:309
  790.0 6.0 copy-start.50
  790.0 6.0 copy-start.51
  (16 other events, 16.7 us)
Sparse Core Ops, SparseCore 0:
  10.9 65.2 all-gather.11
  79.0 55.2 all-gather.15
  136.4 20.2 all-gather.13
  158.8 22.5 all-gather.17
  184.1 62.9 all-gather.9
  249.9 60.6 all-gather.19
  313.4 68.2 all-gather.21
  384.5 67.9 all-gather.23
  455.4 68.0 all-gather.25
  655.3 28.5 reduce-scatter.9
  686.6 31.4 reduce-scatter.11
  720.8 134.2 reduce-scatter.15
  857.9 136.9 reduce-scatter.17
  997.6 144.8 reduce-scatter.13
  1145.2 144.3 reduce-scatter.19
  1296.1 160.7 reduce-scatter.21
  1464.3 154.4 reduce-scatter.23
  1625.3 154.4 reduce-scatter.25
where the time goes:
time: 1800 us; the launch traced here: 1790 us
  waiting for transfers between devices  1330 us (74%)
  matrix products  200 us (11%)
  blocking collectives  92.6 us (5%)
  local copies, waits for them, and re-layouts  67.1 us (4%)
  other arithmetic  62 us (3%)
    reduce_scatter x1, waiting for transfers between devices, local(): lax.psum_scatter(grad_gate_full, ('dp', 'ctx'), scatter_dimension=0, tile...  167 us
    reduce_scatter x1, waiting for transfers between devices, local(): lax.psum_scatter(grad_up_full, ('dp', 'ctx'), scatter_dimension=0, tiled=...  162 us
    reduce_scatter x1, waiting for transfers between devices, local(): lax.psum_scatter(grad_down_full, ('dp', 'ctx'), scatter_dimension=0, tile...  161 us
    reduce_scatter x1, waiting for transfers between devices, local(): lax.psum_scatter(grad_query_full, ('dp', 'ctx'), scatter_dimension=0, til...  148 us
    reduce_scatter x1, waiting for transfers between devices, local(): lax.psum_scatter(grad_out_full, ('dp', 'ctx'), scatter_dimension=0, tiled...  147 us
    reduce_scatter x1, waiting for transfers between devices, local(): lax.psum_scatter(grad_value_full, ('dp', 'ctx'), scatter_dimension=0, til...  140 us
    unnamed x2, blocking collectives  92.6 us
    all_gather x1, waiting for transfers between devices, local(): lax.all_gather(w_up, ('dp', 'ctx'), axis=0, tiled=True)  64.7 us
  transfers between devices with their start and end apart: 21, of which 17 were waited for; matrix products, arithmetic and copies ran while one was open for 10% of the time, Pallas kernels for 0%

commit v1 on v0

v1 whole, which is shorter than its diff:
```python
import functools
import math

import jax
import jax.numpy as jnp
import numpy as np
from jax import lax
from jax.experimental import pallas as pl
from jax.experimental.pallas import tpu as pltpu
from jax.sharding import PartitionSpec as P

H = 16
KVH = 8
HD = 128
EPS = 1e-06
THETA = 1000000.0
MASKED = -1e30
QB = 256
SCALE = HD ** (-0.5)
LOG2E = math.log2(math.e)
BF = jnp.bfloat16
F32 = jnp.float32
BOTH = ("dp", "ctx")
VMEM_LIMIT = 60 << 20


def dot(a, b):
    return lax.dot_general(a, b, (((1,), (0,)), ((), ())), preferred_element_type=F32)


def dot_nt(a, b):
    return lax.dot_general(a, b, (((1,), (1,)), ((), ())), preferred_element_type=F32)


def dot_tn(a, b):
    return lax.dot_general(a, b, (((0,), (0,)), ((), ())), preferred_element_type=F32)


def lanes(start, size):
    return pl.ds(pl.multiple_of(start * size, size), size)


def rope_tables(rows):
    inverse = np.exp(np.arange(HD // 2, dtype=np.float32) * np.float32(-2.0 / HD * math.log(THETA)))
    doubled = np.concatenate([inverse, inverse]).astype(np.float32)
    angles = np.arange(rows, dtype=np.float32)[:, None] * doubled[None, :]
    sign = np.where(np.arange(HD) < HD // 2, -1.0, 1.0).astype(np.float32)
    return np.cos(angles), np.sin(angles) * sign[None, :]


def mask_block(off_bias):
    rows = lax.broadcasted_iota(jnp.int32, (QB, QB), 0)
    cols = lax.broadcasted_iota(jnp.int32, (QB, QB), 1)
    return jnp.where(rows == cols, 0.0, jnp.where(cols < rows, off_bias, MASKED))


def attn_fwd_body(
    x_ref, wqkv_ref, wo_ref, ga_ref, gq_ref, gk_ref, cos_ref, sin_ref, bias_ref,
    part_ref, q_ref, k_ref, v_ref, p_ref, xn_ref, att_ref, mask_ref,
):
    rows = x_ref.shape[0]
    nq = q_ref.shape[1] // HD
    nk = k_ref.shape[1] // HD
    gain_a = ga_ref[...]

    @pl.loop(0, rows // QB)
    def _(i):
        here = lanes(i, QB)
        x = x_ref[here, :].astype(F32)
        r = lax.rsqrt(jnp.mean(x * x, axis=-1, keepdims=True) + EPS)
        xn = (x * r * gain_a).astype(BF)
        xn_ref[here, :] = xn
        p = dot(xn, wqkv_ref[...])
        p_ref[here, :] = p[:, : (nq + nk) * HD]
        v_ref[here, :] = p[:, (nq + nk) * HD :].astype(BF)
        cos = cos_ref[here, :]
        sin = sin_ref[here, :]
        for h in range(nq + nk):
            ph = p[:, h * HD : (h + 1) * HD]
            g = gq_ref[...] if h < nq else gk_ref[...]
            n = ph * lax.rsqrt(jnp.mean(ph * ph, axis=-1, keepdims=True) + EPS) * g
            rot = (n * cos + pltpu.roll(n, HD // 2, 1) * sin).astype(BF)
            if h < nq:
                q_ref[here, h * HD : (h + 1) * HD] = rot
            else:
                k_ref[here, (h - nq) * HD : (h - nq + 1) * HD] = rot

    off = bias_ref[0:1, 0:1]
    mask_ref[...] = mask_block(off)

    @pl.loop(0, nq)
    def _(h):
        hq = lanes(h, HD)
        hk = lanes(lax.div(h * nk, nq), HD)
        for i in range(rows // QB):
            q = q_ref[i * QB : (i + 1) * QB, hq]
            es, total = [], None
            for j in range(i + 1):
                s = dot_nt(q, k_ref[j * QB : (j + 1) * QB, hk]) * (SCALE * LOG2E)
                e = jnp.exp2(s + (mask_ref[...] if j == i else off))
                t = jnp.sum(e, axis=-1, keepdims=True)
                total = t if total is None else total + t
                es.append(e)
            inv = 1.0 / total
            o = None
            for j in range(i + 1):
                c = dot((es[j] * inv).astype(BF), v_ref[j * QB : (j + 1) * QB, hk])
                o = c if o is None else o + c
            att_ref[i * QB : (i + 1) * QB, hq] = o.astype(BF)

    @pl.loop(0, rows // QB)
    def _(i):
        here = lanes(i, QB)
        part_ref[here, :] = dot(att_ref[here, :], wo_ref[...]).astype(BF)


def attn_bwd_body(
    db_ref, wo_ref, wqkv_ref, q_ref, k_ref, v_ref, p_ref, xn_ref, att_ref,
    gq_ref, gk_ref, cos_ref, sin_ref, bias_ref,
    gwqkv_ref, gwo_ref, dxn_ref, ggq_ref, ggk_ref,
    mask_ref, da_ref, dq_ref, dk_ref, dv_ref, dp_ref,
):
    rows = db_ref.shape[0]
    nq = q_ref.shape[1] // HD
    nk = k_ref.shape[1] // HD
    group = nq // nk

    @pl.loop(0, rows // QB)
    def _(i):
        here = lanes(i, QB)
        da_ref[here, :] = dot_nt(db_ref[here, :], wo_ref[...]).astype(BF)

    off = bias_ref[0:1, 0:1]
    mask_ref[...] = mask_block(off)
    dk_ref[...] = jnp.zeros_like(dk_ref)
    dv_ref[...] = jnp.zeros_like(dv_ref)

    @pl.loop(0, nq)
    def _(h):
        hq = lanes(h, HD)
        hk = lanes(lax.div(h, group), HD)
        for i in range(rows // QB):
            here = slice(i * QB, (i + 1) * QB)
            q = q_ref[here, hq]
            da = da_ref[here, hq]
            inner = jnp.sum(da.astype(F32) * att_ref[here, hq].astype(F32), axis=-1, keepdims=True)
            es, total = [], None
            for j in range(i + 1):
                s = dot_nt(q, k_ref[j * QB : (j + 1) * QB, hk]) * (SCALE * LOG2E)
                e = jnp.exp2(s + (mask_ref[...] if j == i else off))
                t = jnp.sum(e, axis=-1, keepdims=True)
                total = t if total is None else total + t
                es.append(e)
            inv = 1.0 / total
            dq = None
            for j in range(i + 1):
                keys = slice(j * QB, (j + 1) * QB)
                probs = es[j] * inv
                ds = (probs * (dot_nt(da, v_ref[keys, hk]) - inner)).astype(BF)
                c = dot(ds, k_ref[keys, hk])
                dq = c if dq is None else dq + c
                dk_ref[keys, hk] += dot_tn(ds, q)
                dv_ref[keys, hk] += dot_tn(probs.astype(BF), da)
            dq_ref[here, hq] = dq

    ggq_ref[...] = jnp.zeros_like(ggq_ref)
    ggk_ref[...] = jnp.zeros_like(ggk_ref)

    @pl.loop(0, rows // QB)
    def _(i):
        here = lanes(i, QB)
        cos = cos_ref[here, :]
        sin = sin_ref[here, :]
        sums = [jnp.zeros((1, HD), F32), jnp.zeros((1, HD), F32)]
        for h in range(nq + nk):
            which = 0 if h < nq else 1
            g = (gq_ref if h < nq else gk_ref)[...]
            cols = slice(h * HD, (h + 1) * HD)
            if h < nq:
                d = dq_ref[here, cols] * SCALE
            else:
                d = dk_ref[here, (h - nq) * HD : (h - nq + 1) * HD] * SCALE
            dn = d * cos + pltpu.roll(d * sin, HD // 2, 1)
            ph = p_ref[here, cols]
            r = lax.rsqrt(jnp.mean(ph * ph, axis=-1, keepdims=True) + EPS)
            nh = ph * r
            sums[which] += jnp.sum(dn * nh, axis=0, keepdims=True)
            cg = dn * g
            dp_ref[here, cols] = (r * (cg - nh * jnp.mean(cg * nh, axis=-1, keepdims=True))).astype(BF)
        dp_ref[here, (nq + nk) * HD :] = dv_ref[here, :].astype(BF)
        ggq_ref[0:1, :] += sums[0]
        ggk_ref[0:1, :] += sums[1]
        dxn_ref[here, :] = dot_nt(dp_ref[here, :], wqkv_ref[...]).astype(BF)

    @pl.loop(0, gwo_ref.shape[0] // 128)
    def _(i):
        cols = lanes(i, 128)
        gwo_ref[cols, :] = dot_tn(att_ref[:, cols], db_ref[...]).astype(BF)

    @pl.loop(0, gwqkv_ref.shape[0] // 128)
    def _(i):
        cols = lanes(i, 128)
        gwqkv_ref[cols, :] = dot_tn(xn_ref[:, cols], dp_ref[...]).astype(BF)


def shape(*dims, dtype=BF):
    return jax.ShapeDtypeStruct(dims, dtype)


def in_vmem(body, outs, scratch, name):
    return pl.pallas_call(
        body,
        out_shape=outs,
        scratch_shapes=scratch,
        compiler_params=pltpu.CompilerParams(vmem_limit_bytes=VMEM_LIMIT),
        name=name,
    )


def slab_moves(n_data):
    return [(s, (s % n_data) * 4 + s // n_data) for s in range(4 * n_data)]


def to_quarters(weight):
    rows, cols = weight.shape
    return weight.reshape(rows, 4, cols // 4).transpose(1, 0, 2)


def from_quarters(blocks):
    n, rows, cols = blocks.shape
    return blocks.transpose(1, 0, 2).reshape(rows, n * cols)


def rms_back(c, v, gain):
    r = lax.rsqrt(jnp.mean(v * v, axis=-1, keepdims=True) + EPS)
    n = v * r
    cg = c * gain
    return jnp.sum(c * n, axis=0), r * (cg - n * jnp.mean(cg * n, axis=-1, keepdims=True))


def local(
    layer_input, dest_slot, doc_len, out_grad, attn_gain, w_query, w_key, w_value, q_gain, k_gain,
    w_out, mlp_gain, w_gate, w_up, w_down,
):
    tok, width = layer_input.shape
    n = lax.axis_size("dp")
    cap = 2 * tok // n
    rows = 4 * tok
    owner = dest_slot // (4 * tok)
    slot = dest_slot % tok
    hot = (owner[:, None] == jnp.arange(n, dtype=jnp.int32)[None, :]).astype(BF)
    lower = (jnp.arange(tok)[:, None] > jnp.arange(tok)[None, :]).astype(BF)
    rank = jnp.sum(dot(lower, hot) * hot.astype(F32), axis=1).astype(jnp.int32)
    send_slot = owner * cap + rank
    place = send_slot[:, None] == jnp.arange(n * cap, dtype=jnp.int32)[None, :]
    outgoing = dot_tn(place.astype(BF), layer_input).astype(BF)
    labels = jnp.sum(jnp.where(place, slot[:, None] - tok, 0), axis=0, dtype=jnp.int32) + tok
    received = lax.all_to_all(outgoing.reshape(n, cap, width), "dp", 0, 0, tiled=True).reshape(n * cap, width)
    in_labels = lax.all_to_all(labels.reshape(n, cap), "dp", 0, 0, tiled=True).reshape(-1)
    pick = (jnp.arange(tok, dtype=jnp.int32)[:, None] == in_labels[None, :]).astype(BF)
    owned = dot(pick, received).astype(BF)
    x_all = lax.all_gather(owned, "ctx", axis=0, tiled=True)
    og_all = lax.all_gather(out_grad, "ctx", axis=0, tiled=True)
    gains = lax.all_gather(jnp.concatenate([attn_gain, mlp_gain, q_gain, k_gain])[None, :], BOTH, axis=0, tiled=True)
    g_rows, g_heads = attn_gain.shape[0], q_gain.shape[0]
    gains = gains.astype(F32)
    ga = gains[:, :g_rows].reshape(1, width)
    gm = gains[:, g_rows : 2 * g_rows].reshape(1, width)
    gq = gains[:, 2 * g_rows : 2 * g_rows + g_heads].reshape(1, HD)
    gk = gains[:, 2 * g_rows + g_heads :].reshape(1, HD)
    qkv = jnp.concatenate([to_quarters(w_query), to_quarters(w_key), to_quarters(w_value)], axis=2)
    gu = jnp.concatenate([to_quarters(w_gate), to_quarters(w_up)], axis=2)
    qkv = lax.all_to_all(qkv, "ctx", 0, 0, tiled=True).reshape(-1, qkv.shape[2])
    gu = lax.all_to_all(gu, "ctx", 0, 0, tiled=True).reshape(-1, gu.shape[2])
    wo, wd = (lax.ppermute(w, BOTH, slab_moves(n)) for w in (w_out, w_down))
    wqkv, wo, wgu, wd = (lax.all_gather(w, "dp", axis=0, tiled=True) for w in (qkv, wo, gu, wd))
    cos, sin = rope_tables(rows)
    bias = jnp.where(doc_len[0, 0] > 0, 0.0, MASKED).astype(F32).reshape(1, 1) + jnp.zeros((8, 128), F32)
    part, q, k, v, p, xn, att = in_vmem(
        attn_fwd_body,
        (shape(rows, width), shape(rows, 512), shape(rows, 256), shape(rows, 256),
         shape(rows, 768, dtype=F32), shape(rows, width), shape(rows, 512)),
        [pltpu.VMEM((QB, QB), F32)],
        "attn_fwd",
    )(x_all, wqkv, wo, ga, gq, gk, cos, sin, bias)
    x_own = owned.astype(F32)
    middle = x_own + lax.psum_scatter(part, "ctx", scatter_dimension=0, tiled=True).astype(F32)
    normed = (middle * lax.rsqrt(jnp.mean(middle * middle, axis=-1, keepdims=True) + EPS) * gm).astype(BF)
    nm = lax.all_gather(normed, "ctx", axis=0, tiled=True)
    ff = wd.shape[0]
    wg, wu = wgu[:, :ff], wgu[:, ff:]
    gate, up = dot(nm, wg), dot(nm, wu)
    s = jax.nn.sigmoid(gate)
    silu = gate * s
    hidden = (silu * up).astype(BF)
    out_part = dot(hidden, wd).astype(BF)
    dh = dot_nt(og_all, wd)
    d_gate = (dh * up * s * (1.0 + gate * (1.0 - s))).astype(BF)
    d_up = (dh * silu).astype(BF)
    gwd = dot_tn(hidden, og_all).astype(BF)
    gwgu = jnp.concatenate([dot_tn(nm, d_gate), dot_tn(nm, d_up)], axis=1).astype(BF)
    dnm_part = (dot_nt(d_gate, wg) + dot_nt(d_up, wu)).astype(BF)
    dnm = lax.psum_scatter(dnm_part, "ctx", scatter_dimension=0, tiled=True).astype(F32)
    layer_output = (middle + lax.psum_scatter(out_part, "ctx", scatter_dimension=0, tiled=True).astype(F32)).astype(BF)
    ggm, d_mid = rms_back(dnm, middle, gm)
    d_middle = out_grad.astype(F32) + d_mid
    db = lax.all_gather(d_middle.astype(BF), "ctx", axis=0, tiled=True)
    gwqkv, gwo, dxn_part, ggq, ggk = in_vmem(
        attn_bwd_body,
        (shape(width, 1024), shape(512, width), shape(rows, width), shape(8, HD, dtype=F32), shape(8, HD, dtype=F32)),
        [pltpu.VMEM((QB, QB), F32), pltpu.VMEM((rows, 512), BF), pltpu.VMEM((rows, 512), F32),
         pltpu.VMEM((rows, 256), F32), pltpu.VMEM((rows, 256), F32), pltpu.VMEM((rows, 1024), BF)],
        "attn_bwd",
    )(db, wo, wqkv, q, k, v, p, xn, att, gq, gk, cos, sin, bias)
    dxn = lax.psum_scatter(dxn_part, "ctx", scatter_dimension=0, tiled=True).astype(F32)
    gga, d_x = rms_back(dxn, x_own, ga)
    owned_grad = (d_middle + d_x).astype(BF)
    picked = dot_tn(pick, owned_grad).astype(BF)
    returned = lax.all_to_all(picked.reshape(n, cap, width), "dp", 0, 0, tiled=True).reshape(n * cap, width)
    input_grad = dot(place.astype(BF), returned).astype(BF)
    gwqkv, gwo, gwgu, gwd = (lax.psum_scatter(g, "dp", scatter_dimension=0, tiled=True) for g in (gwqkv, gwo, gwgu, gwd))
    gwo, gwd = (lax.ppermute(g, BOTH, [(b, a) for a, b in slab_moves(n)]).astype(F32) for g in (gwo, gwd))
    gwqkv = lax.all_to_all(gwqkv.reshape(4, -1, 1024), "ctx", 0, 0, tiled=True).astype(F32)
    gwgu = lax.all_to_all(gwgu.reshape(4, -1, 2 * ff), "ctx", 0, 0, tiled=True).astype(F32)
    small = [gga.reshape(4 * n, g_rows), ggm.reshape(4 * n, g_rows), ggq[0].reshape(4 * n, g_heads), ggk[0].reshape(4 * n, g_heads)]
    small = lax.psum_scatter(jnp.concatenate(small, axis=1), BOTH, scatter_dimension=0, tiled=True)[0]
    return (
        layer_output,
        input_grad,
        small[:g_rows],
        from_quarters(gwqkv[:, :, :512]),
        from_quarters(gwqkv[:, :, 512:768]),
        from_quarters(gwqkv[:, :, 768:]),
        small[2 * g_rows : 2 * g_rows + g_heads],
        small[2 * g_rows + g_heads :],
        gwo,
        small[g_rows : 2 * g_rows],
        from_quarters(gwgu[:, :, :ff]),
        from_quarters(gwgu[:, :, ff:]),
        gwd,
    )


def solution(mesh):
    rows = P(BOTH, None)
    vec = P(BOTH)
    return jax.shard_map(
        local,
        mesh=mesh,
        in_specs=(rows, vec, P("dp", None), rows, vec, rows, rows, rows, vec, vec, rows, vec, rows, rows, rows),
        out_specs=(rows, rows, vec, rows, rows, rows, vec, vec, rows, vec, rows, rows, rows),
        check_vma=False,
    )
```

time: 1800 us -> 862 us (0.48)
  waiting for transfers between devices: 1330 us -> 558 us
  matrix products: 200 us -> 45.5 us
  Pallas kernels: 0 us -> 59.3 us
  other arithmetic: 62 us -> 14.7 us
  local copies, waits for them, and re-layouts: 67.1 us -> 20.1 us
  starting transfers between devices: 15.8 us -> 47.1 us
    reduce_scatter x9 -> x8, waiting for transfers between devices: 987 us -> 323 us  [the longest x4 218 us: local(): lax.psum_scatter(g, 'dp', scatter_dimension=0, tiled=True)]
    all_gather x9 -> x8, waiting for transfers between devices: 339 us -> 175 us  [the longest x4 95.2 us: local(): lax.all_gather(w, 'dp', axis=0, tiled=True)]
    dot_general x77 -> x14, matrix products: 200 us -> 45.5 us  [the longest x6 16.9 us: dot(): lax.dot_general(a, b, (((1,), (0,)), ((), ())), preferred_element_type=F32)]
    pallas_call x0 -> x2, Pallas kernels: none -> 59.3 us  [the longest x1 40.3 us: local(): in_vmem(attn_bwd_body, (shape(width, 1024), shape(512, width), shape(rows...]
    all_to_all x3 -> x5, waiting for transfers between devices: 2.06 us -> 37.3 us  [the longest x1 32.6 us: local(): lax.all_to_all(outgoing.reshape(n, cap, width), 'dp', 0, 0, tiled=True)]
    ppermute x0 -> x4, starting transfers between devices: none -> 21.9 us  [the longest x2 11.5 us: local(): lax.ppermute(g, BOTH, [(b, a) for a, b in slab_moves(n)]).astype(F32)]
    all_to_all x0 -> x2, blocking collectives: none -> 20.8 us  [the longest x1 10.4 us: local(): qkv = lax.all_to_all(qkv, 'ctx', 0, 0, tiled=True).reshape(-1, qkv.shape[2])]
    ppermute x0 -> x4, waiting for transfers between devices: none -> 19.8 us  [the longest x2 12.2 us: local(): wo, wd = (lax.ppermute(w, BOTH, slab_moves(n)) for w in (w_out, w_down))]
  transfers between devices with their start and end apart: 21 -> 25, of which waited for: 17 -> 22; matrix products, arithmetic and copies ran while one was open for 10% -> 7% of each run, Pallas kernels for 0% -> 5%
where the time goes in v1:
time: 862 us; the launch traced here: 860 us
  waiting for transfers between devices  558 us (65%)
  blocking collectives  101 us (12%)
  Pallas kernels  59.3 us (7%)
  starting transfers between devices  47.1 us (5%)
  matrix products  45.5 us (5%)
  local copies, waits for them, and re-layouts  20.1 us (2%)
  other arithmetic  14.7 us (2%)
  between operations  14.4 us (2%)
    reduce_scatter x4, waiting for transfers between devices, local(): lax.psum_scatter(g, 'dp', scatter_dimension=0, tiled=True)  218 us
    all_gather x4, waiting for transfers between devices, local(): lax.all_gather(w, 'dp', axis=0, tiled=True)  95.2 us
    unnamed x2, blocking collectives  80 us
    pallas_call x1, Pallas kernels, local(): in_vmem(attn_bwd_body, (shape(width, 1024), shape(512, width), shape(rows...  40.3 us
    all_to_all x1, waiting for transfers between devices, local(): lax.all_to_all(outgoing.reshape(n, cap, width), 'dp', 0, 0, tiled=True)  32.6 us
    reduce_scatter x1, waiting for transfers between devices, local(): lax.psum_scatter(out_part, 'ctx', scatter_dimension=0, tiled=True)  32.2 us
    reduce_scatter x1, waiting for transfers between devices, local(): lax.psum_scatter(dxn_part, 'ctx', scatter_dimension=0, tiled=True)  27.9 us
    reduce_scatter x1, waiting for transfers between devices, local(): lax.psum_scatter(dnm_part, 'ctx', scatter_dimension=0, tiled=True)  26.2 us
  transfers between devices with their start and end apart: 25, of which 22 were waited for; matrix products, arithmetic and copies ran while one was open for 7% of the time, Pallas kernels for 5%

profile of v1, /device:TPU:3, one launch (start us, length us, event | category | flops | bytes accessed | tf_op | source)
XLA Modules:
  0.0 859.5 jit_solution(10919038254015093699)
XLA Ops:
  7.2 4.8 collective-permute-start
  12.1 5.8 collective-permute-done
  18.6 0.9 copy.88
  19.5 0.9 bitcast_bitcast_fusion.1
  20.4 10.4 %all_to_all.36 = bf16[4,32,1024]{2,1,0:T(8,128)(2,1)} all-to-all(bf16[4,32,1024]{2,1,0:T(8,128)(2,1)S(1)} %pad_maximum_fusion.2), channel_id=1, replica_groups=mesh['dp'=8,'ctx'=4] {'ctx'}, dimensions={0} | all-to-all | bytes 524288 | tf_op jit(solution)/shard_map/all_to_all | solution.py:273
  32.6 5.8 all-to-all-start
  38.4 1.6 convolution_convert_fusion.5
  40.0 3.7 all-to-all-done
  43.7 3.7 all-to-all-start.1
  48.7 32.6 %all-to-all-done.1 = bf16[8,64,1024]{2,1,0:T(8,128)(2,1)S(1)} async-done(((bf16[8,64,1024]{2,1,0:T(8,128)(2,1)}), bf16[8,64,1024]{2,1,0:T(8,128)(2,1)S(1)}, u32[]{:S(2)}, u32[]{:S(2)}) %all-to-all-start.1) | async-done | bytes 1048608 | tf_op jit(solution)/shard_map/all_to_all | solution.py:258
  81.3 1.2 convolution_convert_fusion.7
  83.0 38.1 %all-reduce = bf16[2304]{0:T(1024)(128)(2,1)S(1)} all-reduce(bf16[2304]{0:T(1024)(128)(2,1)S(1)} %dynamic-update-slice), channel_id=2, replica_groups=mesh['dp'=8,'ctx'=4] {'dp','ctx'}, use_global_device_ids=true, to_apply=%add | all-reduce | flops 2304 | bytes 9216
  123.3 2.5 all-gather.12.cloned.1.call-done.wqkv_ref
  125.9 23.6 %all-gather.10.cloned.1.call-done.x_ref = bf16[1024,1024]{1,0:T(8,128)(2,1)} async-done(((bf16[256,1024]{1,0:T(8,128)(2,1)}), bf16[1024,1024]{1,0:T(8,128)(2,1)}) %all-gather.10.cloned.1.call-update) | async-done | bytes 2097168 | tf_op jit(solution)/shard_map/all_gather | solution.py:262
  150.1 18.9 %attn_fwd.1 = (bf16[1024,1024]{1,0:T(8,128)(2,1)}, bf16[1024,512]{1,0:T(8,128)(2,1)}, bf16[1024,256]{1,0:T(8,128)(2,1)}, bf16[1024,256]{1,0:T(8,128)(2,1)}, f32[...) custom-call(bf16[1024,1024]{1,0:T(8,128)(2,1)} %all-gather.10.cloned.1.call-done.x_ref, ...), custom_call_target="tpu_custom_call" | custom-call | tf_op jit(solution)/shard_map/attn_fwd/pallas_call | solution.py:279
  169.1 0.8 copy-done.6
  170.5 10.3 %all_to_all.37 = bf16[4,32,1536]{2,1,0:T(8,128)(2,1)} all-to-all(bf16[4,32,1536]{2,1,0:T(8,128)(2,1)S(1)} %copy.68), channel_id=1, replica_groups=mesh['dp'=8,'ctx'=4] {'ctx'}, dimensions={0} | all-to-all | bytes 786432 | tf_op jit(solution)/shard_map/all_to_all | solution.py:274
  181.0 19.5 %reduce-scatter.11.cloned.1.call-done = bf16[256,1024]{1,0:T(8,128)(2,1)} async-done(((bf16[1024,1024]{1,0:T(8,128)(2,1)}), bf16[256,1024]{1,0:T(8,128)(2,1)}) %reduce-scatter.11.cloned.1.call-update) | async-done | bytes 524304 | tf_op jit(solution)/shard_map/reduce_scatter | solution.py:287
  200.5 1.3 multiply_reduce_fusion
  201.8 2.0 multiply_convert_fusion.3
  203.9 5.6 collective-permute-start.1
  209.5 6.4 collective-permute-done.1
  217.5 54.5 %all-gather.18.cloned.1.call-done = bf16[1024,1536]{1,0:T(8,128)(2,1)} async-done(((bf16[128,1536]{1,0:T(8,128)(2,1)}), bf16[1024,1536]{1,0:T(8,128)(2,1)}) %all-gather.18.cloned.1.call-update) | async-done | bytes 3145744 | tf_op jit(solution)/shard_map/all_gather | solution.py:276
  272.0 23.4 %all-gather.16.cloned.1.call-done = bf16[1024,1024]{1,0:T(8,128)(2,1)} async-done(((bf16[256,1024]{1,0:T(8,128)(2,1)}), bf16[1024,1024]{1,0:T(8,128)(2,1)}) %all-gather.16.cloned.1.call-update) | async-done | bytes 2097168 | tf_op jit(solution)/shard_map/all_gather | solution.py:289
  295.4 5.7 fusion.5
  301.1 3.5 fusion.9
  304.6 38.1 %all-gather.20.cloned.1.call-done = bf16[768,1024]{1,0:T(8,128)(2,1)} async-done(((bf16[96,1024]{1,0:T(8,128)(2,1)}), bf16[768,1024]{1,0:T(8,128)(2,1)}) %all-gather.20.cloned.1.call-update) | async-done | bytes 1572880 | tf_op jit(solution)/shard_map/all_gather | solution.py:276
  342.7 22.9 %all-gather.22.cloned.1.call-done = bf16[1024,1024]{1,0:T(8,128)(2,1)} async-done(((bf16[256,1024]{1,0:T(8,128)(2,1)}), bf16[1024,1024]{1,0:T(8,128)(2,1)}) %all-gather.22.cloned.1.call-update) | async-done | bytes 2097168 | tf_op jit(solution)/shard_map/all_gather | solution.py:263
  365.7 8.0 multiply_convert_fusion
  373.7 1.8 fusion.7
  375.5 3.2 add_convert_fusion
  378.8 5.0 convolution_convert_fusion
  383.9 26.2 %reduce-scatter.15.cloned.1.call-done = bf16[256,1024]{1,0:T(8,128)(2,1)} async-done(((bf16[1024,1024]{1,0:T(8,128)(2,1)}), bf16[256,1024]{1,0:T(8,128)(2,1)}) %reduce-scatter.15.cloned.1.call-update) | async-done | bytes 524304 | tf_op jit(solution)/shard_map/reduce_scatter | solution.py:303
  410.1 1.7 fusion.21
  411.8 32.2 %reduce-scatter.13.cloned.1.call-done = bf16[256,1024]{1,0:T(8,128)(2,1)} async-done(((bf16[1024,1024]{1,0:T(8,128)(2,1)}), bf16[256,1024]{1,0:T(8,128)(2,1)}) %reduce-scatter.13.cloned.1.call-update) | async-done | bytes 524304 | tf_op jit(solution)/shard_map/reduce_scatter | solution.py:304
  443.9 2.6 fusion.38
  446.9 4.0 convolution_convert_fusion.2
  451.0 1.9 convolution_convert_fusion.3
  452.9 2.0 pad_maximum_fusion
  454.9 4.7 copy.75
  459.7 9.9 %all-gather.24.cloned.1.call-done.db_ref = bf16[1024,1024]{1,0:T(8,128)(2,1)} async-done(((bf16[256,1024]{1,0:T(8,128)(2,1)}), bf16[1024,1024]{1,0:T(8,128)(2,1)}) %all-gather.24.cloned.1.call-update) | async-done | bytes 2097168 | tf_op jit(solution)/shard_map/all_gather | solution.py:307
  469.6 40.3 %attn_bwd.1 = (bf16[1024,1024]{1,0:T(8,128)(2,1)}, bf16[512,1024]{1,0:T(8,128)(2,1)}, bf16[1024,1024]{1,0:T(8,128)(2,1)}, f32[8,128]{1,0:T(8,128)}, f32[8,128]{1,0:T(8,128)}) custom-call(bf16[1024,1024]{1,0:T(8,128)(2,1)} %all-gather.24.cloned.1.call-done.db_ref, bf16[512,1024]{1,0:T(8,128)(2,1)} %all-gather.14.cloned.1.call-done.wo_ref, ...), custom_call_target="tpu_custom_call" | custom-call | tf_op jit(solution)/shard_map/attn_bwd/pallas_call | solution.py:308
  510.6 5.0 convolution_convert_fusion.1
  516.3 31.7 %reduce-scatter.25.cloned.1.call-done = bf16[128,1536]{1,0:T(8,128)(2,1)} async-done(((bf16[1024,1536]{1,0:T(8,128)(2,1)}), bf16[128,1536]{1,0:T(8,128)(2,1)}) %reduce-scatter.25.cloned.1.call-update) | async-done | bytes 393232 | tf_op jit(solution)/shard_map/reduce_scatter | solution.py:321
  548.0 5.0 all-to-all-start.6
  553.0 27.9 %reduce-scatter.17.cloned.1.call-done = bf16[256,1024]{1,0:T(8,128)(2,1)} async-done(((bf16[1024,1024]{1,0:T(8,128)(2,1)}), bf16[256,1024]{1,0:T(8,128)(2,1)}) %reduce-scatter.17.cloned.1.call-update) | async-done | bytes 524304 | tf_op jit(solution)/shard_map/reduce_scatter | solution.py:315
  580.9 1.5 fusion.23
  582.4 68.8 %reduce-scatter.19.cloned.1.call-done = bf16[128,1024]{1,0:T(8,128)(2,1)} async-done(((bf16[1024,1024]{1,0:T(8,128)(2,1)}), bf16[128,1024]{1,0:T(8,128)(2,1)}) %reduce-scatter.19.cloned.1.call-update) | async-done | bytes 262160 | tf_op jit(solution)/shard_map/reduce_scatter | solution.py:321
  651.3 6.1 all-to-all-start.5
  657.3 3.1 convolution_convert_fusion.4
  660.4 1.0 all-to-all-done.5
  661.5 3.6 all-to-all-start.4
  665.0 64.9 %reduce-scatter.23.cloned.1.call-done = bf16[96,1024]{1,0:T(8,128)(2,1)} async-done(((bf16[768,1024]{1,0:T(8,128)(2,1)}), bf16[96,1024]{1,0:T(8,128)(2,1)}) %reduce-scatter.23.cloned.1.call-update) | async-done | bytes 196624 | tf_op jit(solution)/shard_map/reduce_scatter | solution.py:321
  729.9 5.5 collective-permute-start.3
  735.5 5.3 collective-permute-done.3
  740.7 0.8 convert_element_type.116
  741.7 0.8 copy.84
  742.5 0.8 copy.83
  743.3 52.2 %reduce-scatter.21.cloned.1.call-done = bf16[64,1024]{1,0:T(8,128)(2,1)} async-done(((bf16[512,1024]{1,0:T(8,128)(2,1)}), bf16[64,1024]{1,0:T(8,128)(2,1)}) %reduce-scatter.21.cloned.1.call-update) | async-done | bytes 131088 | tf_op jit(solution)/shard_map/reduce_scatter | solution.py:321
  795.5 6.0 collective-permute-start.2
  803.1 2.4 collective-permute-done.2
  805.6 0.7 convert_element_type.113
  806.4 41.9 %all-reduce.1 = f32[32,72]{1,0:T(8,128)S(1)} all-reduce(f32[32,72]{1,0:T(8,128)S(1)} %pad_maximum_fusion.3), channel_id=7, replica_groups=mesh['dp'=8,'ctx'=4] {'dp','ctx'}, use_global_device_ids=true, to_apply=%region_12.13.clone | all-reduce | flops 2304 | bytes 18432
  851.7 1.3 convolution_convert_fusion.6
  (128 shorter events, 16.4 us)
Async XLA Ops:
  7.2 31.3 %copy-start = (bf16[256,1024]{1,0:T(8,128)(2,1)S(1)}, bf16[256,1024]{1,0:T(8,128)(2,1)}, u32[]{:S(2)}) copy-start(bf16[256,1024]{1,0:T(8,128)(2,1)} %param.17) | copy-start | bytes 1572868
  7.2 116.1 %all-gather.14.cloned.1.call-start = ((), (), s32[]{:S(2)}) async-start(), calls=%async_computation.17 | async-start | bytes 1179648 | tf_op jit(solution)/shard_map/all_gather | solution.py:276
  7.2 10.6 %collective-permute-start = (bf16[64,1024]{1,0:T(8,128)(2,1)}, bf16[64,1024]{1,0:T(8,128)(2,1)S(1)}, u32[]{:S(2)}, u32[]{:S(2)}) collective-permute-start(bf16[64,1024]{1,0:T(8,128)(2,1)} %param.27), channel_id=1, source_target_pairs={{0,0},{1,4},{2,8},{3,12},{4,16},{5,20},{6,24},{7,28},{8,1},{9,5},{... | collective-permute-start | bytes 393224 | tf_op jit(solution)/shard_map/ppermute | solution.py:275
  17.9 0.7 copy-start.9
  18.6 107.3 %all-gather.12.cloned.1.call-start = ((), (), s32[]{:S(2)}) async-start(), calls=%async_computation.16 | async-start | bytes 2359296 | tf_op jit(solution)/shard_map/all_gather | solution.py:276
  32.6 11.1 %all-to-all-start = ((s32[8,1,64]{2,1,0:T(1,128)}), s32[8,1,64]{2,1,0:T(1,128)S(1)}, u32[]{:S(2)}, u32[]{:S(2)}) async-start(s32[8,1,64]{2,1,0:T(1,128)} %add.94), calls=%async_computation | async-start | bytes 8192 | tf_op jit(solution)/shard_map/all_to_all | solution.py:259
  43.7 39.0 %copy-start.10 = (bf16[4]{0:T(256)(128)(2,1)S(1)}, bf16[4]{0:T(256)(128)(2,1)}, u32[]{:S(2)}) copy-start(bf16[4]{0:T(256)(128)(2,1)} %param.26) | copy-start | bytes 28
  43.7 39.0 %copy-start.11 = (bf16[4]{0:T(256)(128)(2,1)S(1)}, bf16[4]{0:T(256)(128)(2,1)}, u32[]{:S(2)}) copy-start(bf16[4]{0:T(256)(128)(2,1)} %param.25) | copy-start | bytes 28
  43.7 39.0 %copy-start.12 = (bf16[32]{0:T(256)(128)(2,1)S(1)}, bf16[32]{0:T(256)(128)(2,1)}, u32[]{:S(2)}) copy-start(bf16[32]{0:T(256)(128)(2,1)} %param.28) | copy-start | bytes 196
  43.7 39.0 %copy-start.13 = (bf16[32]{0:T(256)(128)(2,1)S(1)}, bf16[32]{0:T(256)(128)(2,1)}, u32[]{:S(2)}) copy-start(bf16[32]{0:T(256)(128)(2,1)} %param.21) | copy-start | bytes 196
  43.7 79.6 %copy-start.19 = (s32[1,2]{1,0:T(1,128)S(1)}, s32[1,2]{1,0:T(1,128)}, u32[]{:S(2)}) copy-start(s32[1,2]{1,0:T(1,128)} %param.19) | copy-start | bytes 28
  43.7 37.6 %all-to-all-start.1 = ((bf16[8,64,1024]{2,1,0:T(8,128)(2,1)}), bf16[8,64,1024]{2,1,0:T(8,128)(2,1)S(1)}, u32[]{:S(2)}, u32[]{:S(2)}) async-start(bf16[8,64,1024]{2,1,0:T(8,128)(2,1)} %bitcast), calls=%async_computation.1 | async-start | bytes 2097152 | tf_op jit(solution)/shard_map/all_to_all | solution.py:258
  47.4 102.1 %all-gather.10.cloned.1.call-start = ((), (), s32[]{:S(2)}) async-start(), calls=%async_computation.15 | async-start | bytes 2621440 | tf_op jit(solution)/shard_map/all_gather | solution.py:262
  82.6 117.9 %reduce-scatter.11.cloned.1.call-start = ((), (), s32[]{:S(2)}) async-start(), calls=%async_computation.18 | async-start | bytes 2621440 | tf_op jit(solution)/shard_map/reduce_scatter | solution.py:287
  169.0 0.9 copy-start.6
  169.0 1.1 copy-start.7
  169.0 31.4 %copy-start.2 = (bf16[256,1024]{1,0:T(8,128)(2,1)S(1)}, bf16[256,1024]{1,0:T(8,128)(2,1)}, u32[]{:S(2)}) copy-start(bf16[256,1024]{1,0:T(8,128)(2,1)} %convolution_convert_fusion.7) | copy-start | bytes 1572868
  169.1 102.9 %all-gather.18.cloned.1.call-start = ((), (), s32[]{:S(2)}) async-start(), calls=%async_computation.20 | async-start | bytes 3538944 | tf_op jit(solution)/shard_map/all_gather | solution.py:276
  170.5 33.4 %copy-start.18 = (bf16[96,1024]{1,0:T(8,128)(2,1)S(1)}, bf16[96,1024]{1,0:T(8,128)(2,1)}, u32[]{:S(2)}) copy-start(bf16[96,1024]{1,0:T(8,128)(2,1)} %param.31) | copy-start | bytes 589828
  180.9 114.5 %all-gather.16.cloned.1.call-start = ((), (), s32[]{:S(2)}) async-start(), calls=%async_computation.19 | async-start | bytes 2621440 | tf_op jit(solution)/shard_map/all_gather | solution.py:289
  203.8 138.9 %all-gather.20.cloned.1.call-start = ((), (), s32[]{:S(2)}) async-start(), calls=%async_computation.21 | async-start | bytes 1769472 | tf_op jit(solution)/shard_map/all_gather | solution.py:276
  203.9 11.9 %collective-permute-start.1 = (bf16[96,1024]{1,0:T(8,128)(2,1)S(1)}, bf16[96,1024]{1,0:T(8,128)(2,1)S(1)}, u32[]{:S(2)}, u32[]{:S(2)}) collective-permute-start(bf16[96,1024]{1,0:T(8,128)(2,1)S(1)} %copy-done.18), channel_id=1, source_target_pairs={{0,0},{1,4},{2,8},{3,12},{4,16},{5,20},{6,24},{7,28},{8,1},{9,5},{... | collective-permute-start | bytes 589832 | tf_op jit(solution)/shard_map/ppermute | solution.py:275
  215.8 0.7 copy-start.8
  216.5 149.1 %all-gather.22.cloned.1.call-start = ((), (), s32[]{:S(2)}) async-start(), calls=%async_computation.23 | async-start | bytes 2621440 | tf_op jit(solution)/shard_map/all_gather | solution.py:263
  217.3 192.8 %reduce-scatter.15.cloned.1.call-start = ((), (), s32[]{:S(2)}) async-start(), calls=%async_computation.24 | async-start | bytes 2621440 | tf_op jit(solution)/shard_map/reduce_scatter | solution.py:303
  295.4 5.7 copy-start.14
  295.4 5.7 copy-start.16
  365.7 8.0 copy-start.15
  373.7 1.8 copy-start.21
  373.7 1.8 copy-start.20
  378.7 65.2 %reduce-scatter.13.cloned.1.call-start = ((), (), s32[]{:S(2)}) async-start(), calls=%async_computation.22 | async-start | bytes 2621440 | tf_op jit(solution)/shard_map/reduce_scatter | solution.py:304
  383.8 26.3 %copy-start.3 = (bf16[256,1024]{1,0:T(8,128)(2,1)S(1)}, bf16[256,1024]{1,0:T(8,128)(2,1)}, u32[]{:S(2)}) copy-start(bf16[256,1024]{1,0:T(8,128)(2,1)} %reduce-scatter.11.cloned.1.call-done) | copy-start | bytes 1572868
  383.8 60.2 %copy-start.4 = (bf16[256,1024]{1,0:T(8,128)(2,1)S(1)}, bf16[256,1024]{1,0:T(8,128)(2,1)}, u32[]{:S(2)}) copy-start(bf16[256,1024]{1,0:T(8,128)(2,1)} %param.20) | copy-start | bytes 1572868
  383.8 85.8 %all-gather.24.cloned.1.call-start = ((), (), s32[]{:S(2)}) async-start(), calls=%async_computation.25 | async-start | bytes 2621440 | tf_op jit(solution)/shard_map/all_gather | solution.py:307
  446.6 101.4 %reduce-scatter.25.cloned.1.call-start = ((), (), s32[]{:S(2)}) async-start(), calls=%async_computation.30 | async-start | bytes 3538944 | tf_op jit(solution)/shard_map/reduce_scatter | solution.py:321
  446.9 4.1 copy-start.17
  446.9 4.1 copy-start.22
  459.6 121.3 %reduce-scatter.17.cloned.1.call-start = ((), (), s32[]{:S(2)}) async-start(), calls=%async_computation.26 | async-start | bytes 2621440 | tf_op jit(solution)/shard_map/reduce_scatter | solution.py:315
  510.0 141.3 %reduce-scatter.19.cloned.1.call-start = ((), (), s32[]{:S(2)}) async-start(), calls=%async_computation.27 | async-start | bytes 2359296 | tf_op jit(solution)/shard_map/reduce_scatter | solution.py:321
  510.5 219.4 %reduce-scatter.23.cloned.1.call-start = ((), (), s32[]{:S(2)}) async-start(), calls=%async_computation.29 | async-start | bytes 1769472 | tf_op jit(solution)/shard_map/reduce_scatter | solution.py:321
  515.7 141.7 %copy-start.5 = (bf16[256,1024]{1,0:T(8,128)(2,1)S(1)}, bf16[256,1024]{1,0:T(8,128)(2,1)}, u32[]{:S(2)}) copy-start(bf16[256,1024]{1,0:T(8,128)(2,1)} %reduce-scatter.15.cloned.1.call-done) | copy-start | bytes 1572868
  515.7 279.8 %reduce-scatter.21.cloned.1.call-start = ((), (), s32[]{:S(2)}) async-start(), calls=%async_computation.28 | async-start | bytes 1179648 | tf_op jit(solution)/shard_map/reduce_scatter | solution.py:321
  548.0 34.5 %all-to-all-start.6 = ((bf16[4,32,1536]{2,1,0:T(8,128)(2,1)}), bf16[4,32,1536]{2,1,0:T(8,128)(2,1)S(1)}, u32[]{:S(2)}, u32[]{:S(2)}) async-start(bf16[4,32,1536]{2,1,0:T(8,128)(2,1)} %bitcast.83), calls=%async_computation.12 | async-start | bytes 786432 | tf_op jit(solution)/shard_map/all_to_all | solution.py:324
  651.3 10.2 %all-to-all-start.5 = ((bf16[4,32,1024]{2,1,0:T(8,128)(2,1)}), bf16[4,32,1024]{2,1,0:T(8,128)(2,1)S(1)}, u32[]{:S(2)}, u32[]{:S(2)}) async-start(bf16[4,32,1024]{2,1,0:T(8,128)(2,1)} %bitcast.86), calls=%async_computation.10 | async-start | bytes 524288 | tf_op jit(solution)/shard_map/all_to_all | solution.py:323
  661.5 190.2 %all-to-all-start.4 = ((bf16[8,64,1024]{2,1,0:T(8,128)(2,1)}), bf16[8,64,1024]{2,1,0:T(8,128)(2,1)S(1)}, u32[]{:S(2)}, u32[]{:S(2)}) async-start(bf16[8,64,1024]{2,1,0:T(8,128)(2,1)} %bitcast.78), calls=%async_computation.8 | async-start | bytes 2097152 | tf_op jit(solution)/shard_map/all_to_all | solution.py:319
  729.9 10.8 %collective-permute-start.3 = (bf16[96,1024]{1,0:T(8,128)(2,1)}, bf16[96,1024]{1,0:T(8,128)(2,1)S(1)}, u32[]{:S(2)}, u32[]{:S(2)}) collective-permute-start(bf16[96,1024]{1,0:T(8,128)(2,1)} %reduce-scatter.23.cloned.1.call-done), channel_id=1, source_target_pairs={{0,0},{4,1},{8,2},{12,3},{16,4},{20,5},{24,6},{28,7},{1,8},{5,9},{... | collective-permute-start | bytes 589832 | tf_op jit(solution)/shard_map/ppermute | solution.py:322
  795.5 10.1 %collective-permute-start.2 = (bf16[64,1024]{1,0:T(8,128)(2,1)}, bf16[64,1024]{1,0:T(8,128)(2,1)S(1)}, u32[]{:S(2)}, u32[]{:S(2)}) collective-permute-start(bf16[64,1024]{1,0:T(8,128)(2,1)} %reduce-scatter.21.cloned.1.call-done), channel_id=1, source_target_pairs={{0,0},{4,1},{8,2},{12,3},{16,4},{20,5},{24,6},{28,7},{1,8},{5,9},{... | collective-permute-start | bytes 393224 | tf_op jit(solution)/shard_map/ppermute | solution.py:322
  849.0 4.0 copy-start.1
Sparse Core Ops, SparseCore 0:
  18.7 59.5 all-gather.13
  80.4 45.4 all-gather.11
  128.0 21.4 all-gather.9
  169.2 31.2 reduce-scatter.10
  202.7 69.2 all-gather.17
  274.1 21.2 all-gather.15
  298.4 44.3 all-gather.19
  344.4 21.2 all-gather.21
  378.9 31.1 reduce-scatter.14
  412.5 31.4 reduce-scatter.12
  446.7 22.8 all-gather.23
  473.5 74.4 reduce-scatter.24
  550.7 30.1 reduce-scatter.16
  584.3 66.9 reduce-scatter.18
  654.5 75.3 reduce-scatter.22
  733.6 61.8 reduce-scatter.20

commit v2 on v1

--- a/solution.py
+++ b/solution.py
@@ -203,6 +203,577 @@
         gwqkv_ref[cols, :] = dot_tn(xn_ref[:, cols], dp_ref[...]).astype(BF)
 
 
+MESH = pl.DeviceIdType.MESH
+
+
+def rcopy(src, dst, send, recv, **device):
+    return pltpu.make_async_remote_copy(
+        src_ref=src, dst_ref=dst, send_sem=send, recv_sem=recv, device_id=device, device_id_type=MESH
+    )
+
+
+class Place:
+    def __init__(self, n):
+        self.n, self.line = n, n // 2
+        self.dp, self.ctx = lax.axis_index("dp"), lax.axis_index("ctx")
+        self.outer, self.inner = self.dp // 2, self.dp % 2
+        self.dp_inner = self.outer * 2 + 1 - self.inner
+        self.dp_up, self.dp_down = self.dp + 2, self.dp - 2
+        self.has_up, self.has_down = self.outer < self.line - 1, self.outer > 0
+        core = self.ctx % 2
+        self.c_core = self.ctx + 1 - 2 * core
+        self.c_x = (self.ctx + 2) % 4
+        self.c_far = 3 - self.ctx
+        mine = self.dp * 4 + self.ctx
+        self.slab_to = {"dp": mine % n, "ctx": mine // n}
+        source = self.ctx * n + self.dp
+        self.slab_from = {"dp": source // 4, "ctx": source % 4}
+        self.slab_stays = source == mine
+
+
+def greet(place, line, all_dp, slabs):
+    barrier = pltpu.get_barrier_semaphore()
+
+    def signal(**device):
+        pl.semaphore_signal(barrier, inc=1, device_id=device, device_id_type=MESH)
+
+    for c in (place.c_core, place.c_x, place.c_far):
+        signal(ctx=c)
+    count = 3
+    if all_dp:
+        for k in range(1, place.n):
+            signal(dp=(place.dp + k) % place.n)
+        count = count + place.n - 1
+    elif line:
+        signal(dp=place.dp_inner)
+        count = count + 1
+        for there, dp in ((place.has_up, place.dp_up), (place.has_down, place.dp_down)):
+
+            @pl.when(there)
+            def _():
+                signal(dp=dp)
+
+            count = count + jnp.where(there, 1, 0)
+    if slabs is not None:
+
+        @pl.when(jnp.logical_not(place.slab_stays))
+        def _():
+            signal(**slabs)
+
+        count = count + jnp.where(place.slab_stays, 0, 1)
+    pl.semaphore_wait(barrier, count)
+
+
+class Gather:
+    def __init__(self, place, bufs, sems):
+        self.at, self.bufs, self.sems = place, bufs, sems
+
+    @staticmethod
+    def scratch(n, bufs):
+        return pltpu.SemaphoreType.DMA((5, bufs, n // 2))
+
+    def copy(self, b, p, way):
+        at = self.at
+        block = self.bufs[b].at[p * 2 + at.inner]
+        device = (at.dp_up, at.dp_down, at.dp_inner)[way]
+        recv = self.sems.at[4 if way == 2 else 3, b, p]
+        return rcopy(block, block, self.sems.at[way, b, p], recv, dp=device)
+
+    def send(self, p, up, down):
+        at = self.at
+        for b in range(len(self.bufs)):
+            if up:
+
+                @pl.when(at.has_up)
+                def _():
+                    self.copy(b, p, 0).start()
+
+            if down:
+
+                @pl.when(at.has_down)
+                def _():
+                    self.copy(b, p, 1).start()
+
+            self.copy(b, p, 2).start()
+
+    def start(self):
+        self.send(self.at.outer, True, True)
+
+    def step(self, t):
+        at = self.at
+        for p, there, up in ((at.outer - t, at.outer >= t, True), (at.outer + t, at.outer + t < at.line, False)):
+
+            @pl.when(there)
+            def _():
+                for b in range(len(self.bufs)):
+                    self.copy(b, p, 0).wait_recv()
+                self.send(p, up, not up)
+
+    def finish(self):
+        at = self.at
+        for b in range(len(self.bufs)):
+            for p in range(at.line):
+                block = self.bufs[b].at[p * 2 + 1 - at.inner]
+                rcopy(block, block, self.sems.at[2, b, p], self.sems.at[4, b, p], dp=at.dp_inner).wait_recv()
+                self.copy(b, p, 2).wait_send()
+
+                @pl.when(jnp.logical_and(at.has_up, p <= at.outer))
+                def _():
+                    self.copy(b, p, 0).wait_send()
+
+                @pl.when(jnp.logical_and(at.has_down, p >= at.outer))
+                def _():
+                    self.copy(b, p, 1).wait_send()
+
+
+class Reduce:
+    def __init__(self, place, parts, from_inner, from_line, sems):
+        self.at, self.parts, self.from_inner, self.from_line, self.sems = place, parts, from_inner, from_line, sems
+
+    @staticmethod
+    def scratch(n, blocks):
+        line = n // 2
+        return (
+            [pltpu.VMEM((line, *dims), dtype) for dims, dtype in blocks],
+            [pltpu.VMEM((line + 1, *dims), dtype) for dims, dtype in blocks],
+            pltpu.SemaphoreType.DMA((4, len(blocks), line + 1)),
+        )
+
+    def inner_copy(self, b, p):
+        at = self.at
+        return rcopy(
+            self.parts[b].at[p * 2 + 1 - at.inner], self.from_inner[b].at[p],
+            self.sems.at[0, b, p], self.sems.at[1, b, p], dp=at.dp_inner,
+        )
+
+    def line_copy(self, b, p, slot, up):
+        at = self.at
+        return rcopy(
+            self.parts[b].at[p * 2 + at.inner], self.from_line[b].at[slot],
+            self.sems.at[2, b, p], self.sems.at[3, b, slot], dp=at.dp_up if up else at.dp_down,
+        )
+
+    def start(self, which):
+        at = self.at
+        for d in range(at.line - 1, -1, -1):
+            for p, there in ((at.outer + d, at.outer + d < at.line), (at.outer - d, at.outer >= d))[: 2 if d else 1]:
+
+                @pl.when(there)
+                def _():
+                    for b in which:
+                        self.inner_copy(b, p).start()
+
+    def total(self, b, p, slots):
+        s = self.parts[b][p * 2 + self.at.inner].astype(F32) + self.from_inner[b][p].astype(F32)
+        for slot in slots:
+            s = s + self.from_line[b][slot].astype(F32)
+        return s
+
+    def step(self, d, which):
+        at = self.at
+        for p, there, more, up in (
+            (at.outer + d, at.outer + d < at.line, at.has_down, True),
+            (at.outer - d, at.outer >= d, at.has_up, False),
+        ):
+            for b in which:
+
+                @pl.when(there)
+                def _():
+                    self.inner_copy(b, p).wait_recv()
+                    into = self.parts[b].at[p * 2 + at.inner]
+
+                    @pl.when(more)
+                    def _():
+                        self.line_copy(b, p, p, up).wait_recv()
+                        into[...] = self.total(b, p, [p]).astype(into.dtype)
+
+                    @pl.when(jnp.logical_not(more))
+                    def _():
+                        into[...] = self.total(b, p, []).astype(into.dtype)
+
+                    slot = p if up or d > 1 else at.line
+                    self.line_copy(b, p, slot, up).start()
+
+    def result(self, b, store):
+        at = self.at
+        p = at.outer
+        self.inner_copy(b, p).wait_recv()
+        lo, hi = at.has_down, at.has_up
+
+        @pl.when(lo)
+        def _():
+            self.line_copy(b, p, p, True).wait_recv()
+
+        @pl.when(hi)
+        def _():
+            self.line_copy(b, p, at.line, False).wait_recv()
+
+        @pl.when(jnp.logical_and(lo, hi))
+        def _():
+            store(self.total(b, p, [p, at.line]))
+
+        @pl.when(jnp.logical_and(lo, jnp.logical_not(hi)))
+        def _():
+            store(self.total(b, p, [p]))
+
+        @pl.when(jnp.logical_and(hi, jnp.logical_not(lo)))
+        def _():
+            store(self.total(b, p, [at.line]))
+
+    def finish(self):
+        at = self.at
+        for b in range(len(self.parts)):
+            for p in range(at.line):
+                self.inner_copy(b, p).wait_send()
+
+                @pl.when(p != at.outer)
+                def _():
+                    self.line_copy(b, p, p, True).wait_send()
+
+
+class CtxGather:
+    def __init__(self, place, buf, sems):
+        self.at, self.buf, self.sems = place, buf, sems
+
+    def copy(self, k, owner):
+        block = self.buf.at[owner]
+        ctx = self.at.c_x if k == 1 else self.at.c_core
+        return rcopy(block, block, self.sems.at[0, k], self.sems.at[1, k], ctx=ctx)
+
+    def start(self):
+        self.copy(1, self.at.ctx).start()
+        self.copy(0, self.at.ctx).start()
+
+    def forward(self):
+        self.copy(1, self.at.c_x).wait_recv()
+        self.copy(2, self.at.c_x).start()
+
+    def finish(self):
+        self.copy(0, self.at.c_core).wait_recv()
+        self.copy(2, self.at.c_far).wait_recv()
+        for k in range(3):
+            self.copy(k, self.at.ctx).wait_send()
+
+
+class CtxReduce:
+    def __init__(self, place, part, got, sems):
+        self.at, self.part, self.got, self.sems = place, part, got, sems
+
+    def copy(self, k):
+        at = self.at
+        block = self.part.at[(at.c_core, at.c_far, at.c_x)[k]]
+        return rcopy(block, self.got.at[k], self.sems.at[0, k], self.sems.at[1, k], ctx=at.c_x if k == 2 else at.c_core)
+
+    def start(self):
+        self.copy(1).start()
+        self.copy(0).start()
+
+    def across(self):
+        self.copy(1).wait_recv()
+        into = self.part.at[self.at.c_x]
+        into[...] = (into[...].astype(F32) + self.got[1].astype(F32)).astype(into.dtype)
+        self.copy(2).start()
+
+    def result(self):
+        self.copy(0).wait_recv()
+        self.copy(2).wait_recv()
+        return self.part[self.at.ctx].astype(F32) + self.got[0].astype(F32) + self.got[2].astype(F32)
+
+    def finish(self):
+        for k in range(3):
+            self.copy(k).wait_send()
+
+
+class Quarters:
+    def __init__(self, place, src, dst, sems):
+        self.at, self.src, self.dst, self.sems = place, src, dst, sems
+
+    def copies(self):
+        at = self.at
+        return [
+            rcopy(self.src.at[c], self.dst.at[at.ctx], self.sems.at[0, k], self.sems.at[1, k], ctx=c)
+            for k, c in enumerate((at.c_x, at.c_far, at.c_core))
+        ]
+
+    def start(self):
+        for c in self.copies():
+            c.start()
+        self.dst[self.at.ctx] = self.src[self.at.ctx]
+
+    def finish(self):
+        for c in self.copies():
+            c.wait()
+
+
+class Slab:
+    def __init__(self, place, src, dst, sems, to):
+        self.at, self.src, self.dst, self.sems, self.to = place, src, dst, sems, to
+
+    def copy(self):
+        return rcopy(self.src, self.dst, self.sems.at[0, 0], self.sems.at[1, 0], **self.to)
+
+    def start(self):
+        @pl.when(self.at.slab_stays)
+        def _():
+            self.dst[...] = self.src[...]
+
+        @pl.when(jnp.logical_not(self.at.slab_stays))
+        def _():
+            self.copy().start()
+
+    def finish(self):
+        @pl.when(jnp.logical_not(self.at.slab_stays))
+        def _():
+            self.copy().wait()
+
+
+class Exchange:
+    def __init__(self, place, src, dst, cap, sems):
+        self.at, self.src, self.dst, self.cap, self.sems = place, src, dst, cap, sems
+
+    def rows(self, ref, j):
+        return ref.at[pl.ds(pl.multiple_of(j * self.cap, self.cap), self.cap)]
+
+    def copy(self, k):
+        at = self.at
+        to = (at.dp + k) % at.n
+        return rcopy(self.rows(self.src, to), self.rows(self.dst, at.dp), self.sems.at[0, k], self.sems.at[1, k], dp=to)
+
+    def start(self):
+        for k in range(1, self.at.n):
+            self.copy(k).start()
+        self.rows(self.dst, self.at.dp)[...] = self.rows(self.src, self.at.dp)[...]
+
+    def finish(self):
+        for k in range(1, self.at.n):
+            self.copy(k).wait()
+
+
+def sem_pairs(count):
+    return pltpu.SemaphoreType.DMA((2, count))
+
+
+def fetch_body(
+    n, cap,
+    out_ref, lab_ref, qkv_ref, wo_src, gu_ref, wd_src, gain_ref, og_ref,
+    wqkv_ref, wo_ref, gu_out, wd_out, x_ref, og_all, pick_ref, ga_ref, gm_ref, gqk_ref,
+    recv, labels, gains_c, gains_n,
+    s_gather, s_rows, s_labs, s_qkv, s_gu, s_wo, s_wd, s_gain, s_x, s_og,
+):
+    at = Place(n)
+    greet(at, line=True, all_dp=True, slabs=at.slab_from)
+    qkv = Quarters(at, qkv_ref, wqkv_ref.at[at.dp], s_qkv)
+    wo = Slab(at, wo_src, wo_ref.at[at.slab_to["dp"]], s_wo, at.slab_to)
+    rows = Exchange(at, out_ref, recv, cap, s_rows)
+    labs = Exchange(at, lab_ref, labels, 8, s_labs)
+    wo.start()
+    qkv.start()
+    labs.start()
+    rows.start()
+    gains = [
+        rcopy(gain_ref, gains_c.at[at.ctx], s_gain.at[0, k], s_gain.at[1, k], ctx=c)
+        for k, c in enumerate((at.c_x, at.c_far, at.c_core))
+    ]
+    for g in gains:
+        g.start()
+    gains_c[at.ctx] = gain_ref[...]
+    wd = Slab(at, wd_src, wd_out, s_wd, at.slab_to)
+    gu = Quarters(at, gu_ref, gu_out, s_gu)
+    wd.start()
+    gu.start()
+    og_all[at.ctx] = og_ref[...]
+    og = CtxGather(at, og_all, s_og)
+    og.start()
+    for g in gains:
+        g.wait()
+    gains_n[at.dp] = gains_c[0] + gains_c[1] + gains_c[2] + gains_c[3]
+    qkv.finish()
+    wo.finish()
+    gather = Gather(at, [wqkv_ref, wo_ref, gains_n], s_gather)
+    gather.start()
+    gather.step(1)
+    labs.finish()
+    tok = x_ref.shape[1]
+    slots = lax.broadcasted_iota(jnp.int32, (tok, cap), 0)
+    for j in range(n):
+        pick_ref[:, j * cap : (j + 1) * cap] = (slots == labels[j * 8 : j * 8 + 1, :cap]).astype(BF)
+    rows.finish()
+    x_ref[at.ctx] = dot(pick_ref[...], recv[...]).astype(BF)
+    x = CtxGather(at, x_ref, s_x)
+    x.start()
+    og.forward()
+    for t in range(2, at.line):
+        gather.step(t)
+    x.forward()
+    gather.finish()
+    own = 4 * ga_ref.shape[1] // (4 * n)
+    ga_ref[...] = jnp.zeros_like(ga_ref)
+    gm_ref[...] = jnp.zeros_like(gm_ref)
+    gqk = jnp.zeros((8, 128), F32)
+    for d in range(n):
+        tile = slice(d * own // 128 * 128, d * own // 128 * 128 + 128)
+        block = gains_n[d]
+        ga_ref[0:1, tile] += block[0:1]
+        gm_ref[0:1, tile] += block[1:2]
+        gqk = gqk + block
+    gqk_ref[...] = gqk
+    for part in (og, x, wd, gu):
+        part.finish()
+
+
+def middle_body(
+    n,
+    part_in, x_ref, gm_ref, gu_ref, wd_src,
+    wgu_ref, wd_ref, nm_ref, mid_ref,
+    part_ref, got, s_gather, s_red, s_nm,
+):
+    at = Place(n)
+    wgu_ref[at.dp] = gu_ref[...]
+    wd_ref[at.dp] = wd_src[...]
+    part_ref[...] = part_in[...]
+    greet(at, line=True, all_dp=False, slabs=None)
+    gather = Gather(at, [wgu_ref, wd_ref], s_gather)
+    red = CtxReduce(at, part_ref, got, s_red)
+    red.start()
+    gather.start()
+    red.across()
+    gather.step(1)
+    middle = x_ref[...].astype(F32) + red.result()
+    mid_ref[...] = middle
+    r = lax.rsqrt(jnp.mean(middle * middle, axis=-1, keepdims=True) + EPS)
+    nm_ref[at.ctx] = (middle * r * gm_ref[0:1, :]).astype(BF)
+    nm = CtxGather(at, nm_ref, s_nm)
+    nm.start()
+    for t in range(2, at.line):
+        gather.step(t)
+        if t == 2:
+            nm.forward()
+    gather.finish()
+    nm.finish()
+    red.finish()
+
+
+def norm_back(c, v, gain):
+    r = lax.rsqrt(jnp.mean(v * v, axis=-1, keepdims=True) + EPS)
+    nv = v * r
+    cg = c * gain
+    return jnp.sum(c * nv, axis=0, keepdims=True), r * (cg - nv * jnp.mean(cg * nv, axis=-1, keepdims=True))
+
+
+def back_body(
+    n,
+    dnm_in, outp_in, mid_ref, gm_ref, og_ref, gwgu_in, gwd_in,
+    db_ref, dmid_ref, out_ref, ggm_ref, gu_ref, gd_ref,
+    dnm_part, out_part, gwgu, gwd, got_d, got_o, yi0, yi1, ln0, ln1,
+    s_red, s_dnm, s_out, s_db,
+):
+    at = Place(n)
+    dnm_part[...] = dnm_in[...]
+    out_part[...] = outp_in[...]
+    gwgu[...] = gwgu_in[...]
+    gwd[...] = gwd_in[...]
+    greet(at, line=True, all_dp=False, slabs=None)
+    dnm = CtxReduce(at, dnm_part, got_d, s_dnm)
+    dnm.start()
+    grads = Reduce(at, [gwgu, gwd], [yi0, yi1], [ln0, ln1], s_red)
+    grads.start([0, 1])
+    dnm.across()
+    out = CtxReduce(at, out_part, got_o, s_out)
+    out.start()
+    grads.step(at.line - 1, [0, 1])
+    gg, d = norm_back(dnm.result(), mid_ref[...], gm_ref[0:1, :])
+    ggm_ref[...] = jnp.broadcast_to(gg, ggm_ref.shape)
+    d = d + og_ref[...].astype(F32)
+    dmid_ref[...] = d
+    db_ref[at.ctx] = d.astype(BF)
+    db = CtxGather(at, db_ref, s_db)
+    db.start()
+    out.across()
+    for t in range(at.line - 2, 0, -1):
+        grads.step(t, [0, 1])
+        if t == 1:
+            db.forward()
+    out_ref[...] = (mid_ref[...] + out.result()).astype(BF)
+
+    def to_gu(v):
+        gu_ref[...] = v.astype(BF)
+
+    def to_gd(v):
+        gd_ref[...] = v.astype(BF)
+
+    grads.result(0, to_gu)
+    grads.result(1, to_gd)
+    for part in (grads, db, out, dnm):
+        part.finish()
+
+
+def finish_body(
+    n, cap,
+    dxn_in, dmid_ref, x_ref, ga_ref, pick_ref, place_ref, gwqkv_in, gwo_in, gu_in, gd_in, ggm_ref, ggq_ref, ggk_ref,
+    ig_ref, qkv_out, o_out, gu_out, gd_out, gain_out,
+    dxn_part, gwqkv, gwo, gains, got, sendb, recv, yi0, yi1, yi2, ln0, ln1, ln2, qkv_sum, o_sum, gain_sum, gain_all,
+    s_red, s_dxn, s_rows, s_gu, s_gd, s_qkv, s_o, s_gain,
+):
+    at = Place(n)
+    dxn_part[...] = dxn_in[...]
+    gwqkv[...] = gwqkv_in[...]
+    gwo[...] = gwo_in[...]
+    greet(at, line=True, all_dp=True, slabs=at.slab_to)
+    dxn = CtxReduce(at, dxn_part, got, s_dxn)
+    dxn.start()
+    grads = Reduce(at, [gwqkv, gwo, gains], [yi0, yi1, yi2], [ln0, ln1, ln2], s_red)
+    grads.start([0, 1])
+    dxn.across()
+    gu = Quarters(at, gu_in, gu_out, s_gu)
+    gd = Slab(at, gd_in, gd_out, s_gd, at.slab_from)
+    gu.start()
+    gd.start()
+    gg, d = norm_back(dxn.result(), x_ref[...].astype(F32), ga_ref[0:1, :])
+    owned = (dmid_ref[...] + d).astype(BF)
+    sendb[...] = dot_tn(pick_ref[...], owned).astype(BF)
+    rows = Exchange(at, sendb, recv, cap, s_rows)
+    rows.start()
+    own = 4 * gg.shape[1] // (4 * n)
+    lines = lax.broadcasted_iota(jnp.int32, (8, 128), 0)
+    for j in range(n):
+        tile = slice(j * own // 128 * 128, j * own // 128 * 128 + 128)
+        gains[j] = (
+            jnp.where(lines == 0, gg[:, tile], 0.0) + jnp.where(lines == 1, ggm_ref[0:1, tile], 0.0)
+            + jnp.where(lines == 2, ggq_ref[0:1, :], 0.0) + jnp.where(lines == 3, ggk_ref[0:1, :], 0.0)
+        )
+    grads.start([2])
+    for t in range(at.line - 1, 0, -1):
+        grads.step(t, [0, 1, 2])
+
+    def to(ref):
+        def store(v):
+            ref[...] = v.astype(ref.dtype)
+
+        return store
+
+    grads.result(0, to(qkv_sum))
+    qkv = Quarters(at, qkv_sum, qkv_out, s_qkv)
+    qkv.start()
+    grads.result(1, to(o_sum))
+    o = Slab(at, o_sum, o_out, s_o, at.slab_from)
+    o.start()
+    grads.result(2, to(gain_sum))
+    small = [
+        rcopy(gain_sum, gain_all.at[at.ctx], s_gain.at[0, k], s_gain.at[1, k], ctx=c)
+        for k, c in enumerate((at.c_x, at.c_far, at.c_core))
+    ]
+    for g in small:
+        g.start()
+    gain_all[at.ctx] = gain_sum[...]
+    rows.finish()
+    ig_ref[...] = dot(place_ref[...], recv[...]).astype(BF)
+    for g in small:
+        g.wait()
+    gain_out[...] = gain_all[0] + gain_all[1] + gain_all[2] + gain_all[3]
+    for part in (qkv, o, gu, gd, dxn, grads):
+        part.finish()
+
+
 def shape(*dims, dtype=BF):
     return jax.ShapeDtypeStruct(dims, dtype)
 
@@ -217,8 +788,14 @@
     )
 
 
-def slab_moves(n_data):
-    return [(s, (s % n_data) * 4 + s // n_data) for s in range(4 * n_data)]
+def linked(body, outs, scratch, name, number):
+    return pl.pallas_call(
+        body,
+        out_shape=outs,
+        scratch_shapes=scratch,
+        compiler_params=pltpu.CompilerParams(vmem_limit_bytes=VMEM_LIMIT, collective_id=number, has_side_effects=True),
+        name=name,
+    )
 
 
 def to_quarters(weight):
@@ -229,13 +806,6 @@
 def from_quarters(blocks):
     n, rows, cols = blocks.shape
     return blocks.transpose(1, 0, 2).reshape(rows, n * cols)
-
-
-def rms_back(c, v, gain):
-    r = lax.rsqrt(jnp.mean(v * v, axis=-1, keepdims=True) + EPS)
-    n = v * r
-    cg = c * gain
-    return jnp.sum(c * n, axis=0), r * (cg - n * jnp.mean(cg * n, axis=-1, keepdims=True))
 
 
 def local(
@@ -246,34 +816,45 @@
     n = lax.axis_size("dp")
     cap = 2 * tok // n
     rows = 4 * tok
+    slabs = n * cap
+    rq, ro, rd = w_query.shape[0], w_out.shape[0], w_down.shape[0]
+    ff = rd * n
     owner = dest_slot // (4 * tok)
     slot = dest_slot % tok
     hot = (owner[:, None] == jnp.arange(n, dtype=jnp.int32)[None, :]).astype(BF)
     lower = (jnp.arange(tok)[:, None] > jnp.arange(tok)[None, :]).astype(BF)
     rank = jnp.sum(dot(lower, hot) * hot.astype(F32), axis=1).astype(jnp.int32)
     send_slot = owner * cap + rank
-    place = send_slot[:, None] == jnp.arange(n * cap, dtype=jnp.int32)[None, :]
-    outgoing = dot_tn(place.astype(BF), layer_input).astype(BF)
+    place = send_slot[:, None] == jnp.arange(slabs, dtype=jnp.int32)[None, :]
     labels = jnp.sum(jnp.where(place, slot[:, None] - tok, 0), axis=0, dtype=jnp.int32) + tok
-    received = lax.all_to_all(outgoing.reshape(n, cap, width), "dp", 0, 0, tiled=True).reshape(n * cap, width)
-    in_labels = lax.all_to_all(labels.reshape(n, cap), "dp", 0, 0, tiled=True).reshape(-1)
-    pick = (jnp.arange(tok, dtype=jnp.int32)[:, None] == in_labels[None, :]).astype(BF)
-    owned = dot(pick, received).astype(BF)
-    x_all = lax.all_gather(owned, "ctx", axis=0, tiled=True)
-    og_all = lax.all_gather(out_grad, "ctx", axis=0, tiled=True)
-    gains = lax.all_gather(jnp.concatenate([attn_gain, mlp_gain, q_gain, k_gain])[None, :], BOTH, axis=0, tiled=True)
+    place = place.astype(BF)
+    outgoing = dot_tn(place, layer_input).astype(BF)
+    labels = jnp.broadcast_to(jnp.pad(labels.reshape(n, 1, cap), ((0, 0), (0, 0), (0, 128 - cap))), (n, 8, 128)).reshape(n * 8, 128)
+    index = lax.axis_index("dp") * 4 + lax.axis_index("ctx")
     g_rows, g_heads = attn_gain.shape[0], q_gain.shape[0]
-    gains = gains.astype(F32)
-    ga = gains[:, :g_rows].reshape(1, width)
-    gm = gains[:, g_rows : 2 * g_rows].reshape(1, width)
-    gq = gains[:, 2 * g_rows : 2 * g_rows + g_heads].reshape(1, HD)
-    gk = gains[:, 2 * g_rows + g_heads :].reshape(1, HD)
+
+    def at_lane(values):
+        start = (index * values.shape[0]) % 128
+        return lax.dynamic_update_slice(jnp.zeros((128,), F32), values.astype(F32), (start,))
+
+    gain_block = jnp.stack([at_lane(attn_gain), at_lane(mlp_gain), at_lane(q_gain), at_lane(k_gain)])
+    gain_block = jnp.pad(gain_block, ((0, 4), (0, 0)))
     qkv = jnp.concatenate([to_quarters(w_query), to_quarters(w_key), to_quarters(w_value)], axis=2)
     gu = jnp.concatenate([to_quarters(w_gate), to_quarters(w_up)], axis=2)
-    qkv = lax.all_to_all(qkv, "ctx", 0, 0, tiled=True).reshape(-1, qkv.shape[2])
-    gu = lax.all_to_all(gu, "ctx", 0, 0, tiled=True).reshape(-1, gu.shape[2])
-    wo, wd = (lax.ppermute(w, BOTH, slab_moves(n)) for w in (w_out, w_down))
-    wqkv, wo, wgu, wd = (lax.all_gather(w, "dp", axis=0, tiled=True) for w in (qkv, wo, gu, wd))
+    nb = 4 * rq
+    fw = 2 * ff
+    wqkv, wo, gu, wd, x_all, og_all, pick, ga, gm, gqk = linked(
+        functools.partial(fetch_body, n, cap),
+        (shape(n, 4, rq, width), shape(n, ro, width), shape(4, rq, fw), shape(rd, width), shape(4, tok, width),
+         shape(4, tok, width), shape(tok, slabs), shape(8, width, dtype=F32), shape(8, width, dtype=F32), shape(8, 128, dtype=F32)),
+        [pltpu.VMEM((slabs, width), BF), pltpu.VMEM((n * 8, 128), jnp.int32), pltpu.VMEM((4, 8, 128), F32), pltpu.VMEM((n, 8, 128), F32),
+         Gather.scratch(n, 3), sem_pairs(n), sem_pairs(n), sem_pairs(3), sem_pairs(3), sem_pairs(1), sem_pairs(1), sem_pairs(3), sem_pairs(3), sem_pairs(3)],
+        "fetch", 0,
+    )(outgoing, labels, qkv, w_out, gu, w_down, gain_block, out_grad)
+    wqkv, wo = wqkv.reshape(width, 1024), wo.reshape(512, width)
+    ga, gm, gq, gk = ga[0:1], gm[0:1], gqk[2:3], gqk[3:4]
+    og_all = og_all.reshape(rows, width)
+    x_own = lax.dynamic_index_in_dim(x_all, lax.axis_index("ctx"), 0, keepdims=False)
     cos, sin = rope_tables(rows)
     bias = jnp.where(doc_len[0, 0] > 0, 0.0, MASKED).astype(F32).reshape(1, 1) + jnp.zeros((8, 128), F32)
     part, q, k, v, p, xn, att = in_vmem(
@@ -282,13 +863,16 @@
          shape(rows, 768, dtype=F32), shape(rows, width), shape(rows, 512)),
         [pltpu.VMEM((QB, QB), F32)],
         "attn_fwd",
-    )(x_all, wqkv, wo, ga, gq, gk, cos, sin, bias)
-    x_own = owned.astype(F32)
-    middle = x_own + lax.psum_scatter(part, "ctx", scatter_dimension=0, tiled=True).astype(F32)
-    normed = (middle * lax.rsqrt(jnp.mean(middle * middle, axis=-1, keepdims=True) + EPS) * gm).astype(BF)
-    nm = lax.all_gather(normed, "ctx", axis=0, tiled=True)
-    ff = wd.shape[0]
-    wg, wu = wgu[:, :ff], wgu[:, ff:]
+    )(x_all.reshape(rows, width), wqkv, wo, ga, gq, gk, cos, sin, bias)
+    wgu, wd, nm, middle = linked(
+        functools.partial(middle_body, n),
+        (shape(n, 4, rq, fw), shape(n, rd, width), shape(4, tok, width), shape(tok, width, dtype=F32)),
+        [pltpu.VMEM((4, tok, width), BF), pltpu.VMEM((3, tok, width), BF), Gather.scratch(n, 2), sem_pairs(3), sem_pairs(3)],
+        "middle", 1,
+    )(part.reshape(4, tok, width), x_own, gm, gu, wd)
+    nm = nm.reshape(rows, width)
+    wgu, wd = wgu.reshape(width, fw), wd.reshape(fw // 2, width)
+    wg, wu = wgu[:, : fw // 2], wgu[:, fw // 2 :]
     gate, up = dot(nm, wg), dot(nm, wu)
     s = jax.nn.sigmoid(gate)
     silu = gate * s
@@ -300,44 +884,52 @@
     gwd = dot_tn(hidden, og_all).astype(BF)
     gwgu = jnp.concatenate([dot_tn(nm, d_gate), dot_tn(nm, d_up)], axis=1).astype(BF)
     dnm_part = (dot_nt(d_gate, wg) + dot_nt(d_up, wu)).astype(BF)
-    dnm = lax.psum_scatter(dnm_part, "ctx", scatter_dimension=0, tiled=True).astype(F32)
-    layer_output = (middle + lax.psum_scatter(out_part, "ctx", scatter_dimension=0, tiled=True).astype(F32)).astype(BF)
-    ggm, d_mid = rms_back(dnm, middle, gm)
-    d_middle = out_grad.astype(F32) + d_mid
-    db = lax.all_gather(d_middle.astype(BF), "ctx", axis=0, tiled=True)
+    red, lines, sems = Reduce.scratch(n, [((4, rq, fw), BF), ((rd, width), BF)])
+    db, d_middle, layer_output, ggm, gu, gd = linked(
+        functools.partial(back_body, n),
+        (shape(4, tok, width), shape(tok, width, dtype=F32), shape(tok, width), shape(8, width, dtype=F32), shape(4, rq, fw), shape(rd, width)),
+        [pltpu.VMEM((4, tok, width), BF), pltpu.VMEM((4, tok, width), BF), pltpu.VMEM((n, 4, rq, fw), BF), pltpu.VMEM((n, rd, width), BF),
+         pltpu.VMEM((3, tok, width), BF), pltpu.VMEM((3, tok, width), BF), *red, *lines, sems, sem_pairs(3), sem_pairs(3), sem_pairs(3)],
+        "back", 2,
+    )(dnm_part.reshape(4, tok, width), out_part.reshape(4, tok, width), middle, gm, out_grad,
+      gwgu.reshape(n, 4, rq, fw), gwd.reshape(n, rd, width))
     gwqkv, gwo, dxn_part, ggq, ggk = in_vmem(
         attn_bwd_body,
         (shape(width, 1024), shape(512, width), shape(rows, width), shape(8, HD, dtype=F32), shape(8, HD, dtype=F32)),
         [pltpu.VMEM((QB, QB), F32), pltpu.VMEM((rows, 512), BF), pltpu.VMEM((rows, 512), F32),
          pltpu.VMEM((rows, 256), F32), pltpu.VMEM((rows, 256), F32), pltpu.VMEM((rows, 1024), BF)],
         "attn_bwd",
-    )(db, wo, wqkv, q, k, v, p, xn, att, gq, gk, cos, sin, bias)
-    dxn = lax.psum_scatter(dxn_part, "ctx", scatter_dimension=0, tiled=True).astype(F32)
-    gga, d_x = rms_back(dxn, x_own, ga)
-    owned_grad = (d_middle + d_x).astype(BF)
-    picked = dot_tn(pick, owned_grad).astype(BF)
-    returned = lax.all_to_all(picked.reshape(n, cap, width), "dp", 0, 0, tiled=True).reshape(n * cap, width)
-    input_grad = dot(place.astype(BF), returned).astype(BF)
-    gwqkv, gwo, gwgu, gwd = (lax.psum_scatter(g, "dp", scatter_dimension=0, tiled=True) for g in (gwqkv, gwo, gwgu, gwd))
-    gwo, gwd = (lax.ppermute(g, BOTH, [(b, a) for a, b in slab_moves(n)]).astype(F32) for g in (gwo, gwd))
-    gwqkv = lax.all_to_all(gwqkv.reshape(4, -1, 1024), "ctx", 0, 0, tiled=True).astype(F32)
-    gwgu = lax.all_to_all(gwgu.reshape(4, -1, 2 * ff), "ctx", 0, 0, tiled=True).astype(F32)
-    small = [gga.reshape(4 * n, g_rows), ggm.reshape(4 * n, g_rows), ggq[0].reshape(4 * n, g_heads), ggk[0].reshape(4 * n, g_heads)]
-    small = lax.psum_scatter(jnp.concatenate(small, axis=1), BOTH, scatter_dimension=0, tiled=True)[0]
+    )(db.reshape(rows, width), wo, wqkv, q, k, v, p, xn, att, gq, gk, cos, sin, bias)
+    red, lines, sems = Reduce.scratch(n, [((4, rq, 1024), BF), ((ro, width), BF), ((8, 128), F32)])
+    input_grad, g_qkv, g_o, g_gu, g_d, small = linked(
+        functools.partial(finish_body, n, cap),
+        (shape(tok, width), shape(4, rq, 1024), shape(ro, width), shape(4, rq, fw), shape(rd, width), shape(8, 128, dtype=F32)),
+        [pltpu.VMEM((4, tok, width), BF), pltpu.VMEM((n, 4, rq, 1024), BF), pltpu.VMEM((n, ro, width), BF), pltpu.VMEM((n, 8, 128), F32),
+         pltpu.VMEM((3, tok, width), BF), pltpu.VMEM((slabs, width), BF), pltpu.VMEM((slabs, width), BF), *red, *lines,
+         pltpu.VMEM((4, rq, 1024), BF), pltpu.VMEM((ro, width), BF), pltpu.VMEM((8, 128), F32), pltpu.VMEM((4, 8, 128), F32),
+         sems, sem_pairs(3), sem_pairs(n), sem_pairs(3), sem_pairs(1), sem_pairs(3), sem_pairs(1), sem_pairs(3)],
+        "finish", 3,
+    )(dxn_part.reshape(4, tok, width), d_middle, x_own, ga, pick, place, gwqkv.reshape(n, 4, rq, 1024), gwo.reshape(n, ro, width),
+      gu, gd, ggm, ggq, ggk)
+
+    def own_lanes(row, count):
+        return lax.dynamic_slice(small[row], ((index * count) % 128,), (count,))
+
+    g_qkv, g_gu = g_qkv.astype(F32), g_gu.astype(F32)
     return (
         layer_output,
         input_grad,
-        small[:g_rows],
-        from_quarters(gwqkv[:, :, :512]),
-        from_quarters(gwqkv[:, :, 512:768]),
-        from_quarters(gwqkv[:, :, 768:]),
-        small[2 * g_rows : 2 * g_rows + g_heads],
-        small[2 * g_rows + g_heads :],
-        gwo,
-        small[g_rows : 2 * g_rows],
-        from_quarters(gwgu[:, :, :ff]),
-        from_quarters(gwgu[:, :, ff:]),
-        gwd,
+        own_lanes(0, g_rows),
+        from_quarters(g_qkv[:, :, :512]),
+        from_quarters(g_qkv[:, :, 512:768]),
+        from_quarters(g_qkv[:, :, 768:]),
+        own_lanes(2, g_heads),
+        own_lanes(3, g_heads),
+        g_o.astype(F32),
+        own_lanes(1, g_rows),
+        from_quarters(g_gu[:, :, : fw // 2]),
+        from_quarters(g_gu[:, :, fw // 2 :]),
+        g_d.astype(F32),
     )
 
 

time: 862 us -> 420 us (0.49)
  waiting for transfers between devices: 558 us -> 0 us
  Pallas kernels: 59.3 us -> 350 us
  blocking collectives: 101 us -> 0 us
  starting transfers between devices: 47.1 us -> 0 us
  matrix products: 45.5 us -> 29.9 us
  between operations: 14.4 us -> 1.47 us
    reduce_scatter x8 -> x0, waiting for transfers between devices: 323 us -> none  [the longest x4 218 us: local(): lax.psum_scatter(g, 'dp', scatter_dimension=0, tiled=True)]
    pallas_call x0 -> x4, Pallas kernels: none -> 290 us  [the longest x1 83.5 us: local(): linked(functools.partial(fetch_body, n, cap), (shape(n, 4, rq, width), sh...]
    all_gather x8 -> x0, waiting for transfers between devices: 175 us -> none  [the longest x4 95.2 us: local(): lax.all_gather(w, 'dp', axis=0, tiled=True)]
    unnamed x2 -> x0, blocking collectives: 80 us -> none
    all_to_all x5 -> x0, waiting for transfers between devices: 37.3 us -> none  [the longest x1 32.6 us: local(): lax.all_to_all(outgoing.reshape(n, cap, width), 'dp', 0, 0, tiled=True)]
    all_to_all x5 -> x0, starting transfers between devices: 24.2 us -> none  [the longest x1 6.08 us: local(): lax.all_to_all(gwqkv.reshape(4, -1, 1024), 'ctx', 0, 0, tiled=True)]
    ppermute x4 -> x0, starting transfers between devices: 21.9 us -> none  [the longest x2 11.5 us: local(): lax.ppermute(g, BOTH, [(b, a) for a, b in slab_moves(n)]).astype(F32)]
    all_to_all x2 -> x0, blocking collectives: 20.8 us -> none  [the longest x1 10.4 us: local(): qkv = lax.all_to_all(qkv, 'ctx', 0, 0, tiled=True).reshape(-1, qkv.shape[2])]
  transfers between devices with their start and end apart: 25 -> 0, of which waited for: 22 -> 0; matrix products, arithmetic and copies ran while one was open for 7% -> 0% of each run, Pallas kernels for 5% -> 0%
where the time goes in v2:
time: 420 us; the launch traced here: 413 us
  Pallas kernels  350 us (83%)
  matrix products  29.9 us (7%)
  local copies, waits for them, and re-layouts  20.5 us (5%)
  other arithmetic  11.1 us (3%)
    pallas_call x1, Pallas kernels, local(): linked(functools.partial(fetch_body, n, cap), (shape(n, 4, rq, width), sh...  83.5 us
    pallas_call x1, Pallas kernels, local(): linked(functools.partial(finish_body, n, cap), (shape(tok, width), shape(...  81.9 us
    pallas_call x1, Pallas kernels, local(): linked(functools.partial(back_body, n), (shape(4, tok, width), shape(tok,...  62.6 us
    pallas_call x1, Pallas kernels, local(): linked(functools.partial(middle_body, n), (shape(n, 4, rq, fw), shape(n,...  62.3 us
    pallas_call x1, Pallas kernels, local(): in_vmem(attn_bwd_body, (shape(width, 1024), shape(512, width), shape(rows...  40.3 us
    pallas_call x1, Pallas kernels, local(): in_vmem(attn_fwd_body, (shape(rows, width), shape(rows, 512), shape(rows,...  19 us
    dot_general x4, matrix products, dot(): lax.dot_general(a, b, (((1,), (0,)), ((), ())), preferred_element_type=F32)  10.6 us
    dot_general x4, matrix products, dot_tn(): lax.dot_general(a, b, (((0,), (0,)), ((), ())), preferred_element_type=F32)  10.3 us

profile of v2, /device:TPU:3, one launch (start us, length us, event | category | flops | bytes accessed | tf_op | source)
XLA Modules:
  0.0 412.5 jit_solution(8294127203669794395)
XLA Ops:
  0.6 0.0 copy-start
  0.7 0.0 copy-start.11
  0.7 0.0 copy-start.10
  0.7 0.0 copy-start.9
  0.7 0.7 bitcast_convert_fusion.3
  1.4 0.2 dynamic_update_slice.16
  1.6 0.7 bitcast_convert_fusion.2
  2.3 0.2 dynamic_update_slice.17
  2.5 0.7 bitcast_convert_fusion.1
  3.2 0.2 dynamic_update_slice.18
  3.3 0.7 bitcast_convert_fusion
  4.0 0.2 dynamic_update_slice.19
  4.2 0.6 select_maximum_fusion.gain_ref
  4.8 0.7 fusion.15
  5.5 0.2 fusion.10
  5.7 0.1 select_reduce_fusion
  5.9 0.1 add.82
  6.0 0.6 broadcast_bitcast_fusion.lab_ref
  6.6 1.6 convolution_convert_fusion.4.out_ref
  8.1 1.0 bitcast_bitcast_fusion
  9.2 0.0 copy-start.17
  9.2 0.8 pad_maximum_fusion.1.gu_ref
  10.0 0.7 pad_maximum_fusion.2.qkv_ref
  10.8 83.5 %fetch.1 = (bf16[8,4,32,1024]{3,2,1,0:T(8,128)(2,1)}, bf16[8,64,1024]{2,1,0:T(8,128)(2,1)}, bf16[4,32,1536]{2,1,0:T(8,128)(2,1)}, bf16[96,1024]{1,0:T(8,128)(2,1...) custom-call(bf16[512,1024]{1,0:T(8,128)(2,1)} %convolution_convert_f, ...), custom_call_target="tpu_custom_call" | custom-call | tf_op jit(solution)/shard_map/fetch/pallas_call | solution.py:846
  94.3 1.4 slice.48.ga_ref
  95.6 1.3 fusion.21
  96.9 0.6 add.88.bias_ref
  97.5 19.0 %attn_fwd.1 = (bf16[1024,1024]{1,0:T(8,128)(2,1)}, bf16[1024,512]{1,0:T(8,128)(2,1)}, bf16[1024,256]{1,0:T(8,128)(2,1)}, bf16[1024,256]{1,0:T(8,128)(2,1)}, f32[...) custom-call(bf16[1024,1024]{1,0:T(8,128)(2,1)} %bitcast.120, bf16[1024,1024]{1,0:T(8,128)(2,1)} %bitcast.116, ...), custom_call_target="tpu_custom_call" | custom-call | tf_op jit(solution)/shard_map/attn_fwd/pallas_call | solution.py:860
  116.5 1.9 dynamic-slice_bitcast_fusion.x_ref
  118.4 1.4 slice.52.gm_ref
  119.8 62.3 %middle.1 = (bf16[8,4,32,1536]{3,2,1,0:T(8,128)(2,1)}, bf16[8,96,1024]{2,1,0:T(8,128)(2,1)}, bf16[4,256,1024]{2,1,0:T(8,128)(2,1)}, f32[256,1024]{1,0:T(8,128)}) custom-call(bf16[4,256,1024]{2,1,0:T(8,128)(2,1)} %bitcast.123, bf16[256,1024]{1,0:T(8,128)(2,1)} %dynamic-slice_bitcast_fusion.x_ref, f32[1,1024]{1,0:T(1,128)} %slice.52.gm_ref, ...), custom_call_target="tpu_custom_call" | custom-call | tf_op jit(solution)/shard_map/middle/pallas_call | solution.py:867
  182.1 4.0 fusion.22
  186.1 1.8 fusion.5
  187.9 5.5 %multiply_convert_fusion = (bf16[1024,768]{1,0:T(8,128)(2,1)}, bf16[1024,768]{1,0:T(8,128)(2,1)}, bf16[1024,768]{1,0:T(8,128)(2,1)}) fusion(f32[1024,768]{1,0:T(8,128)S(1)} %fusion.5, f32[1024,768]{1,0:T(8,128)S(1)} %fusion.22, bf16[1024,1024]{1,0:T(8,128)(2,1)S(1)} %bitcast.125, bf16[1024,1536]{1,0:T(8,128)(2,1)S(1)} %bitcast.146), kind=kOutput, calls=%fused_computation.2 | convolution fusion | flops 1622409216 | bytes 14680064 | tf_op jit(solution)/shard_map/dot_general | solution.py:28
  193.4 2.6 copy.36
  196.0 4.0 convolution_convert_fusion.3
  200.0 1.8 convolution_convert_fusion.2
  201.8 2.0 pad_maximum_fusion.gwgu_in
  203.8 0.4 copy-done.15
  204.2 0.8 copy-done.20
  205.0 3.0 convolution_convert_fusion.1
  208.0 3.1 convolution_convert_fusion
  211.1 1.8 fusion.3
  212.9 3.2 add_convert_fusion
  216.1 62.6 %back.1 = (bf16[4,256,1024]{2,1,0:T(8,128)(2,1)}, f32[256,1024]{1,0:T(8,128)}, bf16[256,1024]{1,0:T(8,128)(2,1)}, f32[8,1024]{1,0:T(8,128)}, bf16[4,32,1536]{2,1,0:T(8,128)(2,1)}, /*index=5*/bf16[96,1024]{1,0:T(8,128)(2,1)}) custom-call(bf16[4,256,1024]{2,1,0:T(8,128)(2,1)} %bitcast.122, bf16[4,256,1024]{2,1,0:T(8,128)(2,1)} %bitcast.121, ...), custom_call_target="tpu_custom_call" | custom-call | tf_op jit(solution)/shard_map/back/pallas_call | solution.py:888
  278.7 40.3 %attn_bwd.1 = (bf16[1024,1024]{1,0:T(8,128)(2,1)}, bf16[512,1024]{1,0:T(8,128)(2,1)}, bf16[1024,1024]{1,0:T(8,128)(2,1)}, f32[8,128]{1,0:T(8,128)}, f32[8,128]{1,0:T(8,128)}) custom-call(bf16[1024,1024]{1,0:T(8,128)(2,1)} %bitcast.131, bf16[512,1024]{1,0:T(8,128)(2,1)} %bitcast.119, bf16[1024,1024]{1,0:T(8,128)(2,1)} %bitcast.117, ...), custom_call_target="tpu_custom_call" | custom-call | tf_op jit(solution)/shard_map/attn_bwd/pallas_call | solution.py:896
  319.0 0.8 fusion.11.place_ref
  319.8 81.9 %finish.1 = (bf16[256,1024]{1,0:T(8,128)(2,1)}, bf16[4,32,1024]{2,1,0:T(8,128)(2,1)}, bf16[64,1024]{1,0:T(8,128)(2,1)}, bf16[4,32,1536]{2,1,0:T(8,128)(2,1)}, bf...) custom-call(bf16[4,256,1024]{2,1,0:T(8,128)(2,1)} %bitcast.130, f32[256,1024]{1,0:T(8,128)} %get-tuple-element.74.dmid_ref, ...), custom_call_target="tpu_custom_call" | custom-call | tf_op jit(solution)/shard_map/finish/pallas_call | solution.py:904
  401.7 1.1 convert_element_type.67
  402.8 0.1 slice_bitcast_fusion
  402.9 0.8 copy.52
  403.7 0.8 copy.53
  404.6 0.0 copy-start.1
  404.6 0.7 copy.49
  405.3 0.7 copy.50
  406.0 0.7 copy.51
  406.6 0.6 fusion.16
  407.2 0.6 fusion.17
  407.8 0.6 fusion.18
  408.4 0.6 fusion.19
  409.0 0.8 convert_element_type.68
  409.8 0.7 convert_element_type.66
  410.5 0.8 copy.66
  411.3 0.8 copy.67
  (47 shorter events, 0.2 us)
Async XLA Ops:
  0.6 5.9 %copy-start = (bf16[256,1024]{1,0:T(8,128)(2,1)S(1)}, bf16[256,1024]{1,0:T(8,128)(2,1)}, u32[]{:S(2)}) copy-start(bf16[256,1024]{1,0:T(8,128)(2,1)} %param.17) | copy-start | bytes 1572868
  0.7 9.3 %copy-start.11 = (bf16[32,1024]{1,0:T(8,128)(2,1)S(1)}, bf16[32,1024]{1,0:T(8,128)(2,1)}, u32[]{:S(2)}) copy-start(bf16[32,1024]{1,0:T(8,128)(2,1)} %param.23) | copy-start | bytes 196612
  0.7 9.3 %copy-start.10 = (bf16[32,1024]{1,0:T(8,128)(2,1)S(1)}, bf16[32,1024]{1,0:T(8,128)(2,1)}, u32[]{:S(2)}) copy-start(bf16[32,1024]{1,0:T(8,128)(2,1)} %param.24) | copy-start | bytes 196612
  0.7 9.3 %copy-start.9 = (bf16[32,2048]{1,0:T(8,128)(2,1)S(1)}, bf16[32,2048]{1,0:T(8,128)(2,1)}, u32[]{:S(2)}) copy-start(bf16[32,2048]{1,0:T(8,128)(2,1)} %param.22) | copy-start | bytes 393220
  9.2 87.7 %copy-start.17 = (s32[1,2]{1,0:T(1,128)S(1)}, s32[1,2]{1,0:T(1,128)}, u32[]{:S(2)}) copy-start(s32[1,2]{1,0:T(1,128)} %param.19) | copy-start | bytes 28
  182.1 4.0 copy-start.2
  182.1 4.0 copy-start.13
  196.0 4.0 copy-start.3
  196.0 4.0 copy-start.18
  201.8 2.4 copy-start.15
  201.8 3.2 copy-start.20
  205.0 3.0 copy-start.16
  208.0 3.1 copy-start.14
  208.0 3.1 copy-start.19
  401.7 2.8 copy-start.6
  402.9 3.7 copy-start.12
  402.9 6.1 %copy-start.7 = (bf16[96,1024]{1,0:T(8,128)(2,1)S(1)}, bf16[96,1024]{1,0:T(8,128)(2,1)}, u32[]{:S(2)}) copy-start(bf16[96,1024]{1,0:T(8,128)(2,1)} %get-tuple-element.88) | copy-start | bytes 589828
  403.7 6.1 %copy-start.8 = (bf16[64,1024]{1,0:T(8,128)(2,1)S(1)}, bf16[64,1024]{1,0:T(8,128)(2,1)}, u32[]{:S(2)}) copy-start(bf16[64,1024]{1,0:T(8,128)(2,1)} %get-tuple-element.86) | copy-start | bytes 393220
  404.5 6.0 %copy-start.4 = (bf16[256,1024]{1,0:T(8,128)(2,1)S(1)}, bf16[256,1024]{1,0:T(8,128)(2,1)}, u32[]{:S(2)}) copy-start(bf16[256,1024]{1,0:T(8,128)(2,1)} %get-tuple-element.121) | copy-start | bytes 1572868
  404.5 6.8 %copy-start.5 = (bf16[256,1024]{1,0:T(8,128)(2,1)S(1)}, bf16[256,1024]{1,0:T(8,128)(2,1)}, u32[]{:S(2)}) copy-start(bf16[256,1024]{1,0:T(8,128)(2,1)} %get-tuple-element.122) | copy-start | bytes 1572868
  404.6 7.5 %copy-start.1 = (bf16[256,1024]{1,0:T(8,128)(2,1)S(1)}, bf16[256,1024]{1,0:T(8,128)(2,1)}, u32[]{:S(2)}) copy-start(bf16[256,1024]{1,0:T(8,128)(2,1)} %param.17) | copy-start | bytes 1572868

commit v3 on v2

--- a/solution.py
+++ b/solution.py
@@ -54,127 +54,109 @@
     return jnp.where(rows == cols, 0.0, jnp.where(cols < rows, off_bias, MASKED))
 
 
-def attn_fwd_body(
-    x_ref, wqkv_ref, wo_ref, ga_ref, gq_ref, gk_ref, cos_ref, sin_ref, bias_ref,
-    part_ref, q_ref, k_ref, v_ref, p_ref, xn_ref, att_ref, mask_ref,
-):
-    rows = x_ref.shape[0]
+def rows_of(ref):
+    value = ref[...]
+    return value.reshape(-1, value.shape[-1])
+
+
+def attn_project(x_ref, w, ga, gq, gk, cos_ref, sin_ref, q_ref, k_ref, v_ref, p_ref, xn_ref):
+    rows = xn_ref.shape[0]
+    tok = x_ref.shape[1]
     nq = q_ref.shape[1] // HD
     nk = k_ref.shape[1] // HD
-    gain_a = ga_ref[...]
-
-    @pl.loop(0, rows // QB)
+
+    @pl.loop(0, rows // tok)
     def _(i):
-        here = lanes(i, QB)
-        x = x_ref[here, :].astype(F32)
+        here = lanes(i, tok)
+        x = x_ref[i].astype(F32)
         r = lax.rsqrt(jnp.mean(x * x, axis=-1, keepdims=True) + EPS)
-        xn = (x * r * gain_a).astype(BF)
+        xn = (x * r * ga[0:1, :]).astype(BF)
         xn_ref[here, :] = xn
-        p = dot(xn, wqkv_ref[...])
+        p = dot(xn, rows_of(w))
         p_ref[here, :] = p[:, : (nq + nk) * HD]
         v_ref[here, :] = p[:, (nq + nk) * HD :].astype(BF)
         cos = cos_ref[here, :]
         sin = sin_ref[here, :]
         for h in range(nq + nk):
             ph = p[:, h * HD : (h + 1) * HD]
-            g = gq_ref[...] if h < nq else gk_ref[...]
-            n = ph * lax.rsqrt(jnp.mean(ph * ph, axis=-1, keepdims=True) + EPS) * g
-            rot = (n * cos + pltpu.roll(n, HD // 2, 1) * sin).astype(BF)
+            g = gq if h < nq else gk
+            nv = ph * lax.rsqrt(jnp.mean(ph * ph, axis=-1, keepdims=True) + EPS) * g
+            rot = (nv * cos + pltpu.roll(nv, HD // 2, 1) * sin).astype(BF)
             if h < nq:
                 q_ref[here, h * HD : (h + 1) * HD] = rot
             else:
                 k_ref[here, (h - nq) * HD : (h - nq + 1) * HD] = rot
 
-    off = bias_ref[0:1, 0:1]
-    mask_ref[...] = mask_block(off)
-
-    @pl.loop(0, nq)
-    def _(h):
-        hq = lanes(h, HD)
-        hk = lanes(lax.div(h * nk, nq), HD)
-        for i in range(rows // QB):
-            q = q_ref[i * QB : (i + 1) * QB, hq]
-            es, total = [], None
-            for j in range(i + 1):
-                s = dot_nt(q, k_ref[j * QB : (j + 1) * QB, hk]) * (SCALE * LOG2E)
-                e = jnp.exp2(s + (mask_ref[...] if j == i else off))
-                t = jnp.sum(e, axis=-1, keepdims=True)
-                total = t if total is None else total + t
-                es.append(e)
-            inv = 1.0 / total
-            o = None
-            for j in range(i + 1):
-                c = dot((es[j] * inv).astype(BF), v_ref[j * QB : (j + 1) * QB, hk])
-                o = c if o is None else o + c
-            att_ref[i * QB : (i + 1) * QB, hq] = o.astype(BF)
-
-    @pl.loop(0, rows // QB)
-    def _(i):
-        here = lanes(i, QB)
-        part_ref[here, :] = dot(att_ref[here, :], wo_ref[...]).astype(BF)
-
-
-def attn_bwd_body(
-    db_ref, wo_ref, wqkv_ref, q_ref, k_ref, v_ref, p_ref, xn_ref, att_ref,
-    gq_ref, gk_ref, cos_ref, sin_ref, bias_ref,
-    gwqkv_ref, gwo_ref, dxn_ref, ggq_ref, ggk_ref,
-    mask_ref, da_ref, dq_ref, dk_ref, dv_ref, dp_ref,
-):
-    rows = db_ref.shape[0]
-    nq = q_ref.shape[1] // HD
-    nk = k_ref.shape[1] // HD
-    group = nq // nk
-
-    @pl.loop(0, rows // QB)
-    def _(i):
-        here = lanes(i, QB)
-        da_ref[here, :] = dot_nt(db_ref[here, :], wo_ref[...]).astype(BF)
-
-    off = bias_ref[0:1, 0:1]
-    mask_ref[...] = mask_block(off)
-    dk_ref[...] = jnp.zeros_like(dk_ref)
-    dv_ref[...] = jnp.zeros_like(dv_ref)
-
-    @pl.loop(0, nq)
-    def _(h):
-        hq = lanes(h, HD)
-        hk = lanes(lax.div(h, group), HD)
-        for i in range(rows // QB):
-            here = slice(i * QB, (i + 1) * QB)
-            q = q_ref[here, hq]
-            da = da_ref[here, hq]
-            inner = jnp.sum(da.astype(F32) * att_ref[here, hq].astype(F32), axis=-1, keepdims=True)
-            es, total = [], None
-            for j in range(i + 1):
-                s = dot_nt(q, k_ref[j * QB : (j + 1) * QB, hk]) * (SCALE * LOG2E)
-                e = jnp.exp2(s + (mask_ref[...] if j == i else off))
-                t = jnp.sum(e, axis=-1, keepdims=True)
-                total = t if total is None else total + t
-                es.append(e)
-            inv = 1.0 / total
-            dq = None
-            for j in range(i + 1):
-                keys = slice(j * QB, (j + 1) * QB)
-                probs = es[j] * inv
-                ds = (probs * (dot_nt(da, v_ref[keys, hk]) - inner)).astype(BF)
-                c = dot(ds, k_ref[keys, hk])
-                dq = c if dq is None else dq + c
-                dk_ref[keys, hk] += dot_tn(ds, q)
-                dv_ref[keys, hk] += dot_tn(probs.astype(BF), da)
-            dq_ref[here, hq] = dq
-
+
+def attn_head(h, off, q_ref, k_ref, v_ref, att_ref, mask_ref):
+    rows = q_ref.shape[0]
+    group = q_ref.shape[1] // k_ref.shape[1]
+    hq = lanes(h, HD)
+    hk = lanes(h // group, HD)
+    for i in range(rows // QB):
+        q = q_ref[i * QB : (i + 1) * QB, hq]
+        es, total = [], None
+        for j in range(i + 1):
+            s = dot_nt(q, k_ref[j * QB : (j + 1) * QB, hk]) * (SCALE * LOG2E)
+            e = jnp.exp2(s + (mask_ref[...] if j == i else off))
+            t = jnp.sum(e, axis=-1, keepdims=True)
+            total = t if total is None else total + t
+            es.append(e)
+        inv = 1.0 / total
+        o = None
+        for j in range(i + 1):
+            c = dot((es[j] * inv).astype(BF), v_ref[j * QB : (j + 1) * QB, hk])
+            o = c if o is None else o + c
+        att_ref[i * QB : (i + 1) * QB, hq] = o.astype(BF)
+
+
+def attn_head_back(h, off, q_ref, k_ref, v_ref, att_ref, da_ref, dq_ref, dk_ref, dv_ref, mask_ref):
+    rows = q_ref.shape[0]
+    group = q_ref.shape[1] // k_ref.shape[1]
+    hq = lanes(h, HD)
+    hk = lanes(h // group, HD)
+    for i in range(rows // QB):
+        here = slice(i * QB, (i + 1) * QB)
+        q = q_ref[here, hq]
+        da = da_ref[here, hq]
+        inner = jnp.sum(da.astype(F32) * att_ref[here, hq].astype(F32), axis=-1, keepdims=True)
+        es, total = [], None
+        for j in range(i + 1):
+            s = dot_nt(q, k_ref[j * QB : (j + 1) * QB, hk]) * (SCALE * LOG2E)
+            e = jnp.exp2(s + (mask_ref[...] if j == i else off))
+            t = jnp.sum(e, axis=-1, keepdims=True)
+            total = t if total is None else total + t
+            es.append(e)
+        inv = 1.0 / total
+        dq = None
+        for j in range(i + 1):
+            keys = slice(j * QB, (j + 1) * QB)
+            probs = es[j] * inv
+            ds = (probs * (dot_nt(da, v_ref[keys, hk]) - inner)).astype(BF)
+            c = dot(ds, k_ref[keys, hk])
+            dq = c if dq is None else dq + c
+            dk_ref[keys, hk] += dot_tn(ds, q)
+            dv_ref[keys, hk] += dot_tn(probs.astype(BF), da)
+        dq_ref[here, hq] = dq
+
+
+def attn_unproject(gq, gk, cos_ref, sin_ref, p_ref, dq_ref, dk_ref, dv_ref, dp_ref, w, dxn_ref, ggq_ref, ggk_ref):
+    rows = p_ref.shape[0]
+    tok = dxn_ref.shape[1]
+    nq = dq_ref.shape[1] // HD
+    nk = dk_ref.shape[1] // HD
     ggq_ref[...] = jnp.zeros_like(ggq_ref)
     ggk_ref[...] = jnp.zeros_like(ggk_ref)
 
-    @pl.loop(0, rows // QB)
+    @pl.loop(0, rows // tok)
     def _(i):
-        here = lanes(i, QB)
+        here = lanes(i, tok)
         cos = cos_ref[here, :]
         sin = sin_ref[here, :]
         sums = [jnp.zeros((1, HD), F32), jnp.zeros((1, HD), F32)]
         for h in range(nq + nk):
             which = 0 if h < nq else 1
-            g = (gq_ref if h < nq else gk_ref)[...]
+            g = gq if h < nq else gk
             cols = slice(h * HD, (h + 1) * HD)
             if h < nq:
                 d = dq_ref[here, cols] * SCALE
@@ -190,17 +172,18 @@
         dp_ref[here, (nq + nk) * HD :] = dv_ref[here, :].astype(BF)
         ggq_ref[0:1, :] += sums[0]
         ggk_ref[0:1, :] += sums[1]
-        dxn_ref[here, :] = dot_nt(dp_ref[here, :], wqkv_ref[...]).astype(BF)
-
-    @pl.loop(0, gwo_ref.shape[0] // 128)
+        dxn_ref[i] = dot_nt(dp_ref[here, :], rows_of(w)).astype(BF)
+
+
+def weight_grad(out_ref, left_ref, right, chunk=128):
+    size = math.prod(out_ref.shape[1:-1])
+    width = out_ref.shape[-1]
+
+    @pl.loop(0, left_ref.shape[1] // chunk)
     def _(i):
-        cols = lanes(i, 128)
-        gwo_ref[cols, :] = dot_tn(att_ref[:, cols], db_ref[...]).astype(BF)
-
-    @pl.loop(0, gwqkv_ref.shape[0] // 128)
-    def _(i):
-        cols = lanes(i, 128)
-        gwqkv_ref[cols, :] = dot_tn(xn_ref[:, cols], dp_ref[...]).astype(BF)
+        g = dot_tn(left_ref[:, lanes(i, chunk)], rows_of(right)).astype(BF)
+        for j in range(chunk // size):
+            out_ref[i * (chunk // size) + j] = g[j * size : (j + 1) * size].reshape(out_ref.shape[1:-1] + (width,))
 
 
 MESH = pl.DeviceIdType.MESH
@@ -309,12 +292,17 @@
                     self.copy(b, p, 0).wait_recv()
                 self.send(p, up, not up)
 
-    def finish(self):
+    def arrive(self):
         at = self.at
         for b in range(len(self.bufs)):
             for p in range(at.line):
                 block = self.bufs[b].at[p * 2 + 1 - at.inner]
                 rcopy(block, block, self.sems.at[2, b, p], self.sems.at[4, b, p], dp=at.dp_inner).wait_recv()
+
+    def finish(self):
+        at = self.at
+        for b in range(len(self.bufs)):
+            for p in range(at.line):
                 self.copy(b, p, 2).wait_send()
 
                 @pl.when(jnp.logical_and(at.has_up, p <= at.outer))
@@ -349,7 +337,7 @@
     def line_copy(self, b, p, slot, up):
         at = self.at
         return rcopy(
-            self.parts[b].at[p * 2 + at.inner], self.from_line[b].at[slot],
+            self.from_inner[b].at[p], self.from_line[b].at[slot],
             self.sems.at[2, b, p], self.sems.at[3, b, slot], dp=at.dp_up if up else at.dp_down,
         )
 
@@ -380,7 +368,7 @@
                 @pl.when(there)
                 def _():
                     self.inner_copy(b, p).wait_recv()
-                    into = self.parts[b].at[p * 2 + at.inner]
+                    into = self.from_inner[b].at[p]
 
                     @pl.when(more)
                     def _():
@@ -448,9 +436,11 @@
         self.copy(1, self.at.c_x).wait_recv()
         self.copy(2, self.at.c_x).start()
 
-    def finish(self):
+    def arrive(self):
         self.copy(0, self.at.c_core).wait_recv()
         self.copy(2, self.at.c_far).wait_recv()
+
+    def finish(self):
         for k in range(3):
             self.copy(k, self.at.ctx).wait_send()
 
@@ -461,7 +451,7 @@
 
     def copy(self, k):
         at = self.at
-        block = self.part.at[(at.c_core, at.c_far, at.c_x)[k]]
+        block = self.got.at[1] if k == 2 else self.part.at[(at.c_core, at.c_far)[k]]
         return rcopy(block, self.got.at[k], self.sems.at[0, k], self.sems.at[1, k], ctx=at.c_x if k == 2 else at.c_core)
 
     def start(self):
@@ -470,8 +460,8 @@
 
     def across(self):
         self.copy(1).wait_recv()
-        into = self.part.at[self.at.c_x]
-        into[...] = (into[...].astype(F32) + self.got[1].astype(F32)).astype(into.dtype)
+        into = self.got.at[1]
+        into[...] = (self.part[self.at.c_x].astype(F32) + into[...].astype(F32)).astype(into.dtype)
         self.copy(2).start()
 
     def result(self):
@@ -553,23 +543,20 @@
     return pltpu.SemaphoreType.DMA((2, count))
 
 
-def fetch_body(
+def forward_body(
     n, cap,
-    out_ref, lab_ref, qkv_ref, wo_src, gu_ref, wd_src, gain_ref, og_ref,
-    wqkv_ref, wo_ref, gu_out, wd_out, x_ref, og_all, pick_ref, ga_ref, gm_ref, gqk_ref,
-    recv, labels, gains_c, gains_n,
-    s_gather, s_rows, s_labs, s_qkv, s_gu, s_wo, s_wd, s_gain, s_x, s_og,
+    out_ref, lab_ref, qkv_ref, wo_src, gu_ref, wd_src, gain_ref, og_ref, cos_ref, sin_ref, bias_ref,
+    wqkv_ref, wo_ref, wgu_ref, wd_ref, x_own, og_all, pick_ref, ga_ref, gm_ref, gqk_ref,
+    q_ref, k_ref, v_ref, p_ref, xn_ref, att_ref, nm_ref, mid_ref,
+    recv, labels, gains_c, gains_n, x_ref, part_ref, got, mask_ref,
+    s_ga, s_gb, s_gc, s_rows, s_labs, s_qkv, s_gu, s_wo, s_wd, s_gain, s_x, s_og, s_red, s_nm,
 ):
     at = Place(n)
     greet(at, line=True, all_dp=True, slabs=at.slab_from)
     qkv = Quarters(at, qkv_ref, wqkv_ref.at[at.dp], s_qkv)
-    wo = Slab(at, wo_src, wo_ref.at[at.slab_to["dp"]], s_wo, at.slab_to)
     rows = Exchange(at, out_ref, recv, cap, s_rows)
     labs = Exchange(at, lab_ref, labels, 8, s_labs)
-    wo.start()
     qkv.start()
-    labs.start()
-    rows.start()
     gains = [
         rcopy(gain_ref, gains_c.at[at.ctx], s_gain.at[0, k], s_gain.at[1, k], ctx=c)
         for k, c in enumerate((at.c_x, at.c_far, at.c_core))
@@ -577,35 +564,46 @@
     for g in gains:
         g.start()
     gains_c[at.ctx] = gain_ref[...]
-    wd = Slab(at, wd_src, wd_out, s_wd, at.slab_to)
-    gu = Quarters(at, gu_ref, gu_out, s_gu)
-    wd.start()
-    gu.start()
-    og_all[at.ctx] = og_ref[...]
-    og = CtxGather(at, og_all, s_og)
-    og.start()
+    labs.start()
+    rows.start()
     for g in gains:
         g.wait()
     gains_n[at.dp] = gains_c[0] + gains_c[1] + gains_c[2] + gains_c[3]
     qkv.finish()
-    wo.finish()
-    gather = Gather(at, [wqkv_ref, wo_ref, gains_n], s_gather)
-    gather.start()
-    gather.step(1)
+    first = Gather(at, [wqkv_ref, gains_n], s_ga)
+    first.start()
+    wo = Slab(at, wo_src, wo_ref.at[at.slab_to["dp"]], s_wo, at.slab_to)
+    wd = Slab(at, wd_src, wd_ref.at[at.slab_to["dp"]], s_wd, at.slab_to)
+    gu = Quarters(at, gu_ref, wgu_ref.at[at.dp], s_gu)
+    wo.start()
+    gu.start()
+    wd.start()
+    og_all[at.ctx] = og_ref[...]
+    og = CtxGather(at, og_all, s_og)
     labs.finish()
     tok = x_ref.shape[1]
     slots = lax.broadcasted_iota(jnp.int32, (tok, cap), 0)
     for j in range(n):
         pick_ref[:, j * cap : (j + 1) * cap] = (slots == labels[j * 8 : j * 8 + 1, :cap]).astype(BF)
+    first.step(1)
     rows.finish()
-    x_ref[at.ctx] = dot(pick_ref[...], recv[...]).astype(BF)
+    owned = dot(pick_ref[...], recv[...]).astype(BF)
+    x_ref[at.ctx] = owned
+    x_own[...] = owned
     x = CtxGather(at, x_ref, s_x)
     x.start()
-    og.forward()
+    og.start()
     for t in range(2, at.line):
-        gather.step(t)
+        first.step(t)
+    wo.finish()
+    second = Gather(at, [wo_ref], s_gb)
+    second.start()
+    wd.finish()
+    gu.finish()
+    third = Gather(at, [wgu_ref, wd_ref], s_gc)
+    third.start()
     x.forward()
-    gather.finish()
+    first.arrive()
     own = 4 * ga_ref.shape[1] // (4 * n)
     ga_ref[...] = jnp.zeros_like(ga_ref)
     gm_ref[...] = jnp.zeros_like(gm_ref)
@@ -617,40 +615,47 @@
         gm_ref[0:1, tile] += block[1:2]
         gqk = gqk + block
     gqk_ref[...] = gqk
-    for part in (og, x, wd, gu):
-        part.finish()
-
-
-def middle_body(
-    n,
-    part_in, x_ref, gm_ref, gu_ref, wd_src,
-    wgu_ref, wd_ref, nm_ref, mid_ref,
-    part_ref, got, s_gather, s_red, s_nm,
-):
-    at = Place(n)
-    wgu_ref[at.dp] = gu_ref[...]
-    wd_ref[at.dp] = wd_src[...]
-    part_ref[...] = part_in[...]
-    greet(at, line=True, all_dp=False, slabs=None)
-    gather = Gather(at, [wgu_ref, wd_ref], s_gather)
+    off = bias_ref[0:1, 0:1]
+    mask_ref[...] = mask_block(off)
+    x.arrive()
+    attn_project(x_ref, wqkv_ref, ga_ref, gqk[2:3], gqk[3:4], cos_ref, sin_ref, q_ref, k_ref, v_ref, p_ref, xn_ref)
+    second.step(1)
+    third.step(1)
+    og.forward()
+    nq = q_ref.shape[1] // HD
+    for half in range(2):
+
+        @pl.loop(half * nq // 2, (half + 1) * nq // 2)
+        def _(h):
+            attn_head(h, off, q_ref, k_ref, v_ref, att_ref, mask_ref)
+
+        if half == 0:
+            for t in range(2, at.line):
+                second.step(t)
+    second.arrive()
+
+    @pl.loop(0, 4)
+    def _(i):
+        part_ref[i] = dot(att_ref[lanes(i, tok), :], rows_of(wo_ref)).astype(BF)
+
     red = CtxReduce(at, part_ref, got, s_red)
     red.start()
-    gather.start()
     red.across()
-    gather.step(1)
-    middle = x_ref[...].astype(F32) + red.result()
+    third.step(2)
+    middle = x_own[...].astype(F32) + red.result()
     mid_ref[...] = middle
     r = lax.rsqrt(jnp.mean(middle * middle, axis=-1, keepdims=True) + EPS)
     nm_ref[at.ctx] = (middle * r * gm_ref[0:1, :]).astype(BF)
     nm = CtxGather(at, nm_ref, s_nm)
     nm.start()
-    for t in range(2, at.line):
-        gather.step(t)
-        if t == 2:
-            nm.forward()
-    gather.finish()
-    nm.finish()
-    red.finish()
+    for t in range(3, at.line):
+        third.step(t)
+    nm.forward()
+    nm.arrive()
+    og.arrive()
+    third.arrive()
+    for part in (first, second, third, og, x, nm, red):
+        part.finish()
 
 
 def norm_back(c, v, gain):
@@ -660,74 +665,94 @@
     return jnp.sum(c * nv, axis=0, keepdims=True), r * (cg - nv * jnp.mean(cg * nv, axis=-1, keepdims=True))
 
 
-def back_body(
-    n,
-    dnm_in, outp_in, mid_ref, gm_ref, og_ref, gwgu_in, gwd_in,
-    db_ref, dmid_ref, out_ref, ggm_ref, gu_ref, gd_ref,
-    dnm_part, out_part, gwgu, gwd, got_d, got_o, yi0, yi1, ln0, ln1,
-    s_red, s_dnm, s_out, s_db,
+def into(ref):
+    def store(v):
+        ref[...] = v.astype(ref.dtype)
+
+    return store
+
+
+def backward_body(
+    n, cap,
+    dnm_part, out_part, mid_ref, x_ref, og_ref, ga_ref, gm_ref, gqk_ref, gwgu, gwd, wo_ref, wqkv_ref,
+    q_ref, k_ref, v_ref, p_ref, xn_ref, att_ref, pick_ref, place_ref, cos_ref, sin_ref, bias_ref,
+    ig_ref, layer_ref, qkv_out, o_out, gu_out, gd_out, gain_out,
+    got_d, got_o, got_x, db_ref, dmid_ref, mask_ref, da_ref, dq_ref, dk_ref, dv_ref, dp_ref, ggq_ref, ggk_ref, ggm_ref,
+    gwqkv, gwo, gains, sendb, recv,
+    yi0, yi1, ln0, ln1, s_ra, yo, lo, s_rb, yq, yg, lq, lg, s_rc,
+    gu_sum, gd_sum, qkv_sum, o_sum, gain_sum, gain_all,
+    s_dnm, s_out, s_db, s_dxn, s_rows, s_gu, s_gd, s_qkv, s_o, s_gain,
 ):
     at = Place(n)
-    dnm_part[...] = dnm_in[...]
-    out_part[...] = outp_in[...]
-    gwgu[...] = gwgu_in[...]
-    gwd[...] = gwd_in[...]
-    greet(at, line=True, all_dp=False, slabs=None)
+    greet(at, line=True, all_dp=True, slabs=at.slab_to)
     dnm = CtxReduce(at, dnm_part, got_d, s_dnm)
     dnm.start()
-    grads = Reduce(at, [gwgu, gwd], [yi0, yi1], [ln0, ln1], s_red)
-    grads.start([0, 1])
+    first = Reduce(at, [gwgu, gwd], [yi0, yi1], [ln0, ln1], s_ra)
+    first.start([0, 1])
     dnm.across()
     out = CtxReduce(at, out_part, got_o, s_out)
-    out.start()
-    grads.step(at.line - 1, [0, 1])
+    off = bias_ref[0:1, 0:1]
+    mask_ref[...] = mask_block(off)
+    dk_ref[...] = jnp.zeros_like(dk_ref)
+    dv_ref[...] = jnp.zeros_like(dv_ref)
+    first.step(at.line - 1, [0, 1])
     gg, d = norm_back(dnm.result(), mid_ref[...], gm_ref[0:1, :])
-    ggm_ref[...] = jnp.broadcast_to(gg, ggm_ref.shape)
+    ggm_ref[...] = gg
     d = d + og_ref[...].astype(F32)
     dmid_ref[...] = d
     db_ref[at.ctx] = d.astype(BF)
     db = CtxGather(at, db_ref, s_db)
     db.start()
+    out.start()
+    for t in range(at.line - 2, 1, -1):
+        first.step(t, [0, 1])
+    db.forward()
     out.across()
-    for t in range(at.line - 2, 0, -1):
-        grads.step(t, [0, 1])
-        if t == 1:
-            db.forward()
-    out_ref[...] = (mid_ref[...] + out.result()).astype(BF)
-
-    def to_gu(v):
-        gu_ref[...] = v.astype(BF)
-
-    def to_gd(v):
-        gd_ref[...] = v.astype(BF)
-
-    grads.result(0, to_gu)
-    grads.result(1, to_gd)
-    for part in (grads, db, out, dnm):
-        part.finish()
-
-
-def finish_body(
-    n, cap,
-    dxn_in, dmid_ref, x_ref, ga_ref, pick_ref, place_ref, gwqkv_in, gwo_in, gu_in, gd_in, ggm_ref, ggq_ref, ggk_ref,
-    ig_ref, qkv_out, o_out, gu_out, gd_out, gain_out,
-    dxn_part, gwqkv, gwo, gains, got, sendb, recv, yi0, yi1, yi2, ln0, ln1, ln2, qkv_sum, o_sum, gain_sum, gain_all,
-    s_red, s_dxn, s_rows, s_gu, s_gd, s_qkv, s_o, s_gain,
-):
-    at = Place(n)
-    dxn_part[...] = dxn_in[...]
-    gwqkv[...] = gwqkv_in[...]
-    gwo[...] = gwo_in[...]
-    greet(at, line=True, all_dp=True, slabs=at.slab_to)
-    dxn = CtxReduce(at, dxn_part, got, s_dxn)
+    db.arrive()
+    tok = db_ref.shape[1]
+
+    @pl.loop(0, 4)
+    def _(i):
+        da_ref[lanes(i, tok), :] = dot_nt(db_ref[i], rows_of(wo_ref)).astype(BF)
+
+    weight_grad(gwo, att_ref, db_ref)
+    first.step(1, [0, 1])
+    second = Reduce(at, [gwo], [yo], [lo], s_rb)
+    second.start([0])
+    nq = q_ref.shape[1] // HD
+    for quarter in range(4):
+
+        @pl.loop(quarter * nq // 4, (quarter + 1) * nq // 4)
+        def _(h):
+            attn_head_back(h, off, q_ref, k_ref, v_ref, att_ref, da_ref, dq_ref, dk_ref, dv_ref, mask_ref)
+
+        if quarter == 0:
+            first.result(0, into(gu_sum))
+            first.result(1, into(gd_sum))
+            gu = Quarters(at, gu_sum, gu_out, s_gu)
+            gd = Slab(at, gd_sum, gd_out, s_gd, at.slab_from)
+            gu.start()
+            gd.start()
+            second.step(at.line - 1, [0])
+        if quarter == 1:
+            for t in range(at.line - 2, 1, -1):
+                second.step(t, [0])
+            layer_ref[...] = (mid_ref[...] + out.result()).astype(BF)
+        if quarter == 2:
+            second.step(1, [0])
+    second.result(0, into(o_sum))
+    o = Slab(at, o_sum, o_out, s_o, at.slab_from)
+    o.start()
+    db.finish()
+    dxn_ref = db_ref
+    attn_unproject(gqk_ref[2:3, :], gqk_ref[3:4, :], cos_ref, sin_ref, p_ref, dq_ref, dk_ref, dv_ref, dp_ref, wqkv_ref, dxn_ref, ggq_ref, ggk_ref)
+    dxn = CtxReduce(at, dxn_ref, got_x, s_dxn)
     dxn.start()
-    grads = Reduce(at, [gwqkv, gwo, gains], [yi0, yi1, yi2], [ln0, ln1, ln2], s_red)
-    grads.start([0, 1])
+    weight_grad(gwqkv, xn_ref, dp_ref)
+    third = Reduce(at, [gwqkv, gains], [yq, yg], [lq, lg], s_rc)
+    third.start([0])
     dxn.across()
-    gu = Quarters(at, gu_in, gu_out, s_gu)
-    gd = Slab(at, gd_in, gd_out, s_gd, at.slab_from)
-    gu.start()
-    gd.start()
+    third.step(at.line - 1, [0])
     gg, d = norm_back(dxn.result(), x_ref[...].astype(F32), ga_ref[0:1, :])
     owned = (dmid_ref[...] + d).astype(BF)
     sendb[...] = dot_tn(pick_ref[...], owned).astype(BF)
@@ -741,23 +766,14 @@
             jnp.where(lines == 0, gg[:, tile], 0.0) + jnp.where(lines == 1, ggm_ref[0:1, tile], 0.0)
             + jnp.where(lines == 2, ggq_ref[0:1, :], 0.0) + jnp.where(lines == 3, ggk_ref[0:1, :], 0.0)
         )
-    grads.start([2])
-    for t in range(at.line - 1, 0, -1):
-        grads.step(t, [0, 1, 2])
-
-    def to(ref):
-        def store(v):
-            ref[...] = v.astype(ref.dtype)
-
-        return store
-
-    grads.result(0, to(qkv_sum))
+    third.start([1])
+    third.step(at.line - 1, [1])
+    for t in range(at.line - 2, 0, -1):
+        third.step(t, [0, 1])
+    third.result(0, into(qkv_sum))
     qkv = Quarters(at, qkv_sum, qkv_out, s_qkv)
     qkv.start()
-    grads.result(1, to(o_sum))
-    o = Slab(at, o_sum, o_out, s_o, at.slab_from)
-    o.start()
-    grads.result(2, to(gain_sum))
+    third.result(1, into(gain_sum))
     small = [
         rcopy(gain_sum, gain_all.at[at.ctx], s_gain.at[0, k], s_gain.at[1, k], ctx=c)
         for k, c in enumerate((at.c_x, at.c_far, at.c_core))
@@ -770,22 +786,12 @@
     for g in small:
         g.wait()
     gain_out[...] = gain_all[0] + gain_all[1] + gain_all[2] + gain_all[3]
-    for part in (qkv, o, gu, gd, dxn, grads):
+    for part in (qkv, o, gu, gd, dxn, out, dnm, first, second, third):
         part.finish()
 
 
 def shape(*dims, dtype=BF):
     return jax.ShapeDtypeStruct(dims, dtype)
-
-
-def in_vmem(body, outs, scratch, name):
-    return pl.pallas_call(
-        body,
-        out_shape=outs,
-        scratch_shapes=scratch,
-        compiler_params=pltpu.CompilerParams(vmem_limit_bytes=VMEM_LIMIT),
-        name=name,
-    )
 
 
 def linked(body, outs, scratch, name, number):
@@ -841,76 +847,55 @@
     gain_block = jnp.pad(gain_block, ((0, 4), (0, 0)))
     qkv = jnp.concatenate([to_quarters(w_query), to_quarters(w_key), to_quarters(w_value)], axis=2)
     gu = jnp.concatenate([to_quarters(w_gate), to_quarters(w_up)], axis=2)
-    nb = 4 * rq
     fw = 2 * ff
-    wqkv, wo, gu, wd, x_all, og_all, pick, ga, gm, gqk = linked(
-        functools.partial(fetch_body, n, cap),
-        (shape(n, 4, rq, width), shape(n, ro, width), shape(4, rq, fw), shape(rd, width), shape(4, tok, width),
-         shape(4, tok, width), shape(tok, slabs), shape(8, width, dtype=F32), shape(8, width, dtype=F32), shape(8, 128, dtype=F32)),
-        [pltpu.VMEM((slabs, width), BF), pltpu.VMEM((n * 8, 128), jnp.int32), pltpu.VMEM((4, 8, 128), F32), pltpu.VMEM((n, 8, 128), F32),
-         Gather.scratch(n, 3), sem_pairs(n), sem_pairs(n), sem_pairs(3), sem_pairs(3), sem_pairs(1), sem_pairs(1), sem_pairs(3), sem_pairs(3), sem_pairs(3)],
-        "fetch", 0,
-    )(outgoing, labels, qkv, w_out, gu, w_down, gain_block, out_grad)
-    wqkv, wo = wqkv.reshape(width, 1024), wo.reshape(512, width)
-    ga, gm, gq, gk = ga[0:1], gm[0:1], gqk[2:3], gqk[3:4]
-    og_all = og_all.reshape(rows, width)
-    x_own = lax.dynamic_index_in_dim(x_all, lax.axis_index("ctx"), 0, keepdims=False)
     cos, sin = rope_tables(rows)
     bias = jnp.where(doc_len[0, 0] > 0, 0.0, MASKED).astype(F32).reshape(1, 1) + jnp.zeros((8, 128), F32)
-    part, q, k, v, p, xn, att = in_vmem(
-        attn_fwd_body,
-        (shape(rows, width), shape(rows, 512), shape(rows, 256), shape(rows, 256),
-         shape(rows, 768, dtype=F32), shape(rows, width), shape(rows, 512)),
-        [pltpu.VMEM((QB, QB), F32)],
-        "attn_fwd",
-    )(x_all.reshape(rows, width), wqkv, wo, ga, gq, gk, cos, sin, bias)
-    wgu, wd, nm, middle = linked(
-        functools.partial(middle_body, n),
-        (shape(n, 4, rq, fw), shape(n, rd, width), shape(4, tok, width), shape(tok, width, dtype=F32)),
-        [pltpu.VMEM((4, tok, width), BF), pltpu.VMEM((3, tok, width), BF), Gather.scratch(n, 2), sem_pairs(3), sem_pairs(3)],
-        "middle", 1,
-    )(part.reshape(4, tok, width), x_own, gm, gu, wd)
+    (wqkv, wo, wgu, wd, x_own, og_all, pick, ga, gm, gqk, q, k, v, p, xn, att, nm, middle) = linked(
+        functools.partial(forward_body, n, cap),
+        (shape(n, 4, rq, width), shape(n, ro, width), shape(n, 4, rq, fw), shape(n, rd, width), shape(tok, width), shape(4, tok, width),
+         shape(tok, slabs), shape(8, width, dtype=F32), shape(8, width, dtype=F32), shape(8, 128, dtype=F32),
+         shape(rows, 512), shape(rows, 256), shape(rows, 256), shape(rows, 768, dtype=F32), shape(rows, width), shape(rows, 512),
+         shape(4, tok, width), shape(tok, width, dtype=F32)),
+        [pltpu.VMEM((slabs, width), BF), pltpu.VMEM((n * 8, 128), jnp.int32), pltpu.VMEM((4, 8, 128), F32), pltpu.VMEM((n, 8, 128), F32),
+         pltpu.VMEM((4, tok, width), BF), pltpu.VMEM((4, tok, width), BF), pltpu.VMEM((3, tok, width), BF), pltpu.VMEM((QB, QB), F32),
+         Gather.scratch(n, 2), Gather.scratch(n, 1), Gather.scratch(n, 2), sem_pairs(n), sem_pairs(n), sem_pairs(3), sem_pairs(3),
+         sem_pairs(1), sem_pairs(1), sem_pairs(3), sem_pairs(3), sem_pairs(3), sem_pairs(3), sem_pairs(3)],
+        "forward", 0,
+    )(outgoing, labels, qkv, w_out, gu, w_down, gain_block, out_grad, cos, sin, bias)
+    og_rows = og_all.reshape(rows, width)
     nm = nm.reshape(rows, width)
-    wgu, wd = wgu.reshape(width, fw), wd.reshape(fw // 2, width)
-    wg, wu = wgu[:, : fw // 2], wgu[:, fw // 2 :]
+    wgu, wd = wgu.reshape(width, fw), wd.reshape(ff, width)
+    wg, wu = wgu[:, :ff], wgu[:, ff:]
     gate, up = dot(nm, wg), dot(nm, wu)
     s = jax.nn.sigmoid(gate)
     silu = gate * s
     hidden = (silu * up).astype(BF)
     out_part = dot(hidden, wd).astype(BF)
-    dh = dot_nt(og_all, wd)
+    dh = dot_nt(og_rows, wd)
     d_gate = (dh * up * s * (1.0 + gate * (1.0 - s))).astype(BF)
     d_up = (dh * silu).astype(BF)
-    gwd = dot_tn(hidden, og_all).astype(BF)
+    gwd = dot_tn(hidden, og_rows).astype(BF)
     gwgu = jnp.concatenate([dot_tn(nm, d_gate), dot_tn(nm, d_up)], axis=1).astype(BF)
     dnm_part = (dot_nt(d_gate, wg) + dot_nt(d_up, wu)).astype(BF)
-    red, lines, sems = Reduce.scratch(n, [((4, rq, fw), BF), ((rd, width), BF)])
-    db, d_middle, layer_output, ggm, gu, gd = linked(
-        functools.partial(back_body, n),
-        (shape(4, tok, width), shape(tok, width, dtype=F32), shape(tok, width), shape(8, width, dtype=F32), shape(4, rq, fw), shape(rd, width)),
-        [pltpu.VMEM((4, tok, width), BF), pltpu.VMEM((4, tok, width), BF), pltpu.VMEM((n, 4, rq, fw), BF), pltpu.VMEM((n, rd, width), BF),
-         pltpu.VMEM((3, tok, width), BF), pltpu.VMEM((3, tok, width), BF), *red, *lines, sems, sem_pairs(3), sem_pairs(3), sem_pairs(3)],
-        "back", 2,
-    )(dnm_part.reshape(4, tok, width), out_part.reshape(4, tok, width), middle, gm, out_grad,
-      gwgu.reshape(n, 4, rq, fw), gwd.reshape(n, rd, width))
-    gwqkv, gwo, dxn_part, ggq, ggk = in_vmem(
-        attn_bwd_body,
-        (shape(width, 1024), shape(512, width), shape(rows, width), shape(8, HD, dtype=F32), shape(8, HD, dtype=F32)),
-        [pltpu.VMEM((QB, QB), F32), pltpu.VMEM((rows, 512), BF), pltpu.VMEM((rows, 512), F32),
-         pltpu.VMEM((rows, 256), F32), pltpu.VMEM((rows, 256), F32), pltpu.VMEM((rows, 1024), BF)],
-        "attn_bwd",
-    )(db.reshape(rows, width), wo, wqkv, q, k, v, p, xn, att, gq, gk, cos, sin, bias)
-    red, lines, sems = Reduce.scratch(n, [((4, rq, 1024), BF), ((ro, width), BF), ((8, 128), F32)])
-    input_grad, g_qkv, g_o, g_gu, g_d, small = linked(
-        functools.partial(finish_body, n, cap),
-        (shape(tok, width), shape(4, rq, 1024), shape(ro, width), shape(4, rq, fw), shape(rd, width), shape(8, 128, dtype=F32)),
-        [pltpu.VMEM((4, tok, width), BF), pltpu.VMEM((n, 4, rq, 1024), BF), pltpu.VMEM((n, ro, width), BF), pltpu.VMEM((n, 8, 128), F32),
-         pltpu.VMEM((3, tok, width), BF), pltpu.VMEM((slabs, width), BF), pltpu.VMEM((slabs, width), BF), *red, *lines,
-         pltpu.VMEM((4, rq, 1024), BF), pltpu.VMEM((ro, width), BF), pltpu.VMEM((8, 128), F32), pltpu.VMEM((4, 8, 128), F32),
-         sems, sem_pairs(3), sem_pairs(n), sem_pairs(3), sem_pairs(1), sem_pairs(3), sem_pairs(1), sem_pairs(3)],
-        "finish", 3,
-    )(dxn_part.reshape(4, tok, width), d_middle, x_own, ga, pick, place, gwqkv.reshape(n, 4, rq, 1024), gwo.reshape(n, ro, width),
-      gu, gd, ggm, ggq, ggk)
+    blocks = ([((4, rq, fw), BF), ((rd, width), BF)], [((ro, width), BF)], [((4, rq, 1024), BF), ((8, 128), F32)])
+    reduces = []
+    for red, lines, sems in (Reduce.scratch(n, b) for b in blocks):
+        reduces += [*red, *lines, sems]
+    input_grad, layer_output, g_qkv, g_o, g_gu, g_d, small = linked(
+        functools.partial(backward_body, n, cap),
+        (shape(tok, width), shape(tok, width), shape(4, rq, 1024), shape(ro, width), shape(4, rq, fw), shape(rd, width), shape(8, 128, dtype=F32)),
+        [pltpu.VMEM((3, tok, width), BF), pltpu.VMEM((3, tok, width), BF), pltpu.VMEM((3, tok, width), BF), pltpu.VMEM((4, tok, width), BF),
+         pltpu.VMEM((tok, width), F32), pltpu.VMEM((QB, QB), F32), pltpu.VMEM((rows, 512), BF), pltpu.VMEM((rows, 512), F32),
+         pltpu.VMEM((rows, 256), F32), pltpu.VMEM((rows, 256), F32), pltpu.VMEM((rows, 1024), BF),
+         pltpu.VMEM((8, HD), F32), pltpu.VMEM((8, HD), F32), pltpu.VMEM((1, width), F32),
+         pltpu.VMEM((n, 4, rq, 1024), BF), pltpu.VMEM((n, ro, width), BF), pltpu.VMEM((n, 8, 128), F32),
+         pltpu.VMEM((slabs, width), BF), pltpu.VMEM((slabs, width), BF), *reduces,
+         pltpu.VMEM((4, rq, fw), BF), pltpu.VMEM((rd, width), BF), pltpu.VMEM((4, rq, 1024), BF), pltpu.VMEM((ro, width), BF),
+         pltpu.VMEM((8, 128), F32), pltpu.VMEM((4, 8, 128), F32),
+         sem_pairs(3), sem_pairs(3), sem_pairs(3), sem_pairs(3), sem_pairs(n), sem_pairs(3), sem_pairs(1), sem_pairs(3), sem_pairs(1), sem_pairs(3)],
+        "backward", 1,
+    )(dnm_part.reshape(4, tok, width), out_part.reshape(4, tok, width), middle, x_own, out_grad, ga, gm, gqk,
+      gwgu.reshape(n, 4, rq, fw), gwd.reshape(n, rd, width), wo, wqkv, q, k, v, p, xn, att, pick, place, cos, sin, bias)
 
     def own_lanes(row, count):
         return lax.dynamic_slice(small[row], ((index * count) % 128,), (count,))
@@ -927,8 +912,8 @@
         own_lanes(3, g_heads),
         g_o.astype(F32),
         own_lanes(1, g_rows),
-        from_quarters(g_gu[:, :, : fw // 2]),
-        from_quarters(g_gu[:, :, fw // 2 :]),
+        from_quarters(g_gu[:, :, :ff]),
+        from_quarters(g_gu[:, :, ff:]),
         g_d.astype(F32),
     )
 

time: 420 us -> 363 us (0.86)
  Pallas kernels: 350 us -> 303 us
  local copies, waits for them, and re-layouts: 20.5 us -> 14.6 us
    pallas_call x6 -> x2, Pallas kernels: 350 us -> 303 us  [the longest x1 154 us: local(): linked(functools.partial(forward_body, n, cap), (shape(n, 4, rq, width),...]
where the time goes in v3:
time: 363 us; the launch traced here: 359 us
  Pallas kernels  303 us (83%)
  matrix products  29.5 us (8%)
  local copies, waits for them, and re-layouts  14.6 us (4%)
  other arithmetic  11.1 us (3%)
    pallas_call x1, Pallas kernels, local(): linked(functools.partial(forward_body, n, cap), (shape(n, 4, rq, width),...  154 us
    pallas_call x1, Pallas kernels, local(): linked(functools.partial(backward_body, n, cap), (shape(tok, width), shap...  149 us
    dot_general x4, matrix products, dot_tn(): lax.dot_general(a, b, (((0,), (0,)), ((), ())), preferred_element_type=F32)  10.4 us
    dot_general x4, matrix products, dot(): lax.dot_general(a, b, (((1,), (0,)), ((), ())), preferred_element_type=F32)  10.1 us
    dot_general x3, matrix products, dot_nt(): lax.dot_general(a, b, (((1,), (1,)), ((), ())), preferred_element_type=F32)  9.05 us

profile of v3, /device:TPU:3, one launch (start us, length us, event | category | flops | bytes accessed | tf_op | source)
XLA Modules:
  0.0 359.3 jit_solution(7790262770517972379)
XLA Ops:
  0.6 0.0 copy-start
  0.7 0.0 copy-start.10
  0.7 0.0 copy-start.9
  0.7 0.0 copy-start.8
  0.7 0.7 bitcast_convert_fusion.3
  1.4 0.2 dynamic_update_slice.16
  1.6 0.7 bitcast_convert_fusion.2
  2.3 0.2 dynamic_update_slice.17
  2.5 0.7 bitcast_convert_fusion.1
  3.2 0.2 dynamic_update_slice.18
  3.3 0.7 bitcast_convert_fusion
  4.0 0.2 dynamic_update_slice.19
  4.2 0.6 select_maximum_fusion.gain_ref
  4.8 0.7 fusion.15
  5.5 0.2 fusion.10
  5.7 0.1 select_reduce_fusion
  5.9 0.1 add.78
  6.0 0.6 broadcast_bitcast_fusion.lab_ref
  6.6 0.0 copy-done
  6.6 1.6 convolution_convert_fusion.4.out_ref
  8.2 1.0 bitcast_bitcast_fusion
  9.2 0.8 pad_maximum_fusion.1.gu_ref
  10.0 0.0 copy-done.10
  10.0 0.0 copy-done.9
  10.0 0.0 copy-done.8
  10.1 0.7 pad_maximum_fusion.2.qkv_ref
  10.8 0.6 add.84.bias_ref
  11.4 153.5 %forward.1 = (bf16[8,4,32,1024]{3,2,1,0:T(8,128)(2,1)}, bf16[8,64,1024]{2,1,0:T(8,128)(2,1)}, bf16[8,4,32,1536]{3,2,1,0:T(8,128)(2,1)}, bf16[8,96,1024]{2,1,0:T(...) custom-call(bf16[512,1024]{1,0:T(8,128)(2,1)} %convolution_convert_f, ...), custom_call_target="tpu_custom_call" | custom-call | tf_op jit(solution)/shard_map/forward/pallas_call | solution.py:853
  165.0 4.0 %fusion.21 = f32[1024,768]{1,0:T(8,128)S(1)} fusion(bf16[1024,1024]{1,0:T(8,128)(2,1)} %bitcast.129, bf16[768,1024]{1,0:T(8,128)(2,1)} %bitcast.131), kind=kOutput, calls=%fused_computation.71 | convolution fusion | flops 1610612736 | bytes 6815744 | tf_op jit(solution)/shard_map/dot_general | solution.py:32
  169.0 1.8 fusion.5
  170.8 5.0 %multiply_convert_fusion = (bf16[1024,768]{1,0:T(8,128)(2,1)S(1)}, bf16[1024,768]{1,0:T(8,128)(2,1)}, bf16[1024,768]{1,0:T(8,128)(2,1)}) fusion(f32[1024,768]{1,0:T(8,128)S(1)} %fusion.5, f32[1024,768]{1,0:T(8,128)S(1)} %fusion.21, bf16[1024,1024]{1,0:T(8,128)(2,1)S(1)} %bitcast.107, bf16[1024,1536]{1,0:T(8,128)(2,1)S(1)} %bitcast.126), kind=kOutput, calls=%fused_computation.2 | convolution fusion | flops 1622409216 | bytes 14680064 | tf_op jit(solution)/shard_map/dot_general | solution.py:28
  175.9 3.0 convolution_convert_fusion.1
  178.9 0.0 copy-done.19
  178.9 2.8 copy.36
  181.7 0.0 copy-start.2
  181.7 0.0 copy-start.17
  181.7 4.0 %convolution_convert_fusion.3 = bf16[8,4,32,768]{3,2,1,0:T(8,128)(2,1)S(1)} fusion(bf16[8,4,32,1024]{3,2,1,0:T(8,128)(2,1)} %bitcast.109, bf16[1024,768]{1,0:T(8,128)(2,1)} %get-tuple-element.64), kind=kOutput, calls=%fused_computation.10 | convolution fusion | flops 1611399168 | bytes 5242880 | tf_op jit(solution)/shard_map/dot_general | solution.py:36
  185.7 1.8 convolution_convert_fusion.2
  187.5 2.0 pad_maximum_fusion.gwgu
  189.5 1.0 copy-done.20
  190.5 3.1 convolution_convert_fusion
  193.6 1.8 fusion.3
  195.4 3.2 add_convert_fusion
  198.7 0.8 fusion.11.place_ref
  199.5 149.3 %backward.1 = (bf16[256,1024]{1,0:T(8,128)(2,1)}, bf16[256,1024]{1,0:T(8,128)(2,1)}, bf16[4,32,1024]{2,1,0:T(8,128)(2,1)}, bf16[64,1024]{1,0:T(8,128)(2,1)}, bf1...) custom-call(bf16[4,256,1024]{2,1,0:T(8,128)(2,1)} %bitcast.112, ...), custom_call_target="tpu_custom_call" | custom-call | tf_op jit(solution)/shard_map/backward/pallas_call | solution.py:884
  348.8 1.1 convert_element_type.67
  349.9 0.1 slice_bitcast_fusion
  350.0 0.0 copy-start.11
  350.0 0.0 copy-start.6
  350.0 0.8 copy.52
  350.8 0.8 copy.53
  351.5 0.0 copy-done.5
  351.6 0.7 copy.49
  352.4 0.7 copy.50
  353.0 0.7 copy.51
  353.7 0.6 fusion.16
  354.3 0.6 fusion.17
  354.9 0.6 fusion.18
  355.5 0.6 fusion.19
  356.0 0.8 convert_element_type.68
  356.8 0.0 copy-done.7
  356.8 0.7 convert_element_type.66
  357.5 0.8 copy.66
  358.3 0.8 copy.67
  (39 shorter events, 0.2 us)
Async XLA Ops:
  0.6 5.9 %copy-start = (bf16[256,1024]{1,0:T(8,128)(2,1)S(1)}, bf16[256,1024]{1,0:T(8,128)(2,1)}, u32[]{:S(2)}) copy-start(bf16[256,1024]{1,0:T(8,128)(2,1)} %param.17) | copy-start | bytes 1572868
  0.7 9.4 %copy-start.10 = (bf16[32,1024]{1,0:T(8,128)(2,1)S(1)}, bf16[32,1024]{1,0:T(8,128)(2,1)}, u32[]{:S(2)}) copy-start(bf16[32,1024]{1,0:T(8,128)(2,1)} %param.23) | copy-start | bytes 196612
  0.7 9.3 %copy-start.9 = (bf16[32,1024]{1,0:T(8,128)(2,1)S(1)}, bf16[32,1024]{1,0:T(8,128)(2,1)}, u32[]{:S(2)}) copy-start(bf16[32,1024]{1,0:T(8,128)(2,1)} %param.24) | copy-start | bytes 196612
  0.7 9.4 %copy-start.8 = (bf16[32,2048]{1,0:T(8,128)(2,1)S(1)}, bf16[32,2048]{1,0:T(8,128)(2,1)}, u32[]{:S(2)}) copy-start(bf16[32,2048]{1,0:T(8,128)(2,1)} %param.22) | copy-start | bytes 393220
  6.6 4.2 %copy-start.16 = (s32[1,2]{1,0:T(1,128)S(1)}, s32[1,2]{1,0:T(1,128)}, u32[]{:S(2)}) copy-start(s32[1,2]{1,0:T(1,128)} %param.19) | copy-start | bytes 28
  165.0 4.0 %copy-start.1 = (bf16[4,256,1024]{2,1,0:T(8,128)(2,1)S(1)}, bf16[4,256,1024]{2,1,0:T(8,128)(2,1)}, u32[]{:S(2)}) copy-start(bf16[4,256,1024]{2,1,0:T(8,128)(2,1)} %get-tuple-element.40) | copy-start | bytes 6291460
  165.0 4.0 %copy-start.12 = (bf16[8,4,32,1536]{3,2,1,0:T(8,128)(2,1)S(1)}, bf16[8,4,32,1536]{3,2,1,0:T(8,128)(2,1)}, u32[]{:S(2)}) copy-start(bf16[8,4,32,1536]{3,2,1,0:T(8,128)(2,1)} %get-tuple-element.41) | copy-start | bytes 9437188
  170.8 5.0 %copy-start.14 = (bf16[4,256,1024]{2,1,0:T(8,128)(2,1)S(1)}, bf16[4,256,1024]{2,1,0:T(8,128)(2,1)}, u32[]{:S(2)}) copy-start(bf16[4,256,1024]{2,1,0:T(8,128)(2,1)} %get-tuple-element.38) | copy-start | bytes 6291460
  175.9 3.0 copy-start.19
  181.7 4.0 %copy-start.2 = (bf16[1024,1024]{1,0:T(8,128)(2,1)S(1)}, bf16[1024,1024]{1,0:T(8,128)(2,1)}, u32[]{:S(2)}) copy-start(bf16[1024,1024]{1,0:T(8,128)(2,1)} %copy.36) | copy-start | bytes 6291460
  181.7 4.0 %copy-start.17 = (bf16[1024,768]{1,0:T(8,128)(2,1)S(1)}, bf16[1024,768]{1,0:T(8,128)(2,1)}, u32[]{:S(2)}) copy-start(bf16[1024,768]{1,0:T(8,128)(2,1)} %get-tuple-element.65) | copy-start | bytes 4718596
  187.5 2.0 copy-start.15
  187.5 3.0 copy-start.20
  190.5 3.1 copy-start.13
  190.5 3.1 copy-start.18
  348.8 2.8 copy-start.5
  350.0 3.7 %copy-start.11 = (f32[8,128]{1,0:T(8,128)S(1)}, f32[8,128]{1,0:T(8,128)}, u32[]{:S(2)}) copy-start(f32[8,128]{1,0:T(8,128)} %get-tuple-element.58) | copy-start | bytes 12292
  350.0 6.1 %copy-start.6 = (bf16[96,1024]{1,0:T(8,128)(2,1)S(1)}, bf16[96,1024]{1,0:T(8,128)(2,1)}, u32[]{:S(2)}) copy-start(bf16[96,1024]{1,0:T(8,128)(2,1)} %get-tuple-element.62) | copy-start | bytes 589828
  350.8 6.1 %copy-start.7 = (bf16[64,1024]{1,0:T(8,128)(2,1)S(1)}, bf16[64,1024]{1,0:T(8,128)(2,1)}, u32[]{:S(2)}) copy-start(bf16[64,1024]{1,0:T(8,128)(2,1)} %get-tuple-element.60) | copy-start | bytes 393220
  351.5 6.0 %copy-start.4 = (bf16[256,1024]{1,0:T(8,128)(2,1)S(1)}, bf16[256,1024]{1,0:T(8,128)(2,1)}, u32[]{:S(2)}) copy-start(bf16[256,1024]{1,0:T(8,128)(2,1)} %get-tuple-element.93) | copy-start | bytes 1572868
  351.6 6.8 %copy-start.3 = (bf16[256,1024]{1,0:T(8,128)(2,1)S(1)}, bf16[256,1024]{1,0:T(8,128)(2,1)}, u32[]{:S(2)}) copy-start(bf16[256,1024]{1,0:T(8,128)(2,1)} %get-tuple-element.94) | copy-start | bytes 1572868

commit v4 on v3

--- a/solution.py
+++ b/solution.py
@@ -15,13 +15,13 @@
 EPS = 1e-06
 THETA = 1000000.0
 MASKED = -1e30
-QB = 256
+QB = 128
 SCALE = HD ** (-0.5)
 LOG2E = math.log2(math.e)
 BF = jnp.bfloat16
 F32 = jnp.float32
 BOTH = ("dp", "ctx")
-VMEM_LIMIT = 60 << 20
+VMEM_LIMIT = 62 << 20
 
 
 def dot(a, b):
@@ -52,6 +52,12 @@
     rows = lax.broadcasted_iota(jnp.int32, (QB, QB), 0)
     cols = lax.broadcasted_iota(jnp.int32, (QB, QB), 1)
     return jnp.where(rows == cols, 0.0, jnp.where(cols < rows, off_bias, MASKED))
+
+
+def lane_mean(v):
+    ones = jnp.full((HD, HD), 1.0 / HD, BF)
+    high = v.astype(BF)
+    return dot(high, ones) + dot((v - high.astype(F32)).astype(BF), ones)
 
 
 def rows_of(ref):
@@ -73,14 +79,14 @@
         xn = (x * r * ga[0:1, :]).astype(BF)
         xn_ref[here, :] = xn
         p = dot(xn, rows_of(w))
-        p_ref[here, :] = p[:, : (nq + nk) * HD]
+        p_ref[here, :] = p[:, : (nq + nk) * HD].astype(BF)
         v_ref[here, :] = p[:, (nq + nk) * HD :].astype(BF)
         cos = cos_ref[here, :]
         sin = sin_ref[here, :]
         for h in range(nq + nk):
             ph = p[:, h * HD : (h + 1) * HD]
             g = gq if h < nq else gk
-            nv = ph * lax.rsqrt(jnp.mean(ph * ph, axis=-1, keepdims=True) + EPS) * g
+            nv = ph * lax.rsqrt(lane_mean(ph * ph) + EPS) * g
             rot = (nv * cos + pltpu.roll(nv, HD // 2, 1) * sin).astype(BF)
             if h < nq:
                 q_ref[here, h * HD : (h + 1) * HD] = rot
@@ -88,56 +94,42 @@
                 k_ref[here, (h - nq) * HD : (h - nq + 1) * HD] = rot
 
 
-def attn_head(h, off, q_ref, k_ref, v_ref, att_ref, mask_ref):
-    rows = q_ref.shape[0]
+def group_rows(ref, here, g, group):
+    return jnp.concatenate([ref[here, lanes(g * group + a, HD)] for a in range(group)], axis=0)
+
+
+def attn_probs(q, k, off, mask_ref, group):
+    s = dot_nt(q, k) * (SCALE * LOG2E)
+    cut = s.shape[1] - QB
+    last = jnp.exp2(s[:, cut:] + jnp.concatenate([mask_ref[...]] * group, axis=0))
+    e = last if cut == 0 else jnp.concatenate([jnp.exp2(s[:, :cut] + off), last], axis=1)
+    return e * (1.0 / jnp.sum(e, axis=-1, keepdims=True))
+
+
+def attn_group(g, off, q_ref, k_ref, v_ref, att_ref, mask_ref):
     group = q_ref.shape[1] // k_ref.shape[1]
-    hq = lanes(h, HD)
-    hk = lanes(h // group, HD)
-    for i in range(rows // QB):
-        q = q_ref[i * QB : (i + 1) * QB, hq]
-        es, total = [], None
-        for j in range(i + 1):
-            s = dot_nt(q, k_ref[j * QB : (j + 1) * QB, hk]) * (SCALE * LOG2E)
-            e = jnp.exp2(s + (mask_ref[...] if j == i else off))
-            t = jnp.sum(e, axis=-1, keepdims=True)
-            total = t if total is None else total + t
-            es.append(e)
-        inv = 1.0 / total
-        o = None
-        for j in range(i + 1):
-            c = dot((es[j] * inv).astype(BF), v_ref[j * QB : (j + 1) * QB, hk])
-            o = c if o is None else o + c
-        att_ref[i * QB : (i + 1) * QB, hq] = o.astype(BF)
-
-
-def attn_head_back(h, off, q_ref, k_ref, v_ref, att_ref, da_ref, dq_ref, dk_ref, dv_ref, mask_ref):
-    rows = q_ref.shape[0]
+    hk = lanes(g, HD)
+    for i in range(q_ref.shape[0] // QB):
+        here, keys = slice(i * QB, (i + 1) * QB), slice(0, (i + 1) * QB)
+        probs = attn_probs(group_rows(q_ref, here, g, group), k_ref[keys, hk], off, mask_ref, group)
+        o = dot(probs.astype(BF), v_ref[keys, hk]).astype(BF)
+        for a in range(group):
+            att_ref[here, lanes(g * group + a, HD)] = o[a * QB : (a + 1) * QB]
+
+
+def attn_group_back(g, i, off, q_ref, k_ref, v_ref, att_ref, da_ref, dq_ref, dk_ref, dv_ref, mask_ref):
     group = q_ref.shape[1] // k_ref.shape[1]
-    hq = lanes(h, HD)
-    hk = lanes(h // group, HD)
-    for i in range(rows // QB):
-        here = slice(i * QB, (i + 1) * QB)
-        q = q_ref[here, hq]
-        da = da_ref[here, hq]
-        inner = jnp.sum(da.astype(F32) * att_ref[here, hq].astype(F32), axis=-1, keepdims=True)
-        es, total = [], None
-        for j in range(i + 1):
-            s = dot_nt(q, k_ref[j * QB : (j + 1) * QB, hk]) * (SCALE * LOG2E)
-            e = jnp.exp2(s + (mask_ref[...] if j == i else off))
-            t = jnp.sum(e, axis=-1, keepdims=True)
-            total = t if total is None else total + t
-            es.append(e)
-        inv = 1.0 / total
-        dq = None
-        for j in range(i + 1):
-            keys = slice(j * QB, (j + 1) * QB)
-            probs = es[j] * inv
-            ds = (probs * (dot_nt(da, v_ref[keys, hk]) - inner)).astype(BF)
-            c = dot(ds, k_ref[keys, hk])
-            dq = c if dq is None else dq + c
-            dk_ref[keys, hk] += dot_tn(ds, q)
-            dv_ref[keys, hk] += dot_tn(probs.astype(BF), da)
-        dq_ref[here, hq] = dq
+    hk = lanes(g, HD)
+    here, keys = slice(i * QB, (i + 1) * QB), slice(0, (i + 1) * QB)
+    q, da, att = (group_rows(ref, here, g, group) for ref in (q_ref, da_ref, att_ref))
+    inner = jnp.sum(da.astype(F32) * att.astype(F32), axis=-1, keepdims=True)
+    probs = attn_probs(q, k_ref[keys, hk], off, mask_ref, group)
+    ds = (probs * (dot_nt(da, v_ref[keys, hk]) - inner)).astype(BF)
+    dq = dot(ds, k_ref[keys, hk])
+    for a in range(group):
+        dq_ref[here, lanes(g * group + a, HD)] = dq[a * QB : (a + 1) * QB]
+    dk_ref[keys, hk] += dot_tn(ds, q)
+    dv_ref[keys, hk] += dot_tn(probs.astype(BF), da)
 
 
 def attn_unproject(gq, gk, cos_ref, sin_ref, p_ref, dq_ref, dk_ref, dv_ref, dp_ref, w, dxn_ref, ggq_ref, ggk_ref):
@@ -163,25 +155,46 @@
             else:
                 d = dk_ref[here, (h - nq) * HD : (h - nq + 1) * HD] * SCALE
             dn = d * cos + pltpu.roll(d * sin, HD // 2, 1)
-            ph = p_ref[here, cols]
-            r = lax.rsqrt(jnp.mean(ph * ph, axis=-1, keepdims=True) + EPS)
+            ph = p_ref[here, cols].astype(F32)
+            r = lax.rsqrt(lane_mean(ph * ph) + EPS)
             nh = ph * r
-            sums[which] += jnp.sum(dn * nh, axis=0, keepdims=True)
-            cg = dn * g
-            dp_ref[here, cols] = (r * (cg - nh * jnp.mean(cg * nh, axis=-1, keepdims=True))).astype(BF)
+            dnh = dn * nh
+            sums[which] += jnp.sum(dnh, axis=0, keepdims=True)
+            dp_ref[here, cols] = (r * (dn * g - nh * lane_mean(dnh * g))).astype(BF)
         dp_ref[here, (nq + nk) * HD :] = dv_ref[here, :].astype(BF)
         ggq_ref[0:1, :] += sums[0]
         ggk_ref[0:1, :] += sums[1]
         dxn_ref[i] = dot_nt(dp_ref[here, :], rows_of(w)).astype(BF)
 
 
-def weight_grad(out_ref, left_ref, right, chunk=128):
+def feed_forward(nm_ref, og_ref, wgu_ref, wd_ref, hid_ref, dgu_ref, out_ref, dnm_ref):
+    rows = nm_ref.shape[1]
+    ff = hid_ref.shape[1]
+
+    @pl.loop(0, nm_ref.shape[0])
+    def _(i):
+        here = lanes(i, rows)
+        both = dot(nm_ref[i], rows_of(wgu_ref))
+        gate, up = both[:, :ff], both[:, ff:]
+        s = 1.0 / (1.0 + jnp.exp2(gate * -LOG2E))
+        silu = gate * s
+        hidden = (silu * up).astype(BF)
+        hid_ref[here, :] = hidden
+        dh = dot_nt(og_ref[i], rows_of(wd_ref))
+        dgu_ref[here, :ff] = (dh * up * (s * (1.0 + gate * (1.0 - s)))).astype(BF)
+        dgu_ref[here, ff:] = (dh * silu).astype(BF)
+        dnm_ref[i] = dot_nt(dgu_ref[here, :], rows_of(wgu_ref)).astype(BF)
+        out_ref[i] = dot(hidden, rows_of(wd_ref)).astype(BF)
+
+
+def weight_grad(out_ref, left_ref, right, chunk=256):
     size = math.prod(out_ref.shape[1:-1])
     width = out_ref.shape[-1]
 
-    @pl.loop(0, left_ref.shape[1] // chunk)
+    @pl.loop(0, left_ref.shape[-1] // chunk)
     def _(i):
-        g = dot_tn(left_ref[:, lanes(i, chunk)], rows_of(right)).astype(BF)
+        left = left_ref[..., lanes(i, chunk)].reshape(-1, chunk)
+        g = dot_tn(left, rows_of(right)).astype(BF)
         for j in range(chunk // size):
             out_ref[i * (chunk // size) + j] = g[j * size : (j + 1) * size].reshape(out_ref.shape[1:-1] + (width,))
 
@@ -214,7 +227,7 @@
         self.slab_stays = source == mine
 
 
-def greet(place, line, all_dp, slabs):
+def greet(place, slabs):
     barrier = pltpu.get_barrier_semaphore()
 
     def signal(**device):
@@ -222,26 +235,14 @@
 
     for c in (place.c_core, place.c_x, place.c_far):
         signal(ctx=c)
-    count = 3
-    if all_dp:
-        for k in range(1, place.n):
-            signal(dp=(place.dp + k) % place.n)
-        count = count + place.n - 1
-    elif line:
-        signal(dp=place.dp_inner)
-        count = count + 1
-        for there, dp in ((place.has_up, place.dp_up), (place.has_down, place.dp_down)):
-
-            @pl.when(there)
-            def _():
-                signal(dp=dp)
-
-            count = count + jnp.where(there, 1, 0)
-    if slabs is not None:
+    for k in range(1, place.n):
+        signal(dp=(place.dp + k) % place.n)
+    count = place.n + 2
+    for slab in slabs:
 
         @pl.when(jnp.logical_not(place.slab_stays))
         def _():
-            signal(**slabs)
+            signal(**slab)
 
         count = count + jnp.where(place.slab_stays, 0, 1)
     pl.semaphore_wait(barrier, count)
@@ -262,7 +263,7 @@
         recv = self.sems.at[4 if way == 2 else 3, b, p]
         return rcopy(block, block, self.sems.at[way, b, p], recv, dp=device)
 
-    def send(self, p, up, down):
+    def send(self, p, up, down, inner=True):
         at = self.at
         for b in range(len(self.bufs)):
             if up:
@@ -277,10 +278,17 @@
                 def _():
                     self.copy(b, p, 1).start()
 
-            self.copy(b, p, 2).start()
+            if inner:
+                self.copy(b, p, 2).start()
 
     def start(self):
         self.send(self.at.outer, True, True)
+
+    def start_inner(self):
+        self.send(self.at.outer, False, False)
+
+    def start_line(self):
+        self.send(self.at.outer, True, True, False)
 
     def step(self, t):
         at = self.at
@@ -543,65 +551,88 @@
     return pltpu.SemaphoreType.DMA((2, count))
 
 
-def forward_body(
+def norm_back(c, v, gain):
+    r = lax.rsqrt(jnp.mean(v * v, axis=-1, keepdims=True) + EPS)
+    nv = v * r
+    cg = c * gain
+    return jnp.sum(c * nv, axis=0, keepdims=True), r * (cg - nv * jnp.mean(cg * nv, axis=-1, keepdims=True))
+
+
+def into(ref):
+    def store(v):
+        ref[...] = v.astype(ref.dtype)
+
+    return store
+
+
+def layer_body(
     n, cap,
-    out_ref, lab_ref, qkv_ref, wo_src, gu_ref, wd_src, gain_ref, og_ref, cos_ref, sin_ref, bias_ref,
-    wqkv_ref, wo_ref, wgu_ref, wd_ref, x_own, og_all, pick_ref, ga_ref, gm_ref, gqk_ref,
-    q_ref, k_ref, v_ref, p_ref, xn_ref, att_ref, nm_ref, mid_ref,
+    out_ref, lab_ref, qkv_ref, wo_src, gu_ref, wd_src, gain_ref, og_ref, place_ref, cos_ref, sin_ref, bias_ref,
+    ig_ref, layer_ref, qkv_out, o_out, gu_out, gd_out, gain_out,
+    wqkv_ref, wo_ref, wgu_ref, wd_ref, og_all, x_own, pick_ref, ga_ref, gm_ref, q_ref, k_ref, v_ref, p_ref, xn_ref, att_ref, nm_ref, mid_ref,
     recv, labels, gains_c, gains_n, x_ref, part_ref, got, mask_ref,
+    hid_ref, dgu_ref, outp_ref, got_d, got_o, dmid_ref, dq_ref, dk_ref, dv_ref, ggq_ref, ggk_ref, ggm_ref, gains, recv_back,
+    yi0, yi1, ln0, ln1, s_ra, yo, lo, s_rb, yq, yg, lq, lg, s_rc,
+    gain_sum, gain_all,
     s_ga, s_gb, s_gc, s_rows, s_labs, s_qkv, s_gu, s_wo, s_wd, s_gain, s_x, s_og, s_red, s_nm,
+    s_dnm, s_out, s_db, s_dxn, s_rows_back, s_gu_back, s_gd, s_qkv_back, s_o, s_gain_back,
 ):
     at = Place(n)
-    greet(at, line=True, all_dp=True, slabs=at.slab_from)
+    greet(at, (at.slab_from, at.slab_to))
     qkv = Quarters(at, qkv_ref, wqkv_ref.at[at.dp], s_qkv)
     rows = Exchange(at, out_ref, recv, cap, s_rows)
     labs = Exchange(at, lab_ref, labels, 8, s_labs)
     qkv.start()
-    gains = [
+    gain_copies = [
         rcopy(gain_ref, gains_c.at[at.ctx], s_gain.at[0, k], s_gain.at[1, k], ctx=c)
         for k, c in enumerate((at.c_x, at.c_far, at.c_core))
     ]
-    for g in gains:
+    for g in gain_copies:
         g.start()
     gains_c[at.ctx] = gain_ref[...]
+    wo = Slab(at, wo_src, wo_ref.at[at.slab_to["dp"]], s_wo, at.slab_to)
+    wd = Slab(at, wd_src, wd_ref.at[at.slab_to["dp"]], s_wd, at.slab_to)
+    gu = Quarters(at, gu_ref, wgu_ref.at[at.dp], s_gu)
     labs.start()
     rows.start()
-    for g in gains:
+    gu.start()
+    wo.start()
+    wd.start()
+    for g in gain_copies:
         g.wait()
     gains_n[at.dp] = gains_c[0] + gains_c[1] + gains_c[2] + gains_c[3]
     qkv.finish()
     first = Gather(at, [wqkv_ref, gains_n], s_ga)
     first.start()
-    wo = Slab(at, wo_src, wo_ref.at[at.slab_to["dp"]], s_wo, at.slab_to)
-    wd = Slab(at, wd_src, wd_ref.at[at.slab_to["dp"]], s_wd, at.slab_to)
-    gu = Quarters(at, gu_ref, wgu_ref.at[at.dp], s_gu)
-    wo.start()
-    gu.start()
-    wd.start()
     og_all[at.ctx] = og_ref[...]
     og = CtxGather(at, og_all, s_og)
+    gu.finish()
+    og.start()
+    wo.finish()
+    second = Gather(at, [wo_ref], s_gb)
+    second.start()
+    wd.finish()
+    third = Gather(at, [wgu_ref, wd_ref], s_gc)
+    third.start_inner()
     labs.finish()
     tok = x_ref.shape[1]
     slots = lax.broadcasted_iota(jnp.int32, (tok, cap), 0)
     for j in range(n):
         pick_ref[:, j * cap : (j + 1) * cap] = (slots == labels[j * 8 : j * 8 + 1, :cap]).astype(BF)
     first.step(1)
+    second.step(1)
     rows.finish()
     owned = dot(pick_ref[...], recv[...]).astype(BF)
     x_ref[at.ctx] = owned
     x_own[...] = owned
     x = CtxGather(at, x_ref, s_x)
     x.start()
-    og.start()
     for t in range(2, at.line):
         first.step(t)
-    wo.finish()
-    second = Gather(at, [wo_ref], s_gb)
-    second.start()
-    wd.finish()
-    gu.finish()
-    third = Gather(at, [wgu_ref, wd_ref], s_gc)
-    third.start()
+        second.step(t)
+        if t == 2:
+            third.start_line()
+    og.forward()
     x.forward()
     first.arrive()
     own = 4 * ga_ref.shape[1] // (4 * n)
@@ -614,24 +645,18 @@
         ga_ref[0:1, tile] += block[0:1]
         gm_ref[0:1, tile] += block[1:2]
         gqk = gqk + block
-    gqk_ref[...] = gqk
     off = bias_ref[0:1, 0:1]
     mask_ref[...] = mask_block(off)
     x.arrive()
     attn_project(x_ref, wqkv_ref, ga_ref, gqk[2:3], gqk[3:4], cos_ref, sin_ref, q_ref, k_ref, v_ref, p_ref, xn_ref)
-    second.step(1)
     third.step(1)
-    og.forward()
-    nq = q_ref.shape[1] // HD
-    for half in range(2):
-
-        @pl.loop(half * nq // 2, (half + 1) * nq // 2)
-        def _(h):
-            attn_head(h, off, q_ref, k_ref, v_ref, att_ref, mask_ref)
-
-        if half == 0:
-            for t in range(2, at.line):
-                second.step(t)
+    nk = k_ref.shape[1] // HD
+
+    @pl.loop(0, nk)
+    def _(g):
+        attn_group(g, off, q_ref, k_ref, v_ref, att_ref, mask_ref)
+
+    third.step(2)
     second.arrive()
 
     @pl.loop(0, 4)
@@ -641,7 +666,6 @@
     red = CtxReduce(at, part_ref, got, s_red)
     red.start()
     red.across()
-    third.step(2)
     middle = x_own[...].astype(F32) + red.result()
     mid_ref[...] = middle
     r = lax.rsqrt(jnp.mean(middle * middle, axis=-1, keepdims=True) + EPS)
@@ -656,43 +680,17 @@
     third.arrive()
     for part in (first, second, third, og, x, nm, red):
         part.finish()
-
-
-def norm_back(c, v, gain):
-    r = lax.rsqrt(jnp.mean(v * v, axis=-1, keepdims=True) + EPS)
-    nv = v * r
-    cg = c * gain
-    return jnp.sum(c * nv, axis=0, keepdims=True), r * (cg - nv * jnp.mean(cg * nv, axis=-1, keepdims=True))
-
-
-def into(ref):
-    def store(v):
-        ref[...] = v.astype(ref.dtype)
-
-    return store
-
-
-def backward_body(
-    n, cap,
-    dnm_part, out_part, mid_ref, x_ref, og_ref, ga_ref, gm_ref, gqk_ref, gwgu, gwd, wo_ref, wqkv_ref,
-    q_ref, k_ref, v_ref, p_ref, xn_ref, att_ref, pick_ref, place_ref, cos_ref, sin_ref, bias_ref,
-    ig_ref, layer_ref, qkv_out, o_out, gu_out, gd_out, gain_out,
-    got_d, got_o, got_x, db_ref, dmid_ref, mask_ref, da_ref, dq_ref, dk_ref, dv_ref, dp_ref, ggq_ref, ggk_ref, ggm_ref,
-    gwqkv, gwo, gains, sendb, recv,
-    yi0, yi1, ln0, ln1, s_ra, yo, lo, s_rb, yq, yg, lq, lg, s_rc,
-    gu_sum, gd_sum, qkv_sum, o_sum, gain_sum, gain_all,
-    s_dnm, s_out, s_db, s_dxn, s_rows, s_gu, s_gd, s_qkv, s_o, s_gain,
-):
-    at = Place(n)
-    greet(at, line=True, all_dp=True, slabs=at.slab_to)
-    dnm = CtxReduce(at, dnm_part, got_d, s_dnm)
+    feed_forward(nm_ref, og_all, wgu_ref, wd_ref, hid_ref, dgu_ref, outp_ref, part_ref)
+    db_ref, da_ref, dp_ref = x_ref, hid_ref.at[:, : q_ref.shape[1]], dgu_ref.at[:, : wqkv_ref.shape[-1]]
+    dnm = CtxReduce(at, part_ref, got_d, s_dnm)
     dnm.start()
-    first = Reduce(at, [gwgu, gwd], [yi0, yi1], [ln0, ln1], s_ra)
-    first.start([0, 1])
+    weight_grad(wd_ref, hid_ref, og_all, 384)
+    first = Reduce(at, [wgu_ref, wd_ref], [yi0, yi1], [ln0, ln1], s_ra)
+    first.start([1])
     dnm.across()
-    out = CtxReduce(at, out_part, got_o, s_out)
-    off = bias_ref[0:1, 0:1]
-    mask_ref[...] = mask_block(off)
+    weight_grad(wgu_ref, nm_ref, dgu_ref)
+    first.start([0])
+    out = CtxReduce(at, outp_ref, got_o, s_out)
     dk_ref[...] = jnp.zeros_like(dk_ref)
     dv_ref[...] = jnp.zeros_like(dv_ref)
     first.step(at.line - 1, [0, 1])
@@ -715,48 +713,41 @@
     def _(i):
         da_ref[lanes(i, tok), :] = dot_nt(db_ref[i], rows_of(wo_ref)).astype(BF)
 
-    weight_grad(gwo, att_ref, db_ref)
+    weight_grad(wo_ref, att_ref, db_ref)
     first.step(1, [0, 1])
-    second = Reduce(at, [gwo], [yo], [lo], s_rb)
+    second = Reduce(at, [wo_ref], [yo], [lo], s_rb)
     second.start([0])
-    nq = q_ref.shape[1] // HD
-    for quarter in range(4):
-
-        @pl.loop(quarter * nq // 4, (quarter + 1) * nq // 4)
-        def _(h):
-            attn_head_back(h, off, q_ref, k_ref, v_ref, att_ref, da_ref, dq_ref, dk_ref, dv_ref, mask_ref)
-
-        if quarter == 0:
-            first.result(0, into(gu_sum))
-            first.result(1, into(gd_sum))
-            gu = Quarters(at, gu_sum, gu_out, s_gu)
-            gd = Slab(at, gd_sum, gd_out, s_gd, at.slab_from)
+    for g in range(k_ref.shape[1] // HD):
+        for i in range(q_ref.shape[0] // QB):
+            attn_group_back(g, i, off, q_ref, k_ref, v_ref, att_ref, da_ref, dq_ref, dk_ref, dv_ref, mask_ref)
+        if g == 0:
+            first.result(0, into(yi0.at[at.outer]))
+            first.result(1, into(yi1.at[at.outer]))
+            gu = Quarters(at, yi0.at[at.outer], gu_out, s_gu_back)
+            gd = Slab(at, yi1.at[at.outer], gd_out, s_gd, at.slab_from)
             gu.start()
             gd.start()
-            second.step(at.line - 1, [0])
-        if quarter == 1:
-            for t in range(at.line - 2, 1, -1):
+            for t in range(at.line - 1, 1, -1):
                 second.step(t, [0])
-            layer_ref[...] = (mid_ref[...] + out.result()).astype(BF)
-        if quarter == 2:
-            second.step(1, [0])
-    second.result(0, into(o_sum))
-    o = Slab(at, o_sum, o_out, s_o, at.slab_from)
+    second.step(1, [0])
+    layer_ref[...] = (mid_ref[...] + out.result()).astype(BF)
+    second.result(0, into(yo.at[at.outer]))
+    o = Slab(at, yo.at[at.outer], o_out, s_o, at.slab_from)
     o.start()
     db.finish()
-    dxn_ref = db_ref
-    attn_unproject(gqk_ref[2:3, :], gqk_ref[3:4, :], cos_ref, sin_ref, p_ref, dq_ref, dk_ref, dv_ref, dp_ref, wqkv_ref, dxn_ref, ggq_ref, ggk_ref)
-    dxn = CtxReduce(at, dxn_ref, got_x, s_dxn)
+    dxn_ref = nm_ref
+    attn_unproject(gqk[2:3], gqk[3:4], cos_ref, sin_ref, p_ref, dq_ref, dk_ref, dv_ref, dp_ref, wqkv_ref, dxn_ref, ggq_ref, ggk_ref)
+    dxn = CtxReduce(at, dxn_ref, got, s_dxn)
     dxn.start()
-    weight_grad(gwqkv, xn_ref, dp_ref)
-    third = Reduce(at, [gwqkv, gains], [yq, yg], [lq, lg], s_rc)
+    weight_grad(wqkv_ref, xn_ref, dp_ref)
+    third = Reduce(at, [wqkv_ref, gains], [yq, yg], [lq, lg], s_rc)
     third.start([0])
     dxn.across()
     third.step(at.line - 1, [0])
-    gg, d = norm_back(dxn.result(), x_ref[...].astype(F32), ga_ref[0:1, :])
+    gg, d = norm_back(dxn.result(), x_own[...].astype(F32), ga_ref[0:1, :])
     owned = (dmid_ref[...] + d).astype(BF)
-    sendb[...] = dot_tn(pick_ref[...], owned).astype(BF)
-    rows = Exchange(at, sendb, recv, cap, s_rows)
+    recv[...] = dot_tn(pick_ref[...], owned).astype(BF)
+    rows = Exchange(at, recv, recv_back, cap, s_rows_back)
     rows.start()
     own = 4 * gg.shape[1] // (4 * n)
     lines = lax.broadcasted_iota(jnp.int32, (8, 128), 0)
@@ -770,19 +761,19 @@
     third.step(at.line - 1, [1])
     for t in range(at.line - 2, 0, -1):
         third.step(t, [0, 1])
-    third.result(0, into(qkv_sum))
-    qkv = Quarters(at, qkv_sum, qkv_out, s_qkv)
+    third.result(0, into(yq.at[at.outer]))
+    qkv = Quarters(at, yq.at[at.outer], qkv_out, s_qkv_back)
     qkv.start()
     third.result(1, into(gain_sum))
     small = [
-        rcopy(gain_sum, gain_all.at[at.ctx], s_gain.at[0, k], s_gain.at[1, k], ctx=c)
+        rcopy(gain_sum, gain_all.at[at.ctx], s_gain_back.at[0, k], s_gain_back.at[1, k], ctx=c)
         for k, c in enumerate((at.c_x, at.c_far, at.c_core))
     ]
     for g in small:
         g.start()
     gain_all[at.ctx] = gain_sum[...]
     rows.finish()
-    ig_ref[...] = dot(place_ref[...], recv[...]).astype(BF)
+    ig_ref[...] = dot(place_ref[...], recv_back[...]).astype(BF)
     for g in small:
         g.wait()
     gain_out[...] = gain_all[0] + gain_all[1] + gain_all[2] + gain_all[3]
@@ -850,52 +841,30 @@
     fw = 2 * ff
     cos, sin = rope_tables(rows)
     bias = jnp.where(doc_len[0, 0] > 0, 0.0, MASKED).astype(F32).reshape(1, 1) + jnp.zeros((8, 128), F32)
-    (wqkv, wo, wgu, wd, x_own, og_all, pick, ga, gm, gqk, q, k, v, p, xn, att, nm, middle) = linked(
-        functools.partial(forward_body, n, cap),
-        (shape(n, 4, rq, width), shape(n, ro, width), shape(n, 4, rq, fw), shape(n, rd, width), shape(tok, width), shape(4, tok, width),
-         shape(tok, slabs), shape(8, width, dtype=F32), shape(8, width, dtype=F32), shape(8, 128, dtype=F32),
-         shape(rows, 512), shape(rows, 256), shape(rows, 256), shape(rows, 768, dtype=F32), shape(rows, width), shape(rows, 512),
-         shape(4, tok, width), shape(tok, width, dtype=F32)),
-        [pltpu.VMEM((slabs, width), BF), pltpu.VMEM((n * 8, 128), jnp.int32), pltpu.VMEM((4, 8, 128), F32), pltpu.VMEM((n, 8, 128), F32),
-         pltpu.VMEM((4, tok, width), BF), pltpu.VMEM((4, tok, width), BF), pltpu.VMEM((3, tok, width), BF), pltpu.VMEM((QB, QB), F32),
-         Gather.scratch(n, 2), Gather.scratch(n, 1), Gather.scratch(n, 2), sem_pairs(n), sem_pairs(n), sem_pairs(3), sem_pairs(3),
-         sem_pairs(1), sem_pairs(1), sem_pairs(3), sem_pairs(3), sem_pairs(3), sem_pairs(3), sem_pairs(3)],
-        "forward", 0,
-    )(outgoing, labels, qkv, w_out, gu, w_down, gain_block, out_grad, cos, sin, bias)
-    og_rows = og_all.reshape(rows, width)
-    nm = nm.reshape(rows, width)
-    wgu, wd = wgu.reshape(width, fw), wd.reshape(ff, width)
-    wg, wu = wgu[:, :ff], wgu[:, ff:]
-    gate, up = dot(nm, wg), dot(nm, wu)
-    s = jax.nn.sigmoid(gate)
-    silu = gate * s
-    hidden = (silu * up).astype(BF)
-    out_part = dot(hidden, wd).astype(BF)
-    dh = dot_nt(og_rows, wd)
-    d_gate = (dh * up * s * (1.0 + gate * (1.0 - s))).astype(BF)
-    d_up = (dh * silu).astype(BF)
-    gwd = dot_tn(hidden, og_rows).astype(BF)
-    gwgu = jnp.concatenate([dot_tn(nm, d_gate), dot_tn(nm, d_up)], axis=1).astype(BF)
-    dnm_part = (dot_nt(d_gate, wg) + dot_nt(d_up, wu)).astype(BF)
     blocks = ([((4, rq, fw), BF), ((rd, width), BF)], [((ro, width), BF)], [((4, rq, 1024), BF), ((8, 128), F32)])
     reduces = []
     for red, lines, sems in (Reduce.scratch(n, b) for b in blocks):
         reduces += [*red, *lines, sems]
+    vm = pltpu.VMEM
+    group = (4, tok, width)
     input_grad, layer_output, g_qkv, g_o, g_gu, g_d, small = linked(
-        functools.partial(backward_body, n, cap),
+        functools.partial(layer_body, n, cap),
         (shape(tok, width), shape(tok, width), shape(4, rq, 1024), shape(ro, width), shape(4, rq, fw), shape(rd, width), shape(8, 128, dtype=F32)),
-        [pltpu.VMEM((3, tok, width), BF), pltpu.VMEM((3, tok, width), BF), pltpu.VMEM((3, tok, width), BF), pltpu.VMEM((4, tok, width), BF),
-         pltpu.VMEM((tok, width), F32), pltpu.VMEM((QB, QB), F32), pltpu.VMEM((rows, 512), BF), pltpu.VMEM((rows, 512), F32),
-         pltpu.VMEM((rows, 256), F32), pltpu.VMEM((rows, 256), F32), pltpu.VMEM((rows, 1024), BF),
-         pltpu.VMEM((8, HD), F32), pltpu.VMEM((8, HD), F32), pltpu.VMEM((1, width), F32),
-         pltpu.VMEM((n, 4, rq, 1024), BF), pltpu.VMEM((n, ro, width), BF), pltpu.VMEM((n, 8, 128), F32),
-         pltpu.VMEM((slabs, width), BF), pltpu.VMEM((slabs, width), BF), *reduces,
-         pltpu.VMEM((4, rq, fw), BF), pltpu.VMEM((rd, width), BF), pltpu.VMEM((4, rq, 1024), BF), pltpu.VMEM((ro, width), BF),
-         pltpu.VMEM((8, 128), F32), pltpu.VMEM((4, 8, 128), F32),
+        [vm((n, 4, rq, 1024), BF), vm((n, ro, width), BF), vm((n, 4, rq, fw), BF), vm((n, rd, width), BF), vm(group, BF), vm((tok, width), BF),
+         vm((tok, slabs), BF), vm((8, width), F32), vm((8, width), F32), vm((rows, 512), BF), vm((rows, 256), BF), vm((rows, 256), BF),
+         vm((rows, 768), BF), vm((rows, width), BF), vm((rows, 512), BF), vm(group, BF), vm((tok, width), F32),
+         vm((slabs, width), BF), vm((n * 8, 128), jnp.int32), vm((4, 8, 128), F32), vm((n, 8, 128), F32),
+         vm(group, BF), vm(group, BF), vm((3, tok, width), BF), vm((QB, QB), F32),
+         vm((rows, ff), BF), vm((rows, fw), BF), vm(group, BF), vm((3, tok, width), BF), vm((3, tok, width), BF),
+         vm((tok, width), F32), vm((rows, 512), F32), vm((rows, 256), F32), vm((rows, 256), F32),
+         vm((8, HD), F32), vm((8, HD), F32), vm((1, width), F32), vm((n, 8, 128), F32), vm((slabs, width), BF),
+         *reduces,
+         vm((8, 128), F32), vm((4, 8, 128), F32),
+         Gather.scratch(n, 2), Gather.scratch(n, 1), Gather.scratch(n, 2), sem_pairs(n), sem_pairs(n), sem_pairs(3), sem_pairs(3),
+         sem_pairs(1), sem_pairs(1), sem_pairs(3), sem_pairs(3), sem_pairs(3), sem_pairs(3), sem_pairs(3),
          sem_pairs(3), sem_pairs(3), sem_pairs(3), sem_pairs(3), sem_pairs(n), sem_pairs(3), sem_pairs(1), sem_pairs(3), sem_pairs(1), sem_pairs(3)],
-        "backward", 1,
-    )(dnm_part.reshape(4, tok, width), out_part.reshape(4, tok, width), middle, x_own, out_grad, ga, gm, gqk,
-      gwgu.reshape(n, 4, rq, fw), gwd.reshape(n, rd, width), wo, wqkv, q, k, v, p, xn, att, pick, place, cos, sin, bias)
+        "layer", 0,
+    )(outgoing, labels, qkv, w_out, gu, w_down, gain_block, out_grad, place, cos, sin, bias)
 
     def own_lanes(row, count):
         return lax.dynamic_slice(small[row], ((index * count) % 128,), (count,))

time: 363 us -> 326 us (0.90)
  matrix products: 29.5 us -> 1.72 us
  Pallas kernels: 303 us -> 296 us
    dot_general x4 -> x1, matrix products: 10.1 us -> 0.19 us  [dot(): lax.dot_general(a, b, (((1,), (0,)), ((), ())), preferred_element_type=F32)]
    dot_general x3 -> x0, matrix products: 9.05 us -> none  [dot_nt(): lax.dot_general(a, b, (((1,), (1,)), ((), ())), preferred_element_type=F32)]
    dot_general x4 -> x1, matrix products: 10.4 us -> 1.53 us  [dot_tn(): lax.dot_general(a, b, (((0,), (0,)), ((), ())), preferred_element_type=F32)]
    pallas_call x2 -> x1, Pallas kernels: 303 us -> 296 us  [local(): linked(functools.partial(layer_body, n, cap), (shape(tok, width), shape(t...]
where the time goes in v4:
time: 326 us; the launch traced here: 322 us
  Pallas kernels  296 us (91%)
  local copies, waits for them, and re-layouts  12.5 us (4%)
  other arithmetic  9.84 us (3%)
    pallas_call x1, Pallas kernels, local(): linked(functools.partial(layer_body, n, cap), (shape(tok, width), shape(t...  296 us

profile of v4, /device:TPU:3, one launch (start us, length us, event | category | flops | bytes accessed | tf_op | source)
XLA Modules:
  0.0 321.8 jit_solution(3276019276961585953)
XLA Ops:
  0.6 0.0 copy-start
  0.7 0.0 copy-start.5
  0.7 0.0 copy-start.6
  1.4 0.7 bitcast_convert_fusion.3
  2.1 0.7 bitcast_convert_fusion.1
  2.8 0.7 bitcast_convert_fusion
  3.4 0.7 bitcast_convert_fusion.2
  4.1 0.2 dynamic_update_slice.17
  4.3 0.2 dynamic_update_slice.18
  4.5 0.2 dynamic_update_slice.19
  4.8 0.2 dynamic_update_slice.16
  5.0 0.6 select_maximum_fusion.gain_ref
  5.6 0.7 fusion.5
  6.3 0.2 fusion
  6.5 0.1 select_reduce_fusion
  6.7 0.1 add.69
  6.8 0.6 add.75.bias_ref
  7.4 0.6 broadcast_bitcast_fusion.lab_ref
  8.0 0.9 copy.55
  8.9 0.9 bitcast_bitcast_fusion.3
  9.8 0.7 pad_maximum_fusion.1.qkv_ref
  10.5 0.8 fusion.1.place_ref
  11.3 0.0 copy-done.5
  11.3 0.0 copy-done.6
  11.4 0.8 pad_maximum_fusion.gu_ref
  12.1 0.0 copy-done
  12.1 1.5 convolution_convert_fusion.out_ref
  13.7 296.2 %layer.1 = (bf16[256,1024]{1,0:T(8,128)(2,1)}, bf16[256,1024]{1,0:T(8,128)(2,1)}, bf16[4,32,1024]{2,1,0:T(8,128)(2,1)}, bf16[64,1024]{1,0:T(8,128)(2,1)}, bf16[4...) custom-call(bf16[512,1024]{1,0:T(8,128)(2,1)} %convolution_convert_fusion.out_ref, ...), custom_call_target="tpu_custom_call" | custom-call | tf_op jit(solution)/shard_map/layer/pallas_call | solution.py:850
  309.8 0.0 copy-start.4
  309.9 0.8 fusion.10
  310.7 0.6 fusion.6
  311.2 0.6 fusion.7
  311.8 0.6 fusion.9
  312.4 0.6 fusion.8
  313.0 1.6 convert_element_type.40
  314.6 1.7 convert_element_type.42
  316.3 0.0 copy-done.4
  316.4 0.0 copy-start.3
  316.4 0.7 copy.47
  317.1 0.7 copy.45
  317.8 0.7 copy.46
  318.5 0.0 copy-done.3
  318.5 0.1 convert_element_type.41
  318.6 0.1 slice_bitcast_fusion
  318.6 0.0 copy-start.2
  318.6 0.8 copy.49
  319.4 0.0 copy-start.1
  319.4 0.8 copy.48
  320.2 0.0 copy-done.2
  320.2 0.8 copy.62
  321.0 0.0 copy-done.1
  321.0 0.8 copy.63
  (11 shorter events, 0.1 us)
Async XLA Ops:
  0.6 11.5 %copy-start = (bf16[256,1024]{1,0:T(8,128)(2,1)S(1)}, bf16[256,1024]{1,0:T(8,128)(2,1)}, u32[]{:S(2)}) copy-start(bf16[256,1024]{1,0:T(8,128)(2,1)} %param.17) | copy-start | bytes 1572868
  0.7 10.7 %copy-start.5 = (bf16[32,3072]{1,0:T(8,128)(2,1)S(1)}, bf16[32,3072]{1,0:T(8,128)(2,1)}, u32[]{:S(2)}) copy-start(bf16[32,3072]{1,0:T(8,128)(2,1)} %param.30) | copy-start | bytes 589828
  0.7 10.7 %copy-start.6 = (bf16[32,3072]{1,0:T(8,128)(2,1)S(1)}, bf16[32,3072]{1,0:T(8,128)(2,1)}, u32[]{:S(2)}) copy-start(bf16[32,3072]{1,0:T(8,128)(2,1)} %param.29) | copy-start | bytes 589828
  309.8 6.5 %copy-start.4 = (bf16[4,32,1024]{2,1,0:T(8,128)(2,1)S(1)}, bf16[4,32,1024]{2,1,0:T(8,128)(2,1)}, u32[]{:S(2)}) copy-start(bf16[4,32,1024]{2,1,0:T(8,128)(2,1)} %get-tuple-element.23) | copy-start | bytes 786436
  316.4 2.1 copy-start.3
  318.6 1.6 copy-start.2
  319.4 1.6 copy-start.1

commit v5 on v4

--- a/solution.py
+++ b/solution.py
@@ -574,7 +574,7 @@
     hid_ref, dgu_ref, outp_ref, got_d, got_o, dmid_ref, dq_ref, dk_ref, dv_ref, ggq_ref, ggk_ref, ggm_ref, gains, recv_back,
     yi0, yi1, ln0, ln1, s_ra, yo, lo, s_rb, yq, yg, lq, lg, s_rc,
     gain_sum, gain_all,
-    s_ga, s_gb, s_gc, s_rows, s_labs, s_qkv, s_gu, s_wo, s_wd, s_gain, s_x, s_og, s_red, s_nm,
+    s_ga, s_gb, s_gc, s_gd4, s_rows, s_labs, s_qkv, s_gu, s_wo, s_wd, s_gain, s_x, s_og, s_red, s_nm,
     s_dnm, s_out, s_db, s_dxn, s_rows_back, s_gu_back, s_gd, s_qkv_back, s_o, s_gain_back,
 ):
     at = Place(n)
@@ -608,11 +608,7 @@
     og = CtxGather(at, og_all, s_og)
     gu.finish()
     og.start()
-    wo.finish()
-    second = Gather(at, [wo_ref], s_gb)
-    second.start()
-    wd.finish()
-    third = Gather(at, [wgu_ref, wd_ref], s_gc)
+    third = Gather(at, [wgu_ref], s_gc)
     third.start_inner()
     labs.finish()
     tok = x_ref.shape[1]
@@ -620,18 +616,20 @@
     for j in range(n):
         pick_ref[:, j * cap : (j + 1) * cap] = (slots == labels[j * 8 : j * 8 + 1, :cap]).astype(BF)
     first.step(1)
-    second.step(1)
     rows.finish()
     owned = dot(pick_ref[...], recv[...]).astype(BF)
     x_ref[at.ctx] = owned
     x_own[...] = owned
     x = CtxGather(at, x_ref, s_x)
     x.start()
-    for t in range(2, at.line):
+    first.step(2)
+    third.start_line()
+    wo.finish()
+    second = Gather(at, [wo_ref], s_gb)
+    second.start()
+    for t in range(3, at.line):
         first.step(t)
-        second.step(t)
-        if t == 2:
-            third.start_line()
+    second.step(1)
     og.forward()
     x.forward()
     first.arrive()
@@ -648,8 +646,14 @@
     off = bias_ref[0:1, 0:1]
     mask_ref[...] = mask_block(off)
     x.arrive()
+    second.step(2)
     attn_project(x_ref, wqkv_ref, ga_ref, gqk[2:3], gqk[3:4], cos_ref, sin_ref, q_ref, k_ref, v_ref, p_ref, xn_ref)
+    for t in range(3, at.line):
+        second.step(t)
     third.step(1)
+    wd.finish()
+    fourth = Gather(at, [wd_ref], s_gd4)
+    fourth.start()
     nk = k_ref.shape[1] // HD
 
     @pl.loop(0, nk)
@@ -657,6 +661,7 @@
         attn_group(g, off, q_ref, k_ref, v_ref, att_ref, mask_ref)
 
     third.step(2)
+    fourth.step(1)
     second.arrive()
 
     @pl.loop(0, 4)
@@ -666,22 +671,26 @@
     red = CtxReduce(at, part_ref, got, s_red)
     red.start()
     red.across()
+    for t in range(3, at.line):
+        third.step(t)
+        fourth.step(t - 1)
     middle = x_own[...].astype(F32) + red.result()
     mid_ref[...] = middle
     r = lax.rsqrt(jnp.mean(middle * middle, axis=-1, keepdims=True) + EPS)
     nm_ref[at.ctx] = (middle * r * gm_ref[0:1, :]).astype(BF)
     nm = CtxGather(at, nm_ref, s_nm)
     nm.start()
-    for t in range(3, at.line):
-        third.step(t)
+    fourth.step(at.line - 1)
     nm.forward()
     nm.arrive()
     og.arrive()
     third.arrive()
-    for part in (first, second, third, og, x, nm, red):
+    fourth.arrive()
+    for part in (first, second, third, fourth, og, x, nm, red):
         part.finish()
     feed_forward(nm_ref, og_all, wgu_ref, wd_ref, hid_ref, dgu_ref, outp_ref, part_ref)
     db_ref, da_ref, dp_ref = x_ref, hid_ref.at[:, : q_ref.shape[1]], dgu_ref.at[:, : wqkv_ref.shape[-1]]
+    last = at.line - 1
     dnm = CtxReduce(at, part_ref, got_d, s_dnm)
     dnm.start()
     weight_grad(wd_ref, hid_ref, og_all, 384)
@@ -693,7 +702,7 @@
     out = CtxReduce(at, outp_ref, got_o, s_out)
     dk_ref[...] = jnp.zeros_like(dk_ref)
     dv_ref[...] = jnp.zeros_like(dv_ref)
-    first.step(at.line - 1, [0, 1])
+    first.step(last, [1])
     gg, d = norm_back(dnm.result(), mid_ref[...], gm_ref[0:1, :])
     ggm_ref[...] = gg
     d = d + og_ref[...].astype(F32)
@@ -702,8 +711,8 @@
     db = CtxGather(at, db_ref, s_db)
     db.start()
     out.start()
-    for t in range(at.line - 2, 1, -1):
-        first.step(t, [0, 1])
+    for t in range(last - 1, 0, -1):
+        first.step(t, [1])
     db.forward()
     out.across()
     db.arrive()
@@ -713,37 +722,32 @@
     def _(i):
         da_ref[lanes(i, tok), :] = dot_nt(db_ref[i], rows_of(wo_ref)).astype(BF)
 
-    weight_grad(wo_ref, att_ref, db_ref)
-    first.step(1, [0, 1])
-    second = Reduce(at, [wo_ref], [yo], [lo], s_rb)
-    second.start([0])
+    first.step(last, [0])
     for g in range(k_ref.shape[1] // HD):
         for i in range(q_ref.shape[0] // QB):
             attn_group_back(g, i, off, q_ref, k_ref, v_ref, att_ref, da_ref, dq_ref, dk_ref, dv_ref, mask_ref)
         if g == 0:
-            first.result(0, into(yi0.at[at.outer]))
-            first.result(1, into(yi1.at[at.outer]))
-            gu = Quarters(at, yi0.at[at.outer], gu_out, s_gu_back)
-            gd = Slab(at, yi1.at[at.outer], gd_out, s_gd, at.slab_from)
-            gu.start()
-            gd.start()
-            for t in range(at.line - 1, 1, -1):
-                second.step(t, [0])
-    second.step(1, [0])
-    layer_ref[...] = (mid_ref[...] + out.result()).astype(BF)
-    second.result(0, into(yo.at[at.outer]))
-    o = Slab(at, yo.at[at.outer], o_out, s_o, at.slab_from)
-    o.start()
-    db.finish()
+            for t in range(last - 1, 1, -1):
+                first.step(t, [0])
     dxn_ref = nm_ref
     attn_unproject(gqk[2:3], gqk[3:4], cos_ref, sin_ref, p_ref, dq_ref, dk_ref, dv_ref, dp_ref, wqkv_ref, dxn_ref, ggq_ref, ggk_ref)
     dxn = CtxReduce(at, dxn_ref, got, s_dxn)
     dxn.start()
+    first.step(1, [0])
     weight_grad(wqkv_ref, xn_ref, dp_ref)
     third = Reduce(at, [wqkv_ref, gains], [yq, yg], [lq, lg], s_rc)
     third.start([0])
     dxn.across()
-    third.step(at.line - 1, [0])
+    weight_grad(wo_ref, att_ref, db_ref)
+    second = Reduce(at, [wo_ref], [yo], [lo], s_rb)
+    second.start([0])
+    first.result(1, into(yi1.at[at.outer]))
+    gd = Slab(at, yi1.at[at.outer], gd_out, s_gd, at.slab_from)
+    gd.start()
+    first.result(0, into(yi0.at[at.outer]))
+    gu = Quarters(at, yi0.at[at.outer], gu_out, s_gu_back)
+    gu.start()
+    third.step(last, [0])
     gg, d = norm_back(dxn.result(), x_own[...].astype(F32), ga_ref[0:1, :])
     owned = (dmid_ref[...] + d).astype(BF)
     recv[...] = dot_tn(pick_ref[...], owned).astype(BF)
@@ -758,9 +762,16 @@
             + jnp.where(lines == 2, ggq_ref[0:1, :], 0.0) + jnp.where(lines == 3, ggk_ref[0:1, :], 0.0)
         )
     third.start([1])
-    third.step(at.line - 1, [1])
-    for t in range(at.line - 2, 0, -1):
-        third.step(t, [0, 1])
+    second.step(last, [0])
+    for t in range(last - 1, 0, -1):
+        third.step(t, [0])
+        second.step(t, [0])
+    layer_ref[...] = (mid_ref[...] + out.result()).astype(BF)
+    for t in range(last, 0, -1):
+        third.step(t, [1])
+    second.result(0, into(yo.at[at.outer]))
+    o = Slab(at, yo.at[at.outer], o_out, s_o, at.slab_from)
+    o.start()
     third.result(0, into(yq.at[at.outer]))
     qkv = Quarters(at, yq.at[at.outer], qkv_out, s_qkv_back)
     qkv.start()
@@ -777,7 +788,7 @@
     for g in small:
         g.wait()
     gain_out[...] = gain_all[0] + gain_all[1] + gain_all[2] + gain_all[3]
-    for part in (qkv, o, gu, gd, dxn, out, dnm, first, second, third):
+    for part in (qkv, o, gu, gd, dxn, db, out, dnm, first, second, third):
         part.finish()
 
 
@@ -860,7 +871,7 @@
          vm((8, HD), F32), vm((8, HD), F32), vm((1, width), F32), vm((n, 8, 128), F32), vm((slabs, width), BF),
          *reduces,
          vm((8, 128), F32), vm((4, 8, 128), F32),
-         Gather.scratch(n, 2), Gather.scratch(n, 1), Gather.scratch(n, 2), sem_pairs(n), sem_pairs(n), sem_pairs(3), sem_pairs(3),
+         Gather.scratch(n, 2), Gather.scratch(n, 1), Gather.scratch(n, 1), Gather.scratch(n, 1), sem_pairs(n), sem_pairs(n), sem_pairs(3), sem_pairs(3),
          sem_pairs(1), sem_pairs(1), sem_pairs(3), sem_pairs(3), sem_pairs(3), sem_pairs(3), sem_pairs(3),
          sem_pairs(3), sem_pairs(3), sem_pairs(3), sem_pairs(3), sem_pairs(n), sem_pairs(3), sem_pairs(1), sem_pairs(3), sem_pairs(1), sem_pairs(3)],
         "layer", 0,

time: 326 us -> 295 us (0.905)
  Pallas kernels: 296 us -> 267 us
    pallas_call x1, Pallas kernels: 296 us -> 267 us  [local(): linked(functools.partial(layer_body, n, cap), (shape(tok, width), shape(t...]
where the time goes in v5:
time: 295 us; the launch traced here: 293 us
  Pallas kernels  267 us (91%)
  local copies, waits for them, and re-layouts  12.5 us (4%)
  other arithmetic  9.84 us (3%)
    pallas_call x1, Pallas kernels, local(): linked(functools.partial(layer_body, n, cap), (shape(tok, width), shape(t...  267 us

profile of v5, /device:TPU:3, one launch (start us, length us, event | category | flops | bytes accessed | tf_op | source)
XLA Modules:
  0.0 292.7 jit_solution(4869795465170096732)
XLA Ops:
  0.6 0.0 copy-start
  0.7 0.0 copy-start.5
  0.7 0.0 copy-start.6
  1.4 0.7 bitcast_convert_fusion.3
  2.1 0.7 bitcast_convert_fusion.1
  2.8 0.7 bitcast_convert_fusion
  3.4 0.7 bitcast_convert_fusion.2
  4.1 0.2 dynamic_update_slice.17
  4.3 0.2 dynamic_update_slice.18
  4.5 0.2 dynamic_update_slice.19
  4.8 0.2 dynamic_update_slice.16
  5.0 0.6 select_maximum_fusion.gain_ref
  5.6 0.7 fusion.5
  6.3 0.2 fusion
  6.5 0.1 select_reduce_fusion
  6.7 0.1 add.69
  6.8 0.6 add.75.bias_ref
  7.4 0.6 broadcast_bitcast_fusion.lab_ref
  8.0 0.9 copy.55
  8.9 0.9 bitcast_bitcast_fusion.3
  9.8 0.7 pad_maximum_fusion.1.qkv_ref
  10.5 0.8 fusion.1.place_ref
  11.3 0.0 copy-done.5
  11.3 0.0 copy-done.6
  11.4 0.8 pad_maximum_fusion.gu_ref
  12.1 0.0 copy-done
  12.1 1.5 convolution_convert_fusion.out_ref
  13.7 267.0 %layer.1 = (bf16[256,1024]{1,0:T(8,128)(2,1)}, bf16[256,1024]{1,0:T(8,128)(2,1)}, bf16[4,32,1024]{2,1,0:T(8,128)(2,1)}, bf16[64,1024]{1,0:T(8,128)(2,1)}, bf16[4...) custom-call(bf16[512,1024]{1,0:T(8,128)(2,1)} %convolution_convert_fusion.out_ref, ...), custom_call_target="tpu_custom_call" | custom-call | tf_op jit(solution)/shard_map/layer/pallas_call | solution.py:861
  280.7 0.0 copy-start.4
  280.7 0.8 fusion.10
  281.5 0.6 fusion.6
  282.1 0.6 fusion.7
  282.7 0.6 fusion.9
  283.3 0.6 fusion.8
  283.9 1.6 convert_element_type.40
  285.5 1.7 convert_element_type.42
  287.2 0.0 copy-done.4
  287.3 0.0 copy-start.3
  287.3 0.7 copy.47
  288.0 0.7 copy.45
  288.7 0.7 copy.46
  289.4 0.0 copy-done.3
  289.4 0.1 convert_element_type.41
  289.4 0.1 slice_bitcast_fusion
  289.5 0.0 copy-start.2
  289.5 0.8 copy.49
  290.3 0.0 copy-start.1
  290.3 0.8 copy.48
  291.1 0.0 copy-done.2
  291.1 0.8 copy.62
  291.9 0.0 copy-done.1
  291.9 0.8 copy.63
  (11 shorter events, 0.1 us)
Async XLA Ops:
  0.6 11.5 %copy-start = (bf16[256,1024]{1,0:T(8,128)(2,1)S(1)}, bf16[256,1024]{1,0:T(8,128)(2,1)}, u32[]{:S(2)}) copy-start(bf16[256,1024]{1,0:T(8,128)(2,1)} %param.17) | copy-start | bytes 1572868
  0.7 10.7 %copy-start.5 = (bf16[32,3072]{1,0:T(8,128)(2,1)S(1)}, bf16[32,3072]{1,0:T(8,128)(2,1)}, u32[]{:S(2)}) copy-start(bf16[32,3072]{1,0:T(8,128)(2,1)} %param.30) | copy-start | bytes 589828
  0.7 10.7 %copy-start.6 = (bf16[32,3072]{1,0:T(8,128)(2,1)S(1)}, bf16[32,3072]{1,0:T(8,128)(2,1)}, u32[]{:S(2)}) copy-start(bf16[32,3072]{1,0:T(8,128)(2,1)} %param.29) | copy-start | bytes 589828
  280.7 6.5 %copy-start.4 = (bf16[4,32,1024]{2,1,0:T(8,128)(2,1)S(1)}, bf16[4,32,1024]{2,1,0:T(8,128)(2,1)}, u32[]{:S(2)}) copy-start(bf16[4,32,1024]{2,1,0:T(8,128)(2,1)} %get-tuple-element.23) | copy-start | bytes 786436
  287.3 2.1 copy-start.3
  289.5 1.6 copy-start.2
  290.3 1.6 copy-start.1

commit v6 on v5

--- a/solution.py
+++ b/solution.py
@@ -245,7 +245,7 @@
             signal(**slab)
 
         count = count + jnp.where(place.slab_stays, 0, 1)
-    pl.semaphore_wait(barrier, count)
+    return barrier, count
 
 
 class Gather:
@@ -530,6 +530,10 @@
         self.at, self.src, self.dst, self.cap, self.sems = place, src, dst, cap, sems
 
     def rows(self, ref, j):
+        if len(ref.shape) == 3:
+            size = ref.shape[1]
+            start = j * self.cap
+            return ref.at[start // size, pl.ds(pl.multiple_of(start % size, self.cap), self.cap)]
         return ref.at[pl.ds(pl.multiple_of(j * self.cap, self.cap), self.cap)]
 
     def copy(self, k):
@@ -565,31 +569,97 @@
     return store
 
 
+def quarter_columns(dst_ref, weights):
+    for c in range(4):
+        start = 0
+        for w in weights:
+            size = w.shape[1] // 4
+            dst_ref[c, :, start : start + size] = w[:, c * size : (c + 1) * size]
+            start += size
+
+
+def route(n, cap, dest_ref, place_ref, labs_ref):
+    tok = dest_ref.shape[1]
+    dest = dest_ref[...]
+    owner = jnp.right_shift(dest, (4 * tok).bit_length() - 1)
+    slot = jnp.bitwise_and(dest, tok - 1)
+    lines = lax.broadcasted_iota(jnp.int32, (n, tok), 0)
+    hot = (lines == owner).astype(F32)
+    before = lax.broadcasted_iota(jnp.int32, (tok, tok), 0) < lax.broadcasted_iota(jnp.int32, (tok, tok), 1)
+    rank = dot(hot.astype(BF), before.astype(BF))
+    send = jnp.sum(hot * (rank + (lines * cap).astype(F32)), axis=0, keepdims=True).astype(jnp.int32)
+    place = (lax.broadcasted_iota(jnp.int32, (n * cap, tok), 0) == send).astype(BF)
+    place_ref[...] = place
+    labels = dot_nt(jnp.broadcast_to((slot + 1).astype(F32), (8, tok)).astype(BF), place)
+    labs_ref[...] = jnp.zeros_like(labs_ref)
+    for j in range(n):
+        labs_ref[j * 8 : j * 8 + 8, :cap] = labels[:, j * cap : (j + 1) * cap]
+
+
+def gain_tile(at, raw_ref, counts):
+    index = at.dp * 4 + at.ctx
+    raw = jnp.broadcast_to(raw_ref[...], (8, 128)).astype(BF)
+    source = lax.broadcasted_iota(jnp.int32, (128, 128), 0)
+    target = lax.broadcasted_iota(jnp.int32, (128, 128), 1)
+    lines = lax.broadcasted_iota(jnp.int32, (8, 128), 0)
+    total, start = jnp.zeros((8, 128), F32), 0
+    for k, count in enumerate(counts):
+        move = (target - (index * count) % 128 == source - start) & (source >= start) & (source < start + count)
+        total = total + jnp.where(lines == k, dot(raw, move.astype(BF)), 0.0)
+        start += count
+    return total
+
+
+def final_body(counts, ig, layer, qkv, o, gu, gd, small, layer_out, ig_out, ga, gq, gk, gv, gqg, gkg, go, gm, gg, gup, gdn):
+    index = lax.axis_index("dp") * 4 + lax.axis_index("ctx")
+    layer_out[...] = layer[...]
+    ig_out[...] = ig[...]
+    for blocks, outs in ((qkv, (gq, gk, gv)), (gu, (gg, gup))):
+        for c in range(4):
+            start = 0
+            for out in outs:
+                size = out.shape[1] // 4
+                out[:, c * size : (c + 1) * size] = blocks[c, :, start : start + size].astype(F32)
+                start += size
+    go[...] = o[...].astype(F32)
+    gdn[...] = gd[...].astype(F32)
+    for k, (out, count) in enumerate(zip((ga, gm, gqg, gkg), counts)):
+        row = pltpu.roll(small[...], (128 - (index * count) % 128) % 128, 1)
+        out[...] = row[k : k + 1, :count]
+
+
 def layer_body(
-    n, cap,
-    out_ref, lab_ref, qkv_ref, wo_src, gu_ref, wd_src, gain_ref, og_ref, place_ref, cos_ref, sin_ref, bias_ref,
+    n, cap, counts,
+    in_ref, dest_ref, doc_ref, raw_ref, og_ref, wq_src, wk_src, wv_src, wo_src, wg_src, wu_src, wd_src, cos_ref, sin_ref,
     ig_ref, layer_ref, qkv_out, o_out, gu_out, gd_out, gain_out,
     wqkv_ref, wo_ref, wgu_ref, wd_ref, og_all, x_own, pick_ref, ga_ref, gm_ref, q_ref, k_ref, v_ref, p_ref, xn_ref, att_ref, nm_ref, mid_ref,
     recv, labels, gains_c, gains_n, x_ref, part_ref, got, mask_ref,
     hid_ref, dgu_ref, outp_ref, got_d, got_o, dmid_ref, dq_ref, dk_ref, dv_ref, ggq_ref, ggk_ref, ggm_ref, gains, recv_back,
     yi0, yi1, ln0, ln1, s_ra, yo, lo, s_rb, yq, yg, lq, lg, s_rc,
-    gain_sum, gain_all,
+    gain_sum, gain_all, qkv_ref, gu_ref, place_ref, lab_ref,
     s_ga, s_gb, s_gc, s_gd4, s_rows, s_labs, s_qkv, s_gu, s_wo, s_wd, s_gain, s_x, s_og, s_red, s_nm,
     s_dnm, s_out, s_db, s_dxn, s_rows_back, s_gu_back, s_gd, s_qkv_back, s_o, s_gain_back,
 ):
     at = Place(n)
-    greet(at, (at.slab_from, at.slab_to))
+    barrier, count = greet(at, (at.slab_from, at.slab_to))
+    quarter_columns(qkv_ref, (wq_src, wk_src, wv_src))
+    gains_c[at.ctx] = gain_tile(at, raw_ref, counts)
+    route(n, cap, dest_ref, place_ref, lab_ref)
+    tok = in_ref.shape[0]
+    for half in range(n * cap // tok):
+        part_ref[half] = dot(place_ref[half * tok : (half + 1) * tok, :], in_ref[...]).astype(BF)
+    pl.semaphore_wait(barrier, count)
     qkv = Quarters(at, qkv_ref, wqkv_ref.at[at.dp], s_qkv)
-    rows = Exchange(at, out_ref, recv, cap, s_rows)
+    rows = Exchange(at, part_ref, recv, cap, s_rows)
     labs = Exchange(at, lab_ref, labels, 8, s_labs)
     qkv.start()
     gain_copies = [
-        rcopy(gain_ref, gains_c.at[at.ctx], s_gain.at[0, k], s_gain.at[1, k], ctx=c)
+        rcopy(gains_c.at[at.ctx], gains_c.at[at.ctx], s_gain.at[0, k], s_gain.at[1, k], ctx=c)
         for k, c in enumerate((at.c_x, at.c_far, at.c_core))
     ]
     for g in gain_copies:
         g.start()
-    gains_c[at.ctx] = gain_ref[...]
+    quarter_columns(gu_ref, (wg_src, wu_src))
     wo = Slab(at, wo_src, wo_ref.at[at.slab_to["dp"]], s_wo, at.slab_to)
     wd = Slab(at, wd_src, wd_ref.at[at.slab_to["dp"]], s_wd, at.slab_to)
     gu = Quarters(at, gu_ref, wgu_ref.at[at.dp], s_gu)
@@ -611,8 +681,7 @@
     third = Gather(at, [wgu_ref], s_gc)
     third.start_inner()
     labs.finish()
-    tok = x_ref.shape[1]
-    slots = lax.broadcasted_iota(jnp.int32, (tok, cap), 0)
+    slots = lax.broadcasted_iota(jnp.int32, (tok, cap), 0).astype(F32) + 1.0
     for j in range(n):
         pick_ref[:, j * cap : (j + 1) * cap] = (slots == labels[j * 8 : j * 8 + 1, :cap]).astype(BF)
     first.step(1)
@@ -643,7 +712,7 @@
         ga_ref[0:1, tile] += block[0:1]
         gm_ref[0:1, tile] += block[1:2]
         gqk = gqk + block
-    off = bias_ref[0:1, 0:1]
+    off = jnp.where(doc_ref[0:1, 0:1] > 0, 0.0, MASKED).astype(F32)
     mask_ref[...] = mask_block(off)
     x.arrive()
     second.step(2)
@@ -784,7 +853,7 @@
         g.start()
     gain_all[at.ctx] = gain_sum[...]
     rows.finish()
-    ig_ref[...] = dot(place_ref[...], recv_back[...]).astype(BF)
+    ig_ref[...] = dot_tn(place_ref[...], recv_back[...]).astype(BF)
     for g in small:
         g.wait()
     gain_out[...] = gain_all[0] + gain_all[1] + gain_all[2] + gain_all[3]
@@ -804,16 +873,6 @@
         compiler_params=pltpu.CompilerParams(vmem_limit_bytes=VMEM_LIMIT, collective_id=number, has_side_effects=True),
         name=name,
     )
-
-
-def to_quarters(weight):
-    rows, cols = weight.shape
-    return weight.reshape(rows, 4, cols // 4).transpose(1, 0, 2)
-
-
-def from_quarters(blocks):
-    n, rows, cols = blocks.shape
-    return blocks.transpose(1, 0, 2).reshape(rows, n * cols)
 
 
 def local(
@@ -827,31 +886,10 @@
     slabs = n * cap
     rq, ro, rd = w_query.shape[0], w_out.shape[0], w_down.shape[0]
     ff = rd * n
-    owner = dest_slot // (4 * tok)
-    slot = dest_slot % tok
-    hot = (owner[:, None] == jnp.arange(n, dtype=jnp.int32)[None, :]).astype(BF)
-    lower = (jnp.arange(tok)[:, None] > jnp.arange(tok)[None, :]).astype(BF)
-    rank = jnp.sum(dot(lower, hot) * hot.astype(F32), axis=1).astype(jnp.int32)
-    send_slot = owner * cap + rank
-    place = send_slot[:, None] == jnp.arange(slabs, dtype=jnp.int32)[None, :]
-    labels = jnp.sum(jnp.where(place, slot[:, None] - tok, 0), axis=0, dtype=jnp.int32) + tok
-    place = place.astype(BF)
-    outgoing = dot_tn(place, layer_input).astype(BF)
-    labels = jnp.broadcast_to(jnp.pad(labels.reshape(n, 1, cap), ((0, 0), (0, 0), (0, 128 - cap))), (n, 8, 128)).reshape(n * 8, 128)
-    index = lax.axis_index("dp") * 4 + lax.axis_index("ctx")
-    g_rows, g_heads = attn_gain.shape[0], q_gain.shape[0]
-
-    def at_lane(values):
-        start = (index * values.shape[0]) % 128
-        return lax.dynamic_update_slice(jnp.zeros((128,), F32), values.astype(F32), (start,))
-
-    gain_block = jnp.stack([at_lane(attn_gain), at_lane(mlp_gain), at_lane(q_gain), at_lane(k_gain)])
-    gain_block = jnp.pad(gain_block, ((0, 4), (0, 0)))
-    qkv = jnp.concatenate([to_quarters(w_query), to_quarters(w_key), to_quarters(w_value)], axis=2)
-    gu = jnp.concatenate([to_quarters(w_gate), to_quarters(w_up)], axis=2)
+    counts = (attn_gain.shape[0], mlp_gain.shape[0], q_gain.shape[0], k_gain.shape[0])
+    raw = jnp.pad(jnp.concatenate([attn_gain, mlp_gain, q_gain, k_gain]), (0, 128 - sum(counts))).astype(F32).reshape(1, 128)
     fw = 2 * ff
     cos, sin = rope_tables(rows)
-    bias = jnp.where(doc_len[0, 0] > 0, 0.0, MASKED).astype(F32).reshape(1, 1) + jnp.zeros((8, 128), F32)
     blocks = ([((4, rq, fw), BF), ((rd, width), BF)], [((ro, width), BF)], [((4, rq, 1024), BF), ((8, 128), F32)])
     reduces = []
     for red, lines, sems in (Reduce.scratch(n, b) for b in blocks):
@@ -859,43 +897,30 @@
     vm = pltpu.VMEM
     group = (4, tok, width)
     input_grad, layer_output, g_qkv, g_o, g_gu, g_d, small = linked(
-        functools.partial(layer_body, n, cap),
+        functools.partial(layer_body, n, cap, counts),
         (shape(tok, width), shape(tok, width), shape(4, rq, 1024), shape(ro, width), shape(4, rq, fw), shape(rd, width), shape(8, 128, dtype=F32)),
         [vm((n, 4, rq, 1024), BF), vm((n, ro, width), BF), vm((n, 4, rq, fw), BF), vm((n, rd, width), BF), vm(group, BF), vm((tok, width), BF),
          vm((tok, slabs), BF), vm((8, width), F32), vm((8, width), F32), vm((rows, 512), BF), vm((rows, 256), BF), vm((rows, 256), BF),
          vm((rows, 768), BF), vm((rows, width), BF), vm((rows, 512), BF), vm(group, BF), vm((tok, width), F32),
-         vm((slabs, width), BF), vm((n * 8, 128), jnp.int32), vm((4, 8, 128), F32), vm((n, 8, 128), F32),
+         vm((slabs, width), BF), vm((n * 8, 128), F32), vm((4, 8, 128), F32), vm((n, 8, 128), F32),
          vm(group, BF), vm(group, BF), vm((3, tok, width), BF), vm((QB, QB), F32),
          vm((rows, ff), BF), vm((rows, fw), BF), vm(group, BF), vm((3, tok, width), BF), vm((3, tok, width), BF),
          vm((tok, width), F32), vm((rows, 512), F32), vm((rows, 256), F32), vm((rows, 256), F32),
          vm((8, HD), F32), vm((8, HD), F32), vm((1, width), F32), vm((n, 8, 128), F32), vm((slabs, width), BF),
          *reduces,
-         vm((8, 128), F32), vm((4, 8, 128), F32),
+         vm((8, 128), F32), vm((4, 8, 128), F32), vm((4, rq, 1024), BF), vm((4, rq, fw), BF), vm((slabs, tok), BF), vm((n * 8, 128), F32),
          Gather.scratch(n, 2), Gather.scratch(n, 1), Gather.scratch(n, 1), Gather.scratch(n, 1), sem_pairs(n), sem_pairs(n), sem_pairs(3), sem_pairs(3),
          sem_pairs(1), sem_pairs(1), sem_pairs(3), sem_pairs(3), sem_pairs(3), sem_pairs(3), sem_pairs(3),
          sem_pairs(3), sem_pairs(3), sem_pairs(3), sem_pairs(3), sem_pairs(n), sem_pairs(3), sem_pairs(1), sem_pairs(3), sem_pairs(1), sem_pairs(3)],
         "layer", 0,
-    )(outgoing, labels, qkv, w_out, gu, w_down, gain_block, out_grad, place, cos, sin, bias)
-
-    def own_lanes(row, count):
-        return lax.dynamic_slice(small[row], ((index * count) % 128,), (count,))
-
-    g_qkv, g_gu = g_qkv.astype(F32), g_gu.astype(F32)
-    return (
-        layer_output,
-        input_grad,
-        own_lanes(0, g_rows),
-        from_quarters(g_qkv[:, :, :512]),
-        from_quarters(g_qkv[:, :, 512:768]),
-        from_quarters(g_qkv[:, :, 768:]),
-        own_lanes(2, g_heads),
-        own_lanes(3, g_heads),
-        g_o.astype(F32),
-        own_lanes(1, g_rows),
-        from_quarters(g_gu[:, :, :ff]),
-        from_quarters(g_gu[:, :, ff:]),
-        g_d.astype(F32),
+    )(layer_input, dest_slot.reshape(1, tok), doc_len, raw, out_grad, w_query, w_key, w_value, w_out, w_gate, w_up, w_down, cos, sin)
+    grads = [shape(*w.shape, dtype=F32) for w in (w_query, w_key, w_value, w_out, w_gate, w_up, w_down)]
+    gains = [shape(1, c, dtype=F32) for c in counts]
+    outs = (shape(tok, width), shape(tok, width), gains[0], *grads[:3], gains[2], gains[3], grads[3], gains[1], *grads[4:])
+    outs = pl.pallas_call(functools.partial(final_body, counts), out_shape=outs, name="final")(
+        input_grad, layer_output, g_qkv, g_o, g_gu, g_d, small
     )
+    return tuple(o.reshape(-1) if o.shape[0] == 1 else o for o in outs)
 
 
 def solution(mesh):

time: 295 us -> 275 us (0.932)
  local copies, waits for them, and re-layouts: 12.5 us -> 0.66 us
  other arithmetic: 9.84 us -> 1.24 us
  Pallas kernels: 267 us -> 270 us
    reshape x7 -> x0, local copies, waits for them, and re-layouts: 5.12 us -> none  [the longest x5 3.59 us: from_quarters(): return blocks.transpose(1, 0, 2).reshape(rows, n * cols)]
    convert_element_type x5 -> x0, other arithmetic: 4.25 us -> none  [the longest x1 1.7 us: local(): g_d.astype(F32)]
    another operation x5 -> x0, other arithmetic: 3.24 us -> none  [local(): jnp.stack([at_lane(attn_gain), at_lane(mlp_gain), at_lane(q_gain), at_lan...]
    pallas_call x1 -> x2, Pallas kernels: 267 us -> 270 us  [the longest x1 267 us: local(): linked(functools.partial(layer_body, n, cap, counts), (shape(tok, width),...]
where the time goes in v6:
time: 275 us; the launch traced here: 273 us
  Pallas kernels  270 us (98%)
    pallas_call x1, Pallas kernels, local(): linked(functools.partial(layer_body, n, cap, counts), (shape(tok, width),...  267 us

profile of v6, /device:TPU:3, one launch (start us, length us, event | category | flops | bytes accessed | tf_op | source)
XLA Modules:
  0.0 272.9 jit_solution(16590846525766252398)
XLA Ops:
  0.6 0.0 copy-start.2
  0.7 0.0 copy-start
  0.7 0.0 copy-start.1
  0.7 0.6 copy-done.2
  1.3 0.0 copy-done
  1.3 0.0 copy-done.1
  1.3 1.2 fusion.1.raw_ref
  2.6 267.1 %layer.1 = (bf16[256,1024]{1,0:T(8,128)(2,1)}, bf16[256,1024]{1,0:T(8,128)(2,1)}, bf16[4,32,1024]{2,1,0:T(8,128)(2,1)}, bf16[64,1024]{1,0:T(8,128)(2,1)}, bf16[4...) custom-call(bf16[256,1024]{1,0:T(8,128)(2,1)} %in_ref.1, s32[1,256]{1,0:T(1,128)} %bitcast.10, ...), custom_call_target="tpu_custom_call" | custom-call | tf_op jit(solution)/shard_map/layer/pallas_call | solution.py:899
  269.6 3.2 %final.1 = (bf16[256,1024]{1,0:T(8,128)(2,1)}, bf16[256,1024]{1,0:T(8,128)(2,1)}, f32[1,32]{1,0:T(1,128)}, f32[32,2048]{1,0:T(8,128)}, f32[32,1024]{1,0:T(8,128)...) custom-call(bf16[256,1024]{1,0:T(8,128)(2,1)} %get-tuple-element.33., ...), custom_call_target="tpu_custom_call" | custom-call | tf_op jit(solution)/shard_map/final/pallas_call | solution.py:920
Async XLA Ops:
  0.6 0.7 copy-start.2
  0.7 0.7 copy-start
  0.7 0.7 copy-start.1

commit v7 on v6

--- a/solution.py
+++ b/solution.py
@@ -578,6 +578,15 @@
             start += size
 
 
+def unit_columns(n, dst_ref, weights):
+    size = weights[0].shape[1] // (4 * n)
+    for c in range(4):
+        for k, w in enumerate(weights):
+            for d in range(n):
+                start = (k * n + d) * size
+                dst_ref[c, :, start : start + size] = w[:, (d * 4 + c) * size : (d * 4 + c + 1) * size]
+
+
 def route(n, cap, dest_ref, place_ref, labs_ref):
     tok = dest_ref.shape[1]
     dest = dest_ref[...]
@@ -614,13 +623,18 @@
     index = lax.axis_index("dp") * 4 + lax.axis_index("ctx")
     layer_out[...] = layer[...]
     ig_out[...] = ig[...]
-    for blocks, outs in ((qkv, (gq, gk, gv)), (gu, (gg, gup))):
-        for c in range(4):
-            start = 0
-            for out in outs:
-                size = out.shape[1] // 4
-                out[:, c * size : (c + 1) * size] = blocks[c, :, start : start + size].astype(F32)
-                start += size
+    for c in range(4):
+        start = 0
+        for out in (gq, gk, gv):
+            size = out.shape[1] // 4
+            out[:, c * size : (c + 1) * size] = qkv[c, :, start : start + size].astype(F32)
+            start += size
+        size = gdn.shape[0]
+        n = gg.shape[1] // (4 * size)
+        for k, out in enumerate((gg, gup)):
+            for d in range(n):
+                start = (k * n + d) * size
+                out[:, (d * 4 + c) * size : (d * 4 + c + 1) * size] = gu[c, :, start : start + size].astype(F32)
     go[...] = o[...].astype(F32)
     gdn[...] = gd[...].astype(F32)
     for k, (out, count) in enumerate(zip((ga, gm, gqg, gkg), counts)):
@@ -637,8 +651,8 @@
     hid_ref, dgu_ref, outp_ref, got_d, got_o, dmid_ref, dq_ref, dk_ref, dv_ref, ggq_ref, ggk_ref, ggm_ref, gains, recv_back,
     yi0, yi1, ln0, ln1, s_ra, yo, lo, s_rb, yq, yg, lq, lg, s_rc,
     gain_sum, gain_all, qkv_ref, gu_ref, place_ref, lab_ref,
-    s_ga, s_gb, s_gc, s_gd4, s_rows, s_labs, s_qkv, s_gu, s_wo, s_wd, s_gain, s_x, s_og, s_red, s_nm,
-    s_dnm, s_out, s_db, s_dxn, s_rows_back, s_gu_back, s_gd, s_qkv_back, s_o, s_gain_back,
+    s_ga, s_gb, s_gc, s_gd4, s_rows, s_labs, s_qkv, s_gu, s_wo, s_gain, s_x, s_og, s_red, s_nm,
+    s_dnm, s_out, s_db, s_dxn, s_rows_back, s_gu_back, s_qkv_back, s_o, s_gain_back,
 ):
     at = Place(n)
     barrier, count = greet(at, (at.slab_from, at.slab_to))
@@ -659,15 +673,14 @@
     ]
     for g in gain_copies:
         g.start()
-    quarter_columns(gu_ref, (wg_src, wu_src))
+    unit_columns(n, gu_ref, (wg_src, wu_src))
     wo = Slab(at, wo_src, wo_ref.at[at.slab_to["dp"]], s_wo, at.slab_to)
-    wd = Slab(at, wd_src, wd_ref.at[at.slab_to["dp"]], s_wd, at.slab_to)
+    wd_ref[at.dp] = wd_src[...]
     gu = Quarters(at, gu_ref, wgu_ref.at[at.dp], s_gu)
     labs.start()
     rows.start()
     gu.start()
     wo.start()
-    wd.start()
     for g in gain_copies:
         g.wait()
     gains_n[at.dp] = gains_c[0] + gains_c[1] + gains_c[2] + gains_c[3]
@@ -720,7 +733,6 @@
     for t in range(3, at.line):
         second.step(t)
     third.step(1)
-    wd.finish()
     fourth = Gather(at, [wd_ref], s_gd4)
     fourth.start()
     nk = k_ref.shape[1] // HD
@@ -810,9 +822,7 @@
     weight_grad(wo_ref, att_ref, db_ref)
     second = Reduce(at, [wo_ref], [yo], [lo], s_rb)
     second.start([0])
-    first.result(1, into(yi1.at[at.outer]))
-    gd = Slab(at, yi1.at[at.outer], gd_out, s_gd, at.slab_from)
-    gd.start()
+    first.result(1, into(gd_out))
     first.result(0, into(yi0.at[at.outer]))
     gu = Quarters(at, yi0.at[at.outer], gu_out, s_gu_back)
     gu.start()
@@ -857,7 +867,7 @@
     for g in small:
         g.wait()
     gain_out[...] = gain_all[0] + gain_all[1] + gain_all[2] + gain_all[3]
-    for part in (qkv, o, gu, gd, dxn, db, out, dnm, first, second, third):
+    for part in (qkv, o, gu, dxn, db, out, dnm, first, second, third):
         part.finish()
 
 
@@ -910,8 +920,8 @@
          *reduces,
          vm((8, 128), F32), vm((4, 8, 128), F32), vm((4, rq, 1024), BF), vm((4, rq, fw), BF), vm((slabs, tok), BF), vm((n * 8, 128), F32),
          Gather.scratch(n, 2), Gather.scratch(n, 1), Gather.scratch(n, 1), Gather.scratch(n, 1), sem_pairs(n), sem_pairs(n), sem_pairs(3), sem_pairs(3),
-         sem_pairs(1), sem_pairs(1), sem_pairs(3), sem_pairs(3), sem_pairs(3), sem_pairs(3), sem_pairs(3),
-         sem_pairs(3), sem_pairs(3), sem_pairs(3), sem_pairs(3), sem_pairs(n), sem_pairs(3), sem_pairs(1), sem_pairs(3), sem_pairs(1), sem_pairs(3)],
+         sem_pairs(1), sem_pairs(3), sem_pairs(3), sem_pairs(3), sem_pairs(3), sem_pairs(3),
+         sem_pairs(3), sem_pairs(3), sem_pairs(3), sem_pairs(3), sem_pairs(n), sem_pairs(3), sem_pairs(3), sem_pairs(1), sem_pairs(3)],
         "layer", 0,
     )(layer_input, dest_slot.reshape(1, tok), doc_len, raw, out_grad, w_query, w_key, w_value, w_out, w_gate, w_up, w_down, cos, sin)
     grads = [shape(*w.shape, dtype=F32) for w in (w_query, w_key, w_value, w_out, w_gate, w_up, w_down)]

time: 275 us -> 265 us (0.964)
  Pallas kernels: 270 us -> 262 us
    pallas_call x1, Pallas kernels: 267 us -> 259 us  [local(): linked(functools.partial(layer_body, n, cap, counts), (shape(tok, width),...]
where the time goes in v7:
time: 265 us
  Pallas kernels  262 us (99%)
    pallas_call x1, Pallas kernels, local(): linked(functools.partial(layer_body, n, cap, counts), (shape(tok, width),...  259 us

profile of v7, /device:TPU:3, one launch (start us, length us, event | category | flops | bytes accessed | tf_op | source)
XLA Modules:
  0.0 264.5 jit_solution(16188885604129067753)
XLA Ops:
  0.6 0.0 copy-start.2
  0.7 0.0 copy-start
  0.7 0.0 copy-start.1
  0.7 0.6 copy-done.2
  1.3 0.0 copy-done
  1.3 0.0 copy-done.1
  1.3 1.2 fusion.1.raw_ref
  2.6 258.5 %layer.1 = (bf16[256,1024]{1,0:T(8,128)(2,1)}, bf16[256,1024]{1,0:T(8,128)(2,1)}, bf16[4,32,1024]{2,1,0:T(8,128)(2,1)}, bf16[64,1024]{1,0:T(8,128)(2,1)}, bf16[4...) custom-call(bf16[256,1024]{1,0:T(8,128)(2,1)} %in_ref.1, s32[1,256]{1,0:T(1,128)} %bitcast.10, ...), custom_call_target="tpu_custom_call" | custom-call | tf_op jit(solution)/shard_map/layer/pallas_call | solution.py:909
  261.1 3.4 %final.1 = (bf16[256,1024]{1,0:T(8,128)(2,1)}, bf16[256,1024]{1,0:T(8,128)(2,1)}, f32[1,32]{1,0:T(1,128)}, f32[32,2048]{1,0:T(8,128)}, f32[32,1024]{1,0:T(8,128)...) custom-call(bf16[256,1024]{1,0:T(8,128)(2,1)} %get-tuple-element.33., ...), custom_call_target="tpu_custom_call" | custom-call | tf_op jit(solution)/shard_map/final/pallas_call | solution.py:930
Async XLA Ops:
  0.6 0.7 copy-start.2
  0.7 0.7 copy-start
  0.7 0.7 copy-start.1

commit v8 on v7

--- a/solution.py
+++ b/solution.py
@@ -21,7 +21,7 @@
 BF = jnp.bfloat16
 F32 = jnp.float32
 BOTH = ("dp", "ctx")
-VMEM_LIMIT = 62 << 20
+VMEM_LIMIT = 63 << 20
 
 
 def dot(a, b):
@@ -167,7 +167,7 @@
         dxn_ref[i] = dot_nt(dp_ref[here, :], rows_of(w)).astype(BF)
 
 
-def feed_forward(nm_ref, og_ref, wgu_ref, wd_ref, hid_ref, dgu_ref, out_ref, dnm_ref):
+def feed_up(nm_ref, wgu_ref, hid_ref, dgu_ref):
     rows = nm_ref.shape[1]
     ff = hid_ref.shape[1]
 
@@ -176,15 +176,24 @@
         here = lanes(i, rows)
         both = dot(nm_ref[i], rows_of(wgu_ref))
         gate, up = both[:, :ff], both[:, ff:]
+        dgu_ref[here, :] = both.astype(BF)
+        hid_ref[here, :] = (gate / (1.0 + jnp.exp2(gate * -LOG2E)) * up).astype(BF)
+
+
+def feed_down(og_ref, wgu_ref, wd_ref, hid_ref, dgu_ref, out_ref, dnm_ref):
+    rows = og_ref.shape[1]
+    ff = hid_ref.shape[1]
+
+    @pl.loop(0, og_ref.shape[0])
+    def _(i):
+        here = lanes(i, rows)
+        gate, up = dgu_ref[here, :ff].astype(F32), dgu_ref[here, ff:].astype(F32)
         s = 1.0 / (1.0 + jnp.exp2(gate * -LOG2E))
-        silu = gate * s
-        hidden = (silu * up).astype(BF)
-        hid_ref[here, :] = hidden
         dh = dot_nt(og_ref[i], rows_of(wd_ref))
         dgu_ref[here, :ff] = (dh * up * (s * (1.0 + gate * (1.0 - s)))).astype(BF)
-        dgu_ref[here, ff:] = (dh * silu).astype(BF)
+        dgu_ref[here, ff:] = (dh * (gate * s)).astype(BF)
         dnm_ref[i] = dot_nt(dgu_ref[here, :], rows_of(wgu_ref)).astype(BF)
-        out_ref[i] = dot(hidden, rows_of(wd_ref)).astype(BF)
+        out_ref[i] = dot(hid_ref[here, :], rows_of(wd_ref)).astype(BF)
 
 
 def weight_grad(out_ref, left_ref, right, chunk=256):
@@ -650,7 +659,7 @@
     recv, labels, gains_c, gains_n, x_ref, part_ref, got, mask_ref,
     hid_ref, dgu_ref, outp_ref, got_d, got_o, dmid_ref, dq_ref, dk_ref, dv_ref, ggq_ref, ggk_ref, ggm_ref, gains, recv_back,
     yi0, yi1, ln0, ln1, s_ra, yo, lo, s_rb, yq, yg, lq, lg, s_rc,
-    gain_sum, gain_all, qkv_ref, gu_ref, place_ref, lab_ref,
+    gain_sum, gain_all, qkv_ref, gu_ref, place_ref, lab_ref, gwd_ref,
     s_ga, s_gb, s_gc, s_gd4, s_rows, s_labs, s_qkv, s_gu, s_wo, s_gain, s_x, s_og, s_red, s_nm,
     s_dnm, s_out, s_db, s_dxn, s_rows_back, s_gu_back, s_qkv_back, s_o, s_gain_back,
 ):
@@ -733,8 +742,6 @@
     for t in range(3, at.line):
         second.step(t)
     third.step(1)
-    fourth = Gather(at, [wd_ref], s_gd4)
-    fourth.start()
     nk = k_ref.shape[1] // HD
 
     @pl.loop(0, nk)
@@ -742,7 +749,6 @@
         attn_group(g, off, q_ref, k_ref, v_ref, att_ref, mask_ref)
 
     third.step(2)
-    fourth.step(1)
     second.arrive()
 
     @pl.loop(0, 4)
@@ -754,36 +760,43 @@
     red.across()
     for t in range(3, at.line):
         third.step(t)
-        fourth.step(t - 1)
+    fourth = Gather(at, [wd_ref], s_gd4)
+    fourth.start()
     middle = x_own[...].astype(F32) + red.result()
     mid_ref[...] = middle
     r = lax.rsqrt(jnp.mean(middle * middle, axis=-1, keepdims=True) + EPS)
     nm_ref[at.ctx] = (middle * r * gm_ref[0:1, :]).astype(BF)
     nm = CtxGather(at, nm_ref, s_nm)
     nm.start()
-    fourth.step(at.line - 1)
+    fourth.step(1)
     nm.forward()
+    fourth.step(2)
     nm.arrive()
     og.arrive()
+    for t in range(3, at.line):
+        fourth.step(t)
     third.arrive()
+    feed_up(nm_ref, wgu_ref, hid_ref, dgu_ref)
+    weight_grad(gwd_ref, hid_ref, og_all, 384)
+    grads = Reduce(at, [wgu_ref, gwd_ref], [yi0, yi1], [ln0, ln1], s_ra)
+    grads.start([1])
     fourth.arrive()
     for part in (first, second, third, fourth, og, x, nm, red):
         part.finish()
-    feed_forward(nm_ref, og_all, wgu_ref, wd_ref, hid_ref, dgu_ref, outp_ref, part_ref)
+    first = grads
+    feed_down(og_all, wgu_ref, wd_ref, hid_ref, dgu_ref, outp_ref, part_ref)
     db_ref, da_ref, dp_ref = x_ref, hid_ref.at[:, : q_ref.shape[1]], dgu_ref.at[:, : wqkv_ref.shape[-1]]
     last = at.line - 1
     dnm = CtxReduce(at, part_ref, got_d, s_dnm)
     dnm.start()
-    weight_grad(wd_ref, hid_ref, og_all, 384)
-    first = Reduce(at, [wgu_ref, wd_ref], [yi0, yi1], [ln0, ln1], s_ra)
-    first.start([1])
+    first.step(last, [1])
     dnm.across()
     weight_grad(wgu_ref, nm_ref, dgu_ref)
     first.start([0])
     out = CtxReduce(at, outp_ref, got_o, s_out)
     dk_ref[...] = jnp.zeros_like(dk_ref)
     dv_ref[...] = jnp.zeros_like(dv_ref)
-    first.step(last, [1])
+    first.step(last - 1, [1])
     gg, d = norm_back(dnm.result(), mid_ref[...], gm_ref[0:1, :])
     ggm_ref[...] = gg
     d = d + og_ref[...].astype(F32)
@@ -792,7 +805,7 @@
     db = CtxGather(at, db_ref, s_db)
     db.start()
     out.start()
-    for t in range(last - 1, 0, -1):
+    for t in range(last - 2, 0, -1):
         first.step(t, [1])
     db.forward()
     out.across()
@@ -918,7 +931,7 @@
          vm((tok, width), F32), vm((rows, 512), F32), vm((rows, 256), F32), vm((rows, 256), F32),
          vm((8, HD), F32), vm((8, HD), F32), vm((1, width), F32), vm((n, 8, 128), F32), vm((slabs, width), BF),
          *reduces,
-         vm((8, 128), F32), vm((4, 8, 128), F32), vm((4, rq, 1024), BF), vm((4, rq, fw), BF), vm((slabs, tok), BF), vm((n * 8, 128), F32),
+         vm((8, 128), F32), vm((4, 8, 128), F32), vm((4, rq, 1024), BF), vm((4, rq, fw), BF), vm((slabs, tok), BF), vm((n * 8, 128), F32), vm((n, rd, width), BF),
          Gather.scratch(n, 2), Gather.scratch(n, 1), Gather.scratch(n, 1), Gather.scratch(n, 1), sem_pairs(n), sem_pairs(n), sem_pairs(3), sem_pairs(3),
          sem_pairs(1), sem_pairs(3), sem_pairs(3), sem_pairs(3), sem_pairs(3), sem_pairs(3),
          sem_pairs(3), sem_pairs(3), sem_pairs(3), sem_pairs(3), sem_pairs(n), sem_pairs(3), sem_pairs(3), sem_pairs(1), sem_pairs(3)],

time: 265 us -> 263 us (level)
  Pallas kernels: 262 us -> 259 us
where the time goes in v8:
time: 263 us; the launch traced here: 262 us
  Pallas kernels  259 us (98%)
    pallas_call x1, Pallas kernels, local(): linked(functools.partial(layer_body, n, cap, counts), (shape(tok, width),...  256 us

profile of v8, /device:TPU:3, one launch (start us, length us, event | category | flops | bytes accessed | tf_op | source)
XLA Modules:
  0.0 261.9 jit_solution(8248710122714418694)
XLA Ops:
  0.6 0.0 copy-start.2
  0.7 0.0 copy-start
  0.7 0.0 copy-start.1
  0.7 0.6 copy-done.2
  1.3 0.0 copy-done
  1.3 0.0 copy-done.1
  1.3 1.2 fusion.1.raw_ref
  2.6 256.0 %layer.1 = (bf16[256,1024]{1,0:T(8,128)(2,1)}, bf16[256,1024]{1,0:T(8,128)(2,1)}, bf16[4,32,1024]{2,1,0:T(8,128)(2,1)}, bf16[64,1024]{1,0:T(8,128)(2,1)}, bf16[4...) custom-call(bf16[256,1024]{1,0:T(8,128)(2,1)} %in_ref.1, s32[1,256]{1,0:T(1,128)} %bitcast.10, ...), custom_call_target="tpu_custom_call" | custom-call | tf_op jit(solution)/shard_map/layer/pallas_call | solution.py:922
  258.5 3.4 %final.1 = (bf16[256,1024]{1,0:T(8,128)(2,1)}, bf16[256,1024]{1,0:T(8,128)(2,1)}, f32[1,32]{1,0:T(1,128)}, f32[32,2048]{1,0:T(8,128)}, f32[32,1024]{1,0:T(8,128)...) custom-call(bf16[256,1024]{1,0:T(8,128)(2,1)} %get-tuple-element.33., ...), custom_call_target="tpu_custom_call" | custom-call | tf_op jit(solution)/shard_map/final/pallas_call | solution.py:943
Async XLA Ops:
  0.6 0.7 copy-start.2
  0.7 0.7 copy-start
  0.7 0.7 copy-start.1

commit v9 on v8

--- a/solution.py
+++ b/solution.py
@@ -856,8 +856,8 @@
     third.start([1])
     second.step(last, [0])
     for t in range(last - 1, 0, -1):
+        second.step(t, [0])
         third.step(t, [0])
-        second.step(t, [0])
     layer_ref[...] = (mid_ref[...] + out.result()).astype(BF)
     for t in range(last, 0, -1):
         third.step(t, [1])

time: 263 us -> 263 us (level)
  no operation moved by 1% of the time
where the time goes in v9:
time: 263 us; the launch traced here: 262 us
  Pallas kernels  259 us (98%)
    pallas_call x1, Pallas kernels, local(): linked(functools.partial(layer_body, n, cap, counts), (shape(tok, width),...  256 us

profile of v9, /device:TPU:3, one launch (start us, length us, event | category | flops | bytes accessed | tf_op | source)
XLA Modules:
  0.0 261.9 jit_solution(7808753895617716054)
XLA Ops:
  0.6 0.0 copy-start.2
  0.7 0.0 copy-start
  0.7 0.0 copy-start.1
  0.7 0.6 copy-done.2
  1.3 0.0 copy-done
  1.3 0.0 copy-done.1
  1.3 1.2 fusion.1.raw_ref
  2.6 256.0 %layer.1 = (bf16[256,1024]{1,0:T(8,128)(2,1)}, bf16[256,1024]{1,0:T(8,128)(2,1)}, bf16[4,32,1024]{2,1,0:T(8,128)(2,1)}, bf16[64,1024]{1,0:T(8,128)(2,1)}, bf16[4...) custom-call(bf16[256,1024]{1,0:T(8,128)(2,1)} %in_ref.1, s32[1,256]{1,0:T(1,128)} %bitcast.10, ...), custom_call_target="tpu_custom_call" | custom-call | tf_op jit(solution)/shard_map/layer/pallas_call | solution.py:922
  258.5 3.4 %final.1 = (bf16[256,1024]{1,0:T(8,128)(2,1)}, bf16[256,1024]{1,0:T(8,128)(2,1)}, f32[1,32]{1,0:T(1,128)}, f32[32,2048]{1,0:T(8,128)}, f32[32,1024]{1,0:T(8,128)...) custom-call(bf16[256,1024]{1,0:T(8,128)(2,1)} %get-tuple-element.33., ...), custom_call_target="tpu_custom_call" | custom-call | tf_op jit(solution)/shard_map/final/pallas_call | solution.py:943
Async XLA Ops:
  0.6 0.7 copy-start.2
  0.7 0.7 copy-start
  0.7 0.7 copy-start.1
